TPU v7x, 32 devices: a whole 2x2x4 slice. The times are simulated.
32 devices in a mesh: cube: 32 (over z, y, x, core).
Axes of the slice: x: 2, y: 2, z: 4, core: 2. Of those that a mesh axis runs over, the one named last changes fastest.
Arguments:
- offsets: float32 [3, 131072], P(None, 'cube'), may hold values from 0 to 1
- charges: float32 [16, 131072], P(None, 'cube'), may hold values from -6 to 6
- counts: int32 [1024], P('cube'), may hold values from 1 to 128, as said below
- u_list: int32 [1024, 27], P('cube'), may hold values from 0 to 1023, as said below
- v_src: int32 [1024, 32], P('cube'), may hold values from 0 to 111, as said below
- v_type: int32 [1024, 32], P('cube'), may hold values from 0 to 15
- wanted: int32 [32, 5, 16], P('cube'), may hold values from 0 to 31, as said below
- m2l: float32 [152, 2432], replicated, may hold values from -0.078125 to 0.078125
- uc2e: float32 [152, 152], replicated, may hold values from -0.5 to 0.5
- dc2e: float32 [152, 152], replicated, may hold values from -0.5 to 0.5
Outputs:
- potential: float32 [16, 131072], P(None, 'cube')
Inputs may be any that keep to these rules, and one draw needn't show every extreme that they name: `counts`: every leaf has at least one live point; the first leaf of each device is full. `u_list`: entry 0 of each row is the leaf itself; every entry lies within 8 leaves of the leaf in the global order. `v_src`: codes below 80 name hypercube dimension v // 16 and reader slot v % 16; larger codes name a leaf of the same device; entry 0 of each row is the leaf itself. `wanted`: entries of one list are distinct local leaf indices of the partner.
All inputs are finite; a program needn't handle non-finite values.
Results may differ from a plain program's by a relative error of at most 0.0003.
Values sent between devices are 32-bit elements; how exact they have to be, the bound alone decides.
No kernel may reach another device: no remote copies, remote signals or barrier semaphores. Data moves between devices by JAX's collectives and lax.ppermute only.
A program may use at most 64 MiB of HBM per device.

v0:
```python
import math

import jax
import jax.numpy as jnp
import numpy as np
from jax import lax
from jax.sharding import PartitionSpec as P

GHOST = 8


soften = 0.01
inv_four_pi = 1.0 / (4.0 * math.pi)
surface_radius = 0.55
highest = lax.Precision.HIGHEST


def with_halo(block, sides, width):
    for axis, dim in sides:
        count = lax.axis_size(axis)
        forward = [(i, i + 1) for i in range(count - 1)]
        backward = [(target, source) for source, target in forward]
        low = lax.ppermute(
            lax.slice_in_dim(block, block.shape[dim] - width, None, axis=dim), axis, forward
        )
        high = lax.ppermute(lax.slice_in_dim(block, 0, width, axis=dim), axis, backward)
        block = jnp.concatenate([low, block, high], axis=dim)
    return block


def from_partner(array, axis, bit):
    return lax.ppermute(array, axis, [(i, i ^ 1 << bit) for i in range(lax.axis_size(axis))])


def surface_table():
    lattice = np.arange(6)
    coords = np.stack(np.meshgrid(lattice, lattice, lattice, indexing="ij"), 0).reshape(3, -1)
    coords = (coords - 2.5) / 2.5
    on_face = np.max(np.abs(coords), axis=0) > 0.99
    return coords[:, on_face].astype(np.float32)


def leaf_corner(leaf_ids):
    corners = []
    for axis_num in range(3):
        summed = jnp.zeros_like(leaf_ids)
        for digit_num in range(10):
            summed = summed + ((leaf_ids >> 3 * digit_num + axis_num & 1) << digit_num)
        corners.append(summed)
    return jnp.stack(corners, 0).astype(jnp.float32)


def kernel(targets, sources):
    squared = jnp.zeros((targets.shape[-1], sources.shape[-1]), jnp.float32)
    for axis_num in range(3):
        squared = squared + (targets[axis_num][:, None] - sources[axis_num][None, :]) ** 2
    return inv_four_pi * lax.rsqrt(squared + soften)


def upward(points, masked, centers, surface, uc2e):
    checks = centers[:, :, None] + surface_radius * surface[:, None, :]
    tiles = jax.vmap(kernel, in_axes=(1, 1))(checks, points)
    potent = jnp.einsum("ljp,qlp->lqj", tiles, masked, precision=highest)
    return jnp.einsum("lqj,ij->lqi", potent, uc2e, precision=highest)


def downward(points, centers, surface, downcheck, dc2e):
    downeq = jnp.einsum("lqi,ji->lqj", downcheck, dc2e, precision=highest)
    equivs = centers[:, :, None] + surface_radius * surface[:, None, :]
    tiles = jax.vmap(kernel, in_axes=(1, 1))(points, equivs)
    return jnp.einsum("lpj,lqj->qlp", tiles, downeq, precision=highest)


def near_field(targets, src_pts, src_chg):
    leaf_count = targets.shape[0]
    group = math.gcd(leaf_count, 8)
    blocks = leaf_count // group

    def one_group(packed):
        tgt, spt, sch = packed
        tiles = jax.vmap(kernel)(tgt, spt)
        return jnp.einsum("gpn,gqn->gqp", tiles, sch, precision=highest)

    result = lax.map(
        one_group,
        (
            targets.reshape(blocks, group, targets.shape[1], targets.shape[2]),
            src_pts.reshape(blocks, group, src_pts.shape[1], src_pts.shape[2]),
            src_chg.reshape(blocks, group, src_chg.shape[1], src_chg.shape[2]),
        ),
    )
    return result.reshape(leaf_count, src_chg.shape[1], targets.shape[2])


def shards(offsets, charges, counts, u_list, v_src, v_type, wanted, m2l, uc2e, dc2e):
    local_leaves = counts.shape[0]
    per_leaf = offsets.shape[1] // local_leaves
    probes = charges.shape[0]
    equiv = uc2e.shape[0]
    kinds_count = m2l.shape[1] // equiv
    m2l_ops = m2l.reshape(equiv, kinds_count, equiv)
    bits = lax.axis_size("cube").bit_length() - 1
    read_cap = wanted.shape[2]
    surface = jnp.asarray(surface_table())
    first = lax.axis_index("cube") * local_leaves
    leaf_ids = first + jnp.arange(local_leaves, dtype=jnp.int32)
    inside = (jnp.arange(per_leaf, dtype=jnp.int32)[None, :] < counts[:, None]).astype(jnp.float32)
    corners = leaf_corner(leaf_ids)
    centers = corners + 0.5
    points = offsets.reshape(3, local_leaves, per_leaf) + corners[:, :, None]
    masked = charges.reshape(probes, local_leaves, per_leaf) * inside[None]
    stacked = jnp.concatenate(
        [
            points.reshape(3, local_leaves * per_leaf),
            masked.reshape(probes, local_leaves * per_leaf),
        ],
        0,
    )
    extended = with_halo(stacked, (("cube", 1),), GHOST * per_leaf)
    up_flat = upward(points, masked, centers, surface, uc2e).reshape(local_leaves, probes * equiv)
    pieces = []
    for bit_num in range(bits):
        pieces.append(from_partner(up_flat, "cube", bit_num))
    table = jnp.concatenate(pieces + [up_flat], 0)
    bit_part = jnp.minimum(v_src // read_cap, bits - 1)
    slot_part = v_src % read_cap
    remote_leaf = wanted[0][bit_part, slot_part]
    rows = jnp.where(
        v_src >= bits * read_cap,
        bits * local_leaves + v_src - bits * read_cap,
        bit_part * local_leaves + remote_leaf,
    )
    row_ids = jnp.arange(table.shape[0], dtype=jnp.int32)
    type_ids = jnp.arange(kinds_count, dtype=jnp.int32)
    onehot_rows = (rows[:, :, None] == row_ids[None, None, :]).astype(jnp.float32)
    onehot_types = (v_type[:, :, None] == type_ids[None, None, :]).astype(jnp.float32)
    tally = jnp.einsum("lvr,lvt->ltr", onehot_rows, onehot_types)
    by_type = jnp.einsum("ltr,rc->ltc", tally, table, precision=highest)
    by_type = by_type.reshape(local_leaves, kinds_count, probes, equiv)
    downcheck = jnp.einsum("ltqj,itj->lqi", by_type, m2l_ops, precision=highest)
    far = downward(points, centers, surface, downcheck, dc2e)
    ghost_leaves = extended.reshape(3 + probes, local_leaves + 2 * GHOST, per_leaf)
    local_ids = u_list - (first - GHOST)
    near_src = ghost_leaves[:, local_ids]
    src_pts = (
        near_src[:3].transpose(1, 0, 2, 3).reshape(local_leaves, 3, u_list.shape[1] * per_leaf)
    )
    src_chg = (
        near_src[3:].transpose(1, 0, 2, 3).reshape(local_leaves, probes, u_list.shape[1] * per_leaf)
    )
    near = near_field(points.transpose(1, 0, 2), src_pts, src_chg).transpose(1, 0, 2)
    potential = (near + far) * inside[None]
    return potential.reshape(probes, local_leaves * per_leaf)


def solution(mesh):
    in_specs = (
        P(None, "cube"),
        P(None, "cube"),
        P("cube"),
        P("cube", None),
        P("cube", None),
        P("cube", None),
        P("cube", None, None),
        P(),
        P(),
        P(),
    )
    out_specs = P(None, "cube")
    return jax.shard_map(shards, mesh=mesh, in_specs=in_specs, out_specs=out_specs, check_vma=False)
```

profile of v0, /device:TPU:0, one launch (start us, length us, event | category | flops | bytes accessed | tf_op | source)
XLA Modules:
  0.0 187.7 jit_solution(11713369803911639899)
XLA Ops:
  3.2 6.8 %fusion.43 = f32[32,16,152]{2,1,0:T(8,128)S(1)} fusion(f32[32,128]{1,0:T(8,128)S(1)} %get-tuple-element.65, f32[32,152]{1,0:T(8,128)S(1)} %get-tuple-element.62, f32[32,128]{1,0:T(8,128)S(1)} %get-tuple-element.66, f32[32,152]{1,0:T(8,128)S(1)} %get-tuple-element.63, f32[32,128]{1,0:T(8,128)S(1)} %get-tuple-element.64, ...), kind=kOutput, calls=%fused_computation.53 | convolution fusion | flops 125829120 | bytes 697344 | tf_op jit(solution)/shard_map/ljp,qlp->lqj/dot_general | solution.py:63
  11.0 4.1 %collective-permute-start.6 = (f32[32,2432]{1,0:T(8,128)S(1)}, f32[32,2432]{1,0:T(8,128)}, u32[]{:S(2)}, u32[]{:S(2)}) collective-permute-start(f32[32,2432]{1,0:T(8,128)S(1)} %reshape.470), channel_id=1, source_target_pairs={{0,16},{1,17},{2,18},{3,19},{4,20},{5,21},{6,22},{7,23},{8,24},{9,... | collective-permute-start | bytes 933896 | tf_op jit(solution)/shard_map/ppermute | solution.py:32
  15.1 1.6 collective-permute-start.5
  16.7 1.5 collective-permute-start.4
  19.1 1.3 collective-permute-start
  20.4 1.3 collective-permute-start.1
  22.0 4.8 %gather_fusion.1 = s32[1024]{0:T(1024)S(1)} fusion(s32[5,16]{1,0:T(8,128)S(1)} %bitcast.124, s32[1024]{0:T(1024)S(1)} %reshape.482), kind=kCustom, calls=%fused_computation.1 | custom fusion | bytes 16384 | tf_op jit(solution)/shard_map/gather | solution.py:127
  26.9 4.5 %reshape.472 = f32[152,16,152]{2,1,0:T(8,128)S(1)} reshape(f32[152,2432]{1,0:T(8,128)} %param.20) | data formatting | bytes 2957312 | tf_op jit(solution)/shard_map/reshape | solution.py:101
  31.4 1.2 fusion.85
  32.6 4.5 %collective-permute-start.3 = (f32[32,2432]{1,0:T(8,128)S(1)}, f32[32,2432]{1,0:T(8,128)}, u32[]{:S(2)}, u32[]{:S(2)}) collective-permute-start(f32[32,2432]{1,0:T(8,128)S(1)} %reshape.470), channel_id=1, source_target_pairs={{0,2},{1,3},{2,0},{3,1},{4,6},{5,7},{6,4},{7,5},{8,10},{9,11},{10,... | collective-permute-start | bytes 933896 | tf_op jit(solution)/shard_map/ppermute | solution.py:32
  37.5 5.2 %gather_fusion = f32[864,19,128]{2,1,0:T(8,128)} fusion(f32[19,48,128]{2,0,1:T(8,128)S(1)} %copy.17, s32[1024]{0:T(1024)S(1)} %pad_clamp_fusion), kind=kCustom, calls=%fused_computation | custom fusion | bytes 16813440 | tf_op jit(solution)/shard_map/gather | solution.py:144
  42.8 5.8 %copy.58 = f32[32,27,19,128]{3,1,0,2:T(8,128)S(1)} copy(f32[32,27,19,128]{3,2,1,0:T(8,128)} %bitcast.125) | data formatting | bytes 16809984 | tf_op jit(solution)/shard_map/gather | solution.py:144
  48.6 1.3 slice_bitcast_fusion.7
  49.8 4.3 %slice_bitcast_fusion.6 = f32[32,16,27,128]{3,2,0,1:T(8,128)} fusion(f32[19,32,27,128]{3,2,1,0:T(8,128)S(1)} %bitcast.127), kind=kLoop, calls=%fused_computation.37 | loop fusion | bytes 14155776 | tf_op jit(solution)/shard_map/transpose | solution.py:149
  54.1 9.1 %reshape.507 = f32[4,8,16,3456]{3,1,0,2:T(8,128)} reshape(f32[32,16,27,128]{3,2,0,1:T(8,128)} %slice_bitcast_fusion.6) | data formatting | bytes 14155776 | tf_op jit(solution)/shard_map/reshape;reshape | solution.py:89
  63.3 2.6 %reshape_reshape.7 = f32[4,8,3,3456]{3,1,0,2:T(8,128)} reshape(f32[32,3,27,128]{3,2,0,1:T(8,128)} %slice_bitcast_fusion.7) | data formatting | bytes 2654208 | tf_op jit(solution)/shard_map/reshape;reshape | solution.py:88
  65.9 78.9 %while.10 = (s32[]{:T(128)}, f32[4,8,16,128]{3,2,1,0:T(8,128)S(1)}, f32[4,8,16,3456]{3,1,0,2:T(8,128)}, f32[4,8,3,128]{3,1,0,2:T(8,128)}, f32[4,8,3,3456]{3,1,0,2:T(8,128)}, /*index=5*/s32[]{:T(128)}) while((s32[]{:T(128)}, f32[4,8,16,128]{3,2,1,0:T(8,128)S(1)}, f32[4,8,16,3456]{3,1,0,2:T(8,128)}, f32[4,8,3,128]{3,1,0,2:T(8,128)}, ...), condition=%wide.region_1.2_spmd, body=%wide.region_0.1_spmd.sunk | while | flops 714866688 | bytes 7094365 | solution.py:84
  66.6 1.0 dynamic-slice_bitcast_fusion.4
  67.6 1.6 constant_dynamic-slice_fusion.2
  69.2 16.3 %fusion.117 = f32[4,8,16,128]{3,2,1,0:T(8,128)S(1)} fusion(f32[4,8,16,128]{3,2,1,0:T(8,128)S(1)} %get-tuple-element.121, s32[]{:T(128)S(6)} %copy.66, f32[8,3456]{1,0:T(8,128)S(1)} %get-tuple-element.108, f32[8,128]{1,0:T(8,128)S(1)} %get-tuple-element.109, f32[8,3456]{1,0:T(8,128)S(1)} %get-tuple-element.110, f32[8,128]{1,0:T(8,128)S(1)} %get-tuple-element.111, ...), kind=kOutput, calls=%fused_computation.24.clone.1 | convolution fusion | flops 714866688 | bytes 2179076 | tf_op jit(solution)/shard_map/while/body/eval_jaxpr/gpn,gqn->gqp/dot_general | solution.py:82
  87.3 1.6 constant_dynamic-slice_fusion.2
  88.9 16.3 %fusion.117 = f32[4,8,16,128]{3,2,1,0:T(8,128)S(1)} fusion(f32[4,8,16,128]{3,2,1,0:T(8,128)S(1)} %get-tuple-element.121, s32[]{:T(128)S(6)} %copy.66, f32[8,3456]{1,0:T(8,128)S(1)} %get-tuple-element.108, f32[8,128]{1,0:T(8,128)S(1)} %get-tuple-element.109, f32[8,3456]{1,0:T(8,128)S(1)} %get-tuple-element.110, f32[8,128]{1,0:T(8,128)S(1)} %get-tuple-element.111, ...), kind=kOutput, calls=%fused_computation.24.clone.1 | convolution fusion | flops 714866688 | bytes 2179076 | tf_op jit(solution)/shard_map/while/body/eval_jaxpr/gpn,gqn->gqp/dot_general | solution.py:82
  107.0 1.6 constant_dynamic-slice_fusion.2
  108.6 16.3 %fusion.117 = f32[4,8,16,128]{3,2,1,0:T(8,128)S(1)} fusion(f32[4,8,16,128]{3,2,1,0:T(8,128)S(1)} %get-tuple-element.121, s32[]{:T(128)S(6)} %copy.66, f32[8,3456]{1,0:T(8,128)S(1)} %get-tuple-element.108, f32[8,128]{1,0:T(8,128)S(1)} %get-tuple-element.109, f32[8,3456]{1,0:T(8,128)S(1)} %get-tuple-element.110, f32[8,128]{1,0:T(8,128)S(1)} %get-tuple-element.111, ...), kind=kOutput, calls=%fused_computation.24.clone.1 | convolution fusion | flops 714866688 | bytes 2179076 | tf_op jit(solution)/shard_map/while/body/eval_jaxpr/gpn,gqn->gqp/dot_general | solution.py:82
  125.7 1.0 dynamic-slice_bitcast_fusion.4
  126.7 1.6 constant_dynamic-slice_fusion.2
  128.3 16.3 %fusion.117 = f32[4,8,16,128]{3,2,1,0:T(8,128)S(1)} fusion(f32[4,8,16,128]{3,2,1,0:T(8,128)S(1)} %get-tuple-element.121, s32[]{:T(128)S(6)} %copy.66, f32[8,3456]{1,0:T(8,128)S(1)} %get-tuple-element.108, f32[8,128]{1,0:T(8,128)S(1)} %get-tuple-element.109, f32[8,3456]{1,0:T(8,128)S(1)} %get-tuple-element.110, f32[8,128]{1,0:T(8,128)S(1)} %get-tuple-element.111, ...), kind=kOutput, calls=%fused_computation.24.clone.1 | convolution fusion | flops 714866688 | bytes 2179076 | tf_op jit(solution)/shard_map/while/body/eval_jaxpr/gpn,gqn->gqp/dot_general | solution.py:82
  144.8 1.0 constant_dynamic-update-slice_fusion.5
  149.9 6.1 %fusion.55 = f32[32,16,2432]{2,1,0:T(8,128)} fusion(f32[32,16,192]{2,1,0:T(8,128)S(1)} %copy-done.2, f32[192,2432]{1,0:T(8,128)S(1)} %constant_dynamic-update-slice_fusion), kind=kOutput, calls=%fused_computation.65 | convolution fusion | flops 2868903936 | bytes 7241728 | tf_op jit(solution)/shard_map/ltr,rc->ltc/dot_general | solution.py:138
  156.0 13.4 %reshape.471 = f32[32,16,16,152]{3,2,1,0:T(8,128)} reshape(f32[32,16,2432]{2,1,0:T(8,128)} %fusion.55) | data formatting | bytes 9961472 | tf_op jit(solution)/shard_map/reshape | solution.py:139
  169.5 11.6 %fusion.73 = f32[32,16,152]{2,1,0:T(8,128)S(1)} fusion(f32[32,16,16,152]{3,2,1,0:T(8,128)} %reshape.471, f32[152,16,152]{2,1,0:T(8,128)S(1)} %reshape.472), kind=kOutput, calls=%fused_computation.84 | convolution fusion | flops 2271215616 | bytes 6770688 | tf_op jit(solution)/shard_map/ltqj,itj->lqi/dot_general | solution.py:140
  181.8 5.2 %fusion.82 = f32[32,2,8,128]{3,2,1,0:T(8,128)S(1)} fusion(f32[32,16,128]{2,1,0:T(8,128)S(1)} %bitcast.133, f32[32,16,152]{2,1,0:T(8,128)S(1)} %fusion.88, f32[32,152]{1,0:T(8,128)S(1)} %copy-done.11, f32[32,128]{1,0:T(8,128)S(1)} %copy-done.21, f32[32,152]{1,0:T(8,128)S(1)} %copy-done.13, f32[32,128]{1,0:T(8,128)S(1)} %copy-done.23, ...), kind=kOutput, calls=%fused_computation.87 | convolution fusion | flops 125894656 | bytes 959488 | tf_op jit(solution)/shard_map/lpj,lqj->qlp/dot_general | solution.py:71
  (112 shorter events, 16.0 us)
Async XLA Ops:
  0.0 10.1 %copy-start = (f32[152,152]{1,0:T(8,128)S(1)}, f32[152,152]{1,0:T(8,128)}, u32[]{:S(2)}) copy-start(f32[152,152]{1,0:T(8,128)} %param.21) | copy-start | bytes 277252
  0.8 9.2 %copy-start.16 = (f32[32,128]{1,0:T(8,128)}, f32[32,128]{1,0:T(8,128)S(1)}, u32[]{:S(2)}) copy-start(f32[32,128]{1,0:T(8,128)S(1)} %fusion.101) | copy-start | bytes 49156
  1.6 8.4 %copy-start.8 = (f32[32,152]{1,0:T(8,128)}, f32[32,152]{1,0:T(8,128)S(1)}, u32[]{:S(2)}) copy-start(f32[32,152]{1,0:T(8,128)S(1)} %get-tuple-element.61) | copy-start | bytes 58372
  1.6 8.4 %copy-start.10 = (f32[32,152]{1,0:T(8,128)}, f32[32,152]{1,0:T(8,128)S(1)}, u32[]{:S(2)}) copy-start(f32[32,152]{1,0:T(8,128)S(1)} %get-tuple-element.62) | copy-start | bytes 58372
  1.6 8.4 %copy-start.12 = (f32[32,152]{1,0:T(8,128)}, f32[32,152]{1,0:T(8,128)S(1)}, u32[]{:S(2)}) copy-start(f32[32,152]{1,0:T(8,128)S(1)} %get-tuple-element.63) | copy-start | bytes 58372
  2.6 7.5 %copy-start.18 = (f32[32,128]{1,0:T(8,128)}, f32[32,128]{1,0:T(8,128)S(1)}, u32[]{:S(2)}) copy-start(f32[32,128]{1,0:T(8,128)S(1)} %get-tuple-element.64) | copy-start | bytes 49156
  2.6 7.5 %copy-start.20 = (f32[32,128]{1,0:T(8,128)}, f32[32,128]{1,0:T(8,128)S(1)}, u32[]{:S(2)}) copy-start(f32[32,128]{1,0:T(8,128)S(1)} %get-tuple-element.65) | copy-start | bytes 49156
  2.6 7.5 %copy-start.22 = (f32[32,128]{1,0:T(8,128)}, f32[32,128]{1,0:T(8,128)S(1)}, u32[]{:S(2)}) copy-start(f32[32,128]{1,0:T(8,128)S(1)} %get-tuple-element.66) | copy-start | bytes 49156
  3.2 15.0 %copy-start.25 = (s32[32]{0:T(128)S(1)}, s32[32]{0:T(128)}, u32[]{:S(2)}) copy-start(s32[32]{0:T(128)} %param.15) | copy-start | bytes 388
  3.2 15.1 %copy-start.5 = (f32[3,4096]{1,0:T(4,128)S(1)}, f32[3,4096]{1,0:T(4,128)}, u32[]{:S(2)}) copy-start(f32[3,4096]{1,0:T(4,128)} %param.13) | copy-start | bytes 147460
  3.2 15.2 %copy-start.4 = (f32[16,4096]{1,0:T(8,128)S(1)}, f32[16,4096]{1,0:T(8,128)}, u32[]{:S(2)}) copy-start(f32[16,4096]{1,0:T(8,128)} %param.14) | copy-start | bytes 786436
  10.1 11.6 %copy-start.24 = (s32[1,5,16]{2,0,1:T(1,128)S(1)}, s32[1,5,16]{2,0,1:T(1,128)}, u32[]{:S(2)}) copy-start(s32[1,5,16]{2,0,1:T(1,128)} %param.19) | copy-start | bytes 964
  10.1 11.6 %copy-start.15 = (s32[32,27]{1,0:T(8,128)S(1)}, s32[32,27]{1,0:T(8,128)}, u32[]{:S(2)}) copy-start(s32[32,27]{1,0:T(8,128)} %param.16) | copy-start | bytes 10372
  10.1 11.7 %copy-start.7 = (s32[32,32]{1,0:T(8,128)S(1)}, s32[32,32]{1,0:T(8,128)}, u32[]{:S(2)}) copy-start(s32[32,32]{1,0:T(8,128)} %param.17) | copy-start | bytes 12292
  11.0 137.8 %collective-permute-start.6 = (f32[32,2432]{1,0:T(8,128)S(1)}, f32[32,2432]{1,0:T(8,128)}, u32[]{:S(2)}, u32[]{:S(2)}) collective-permute-start(f32[32,2432]{1,0:T(8,128)S(1)} %reshape.470), channel_id=1, source_target_pairs={{0,16},{1,17},{2,18},{3,19},{4,20},{5,21},{6,22},{7,23},{8,24},{9,... | collective-permute-start | bytes 933896 | tf_op jit(solution)/shard_map/ppermute | solution.py:32
  15.1 132.7 %collective-permute-start.5 = (f32[32,2432]{1,0:T(8,128)S(1)}, f32[32,2432]{1,0:T(8,128)}, u32[]{:S(2)}, u32[]{:S(2)}) collective-permute-start(f32[32,2432]{1,0:T(8,128)S(1)} %reshape.470), channel_id=1, source_target_pairs={{0,8},{1,9},{2,10},{3,11},{4,12},{5,13},{6,14},{7,15},{8,0},{9,1},... | collective-permute-start | bytes 933896 | tf_op jit(solution)/shard_map/ppermute | solution.py:32
  16.7 130.1 %collective-permute-start.4 = (f32[32,2432]{1,0:T(8,128)S(1)}, f32[32,2432]{1,0:T(8,128)}, u32[]{:S(2)}, u32[]{:S(2)}) collective-permute-start(f32[32,2432]{1,0:T(8,128)S(1)} %reshape.470), channel_id=1, source_target_pairs={{0,4},{1,5},{2,6},{3,7},{4,0},{5,1},{6,2},{7,3},{8,12},{9,13},{10,... | collective-permute-start | bytes 933896 | tf_op jit(solution)/shard_map/ppermute | solution.py:32
  19.1 13.5 %collective-permute-start = (f32[19,1024]{1,0:T(8,128)}, f32[19,1024]{1,0:T(8,128)S(1)}, u32[]{:S(2)}, u32[]{:S(2)}) collective-permute-start(f32[19,1024]{1,0:T(8,128)} %get-tuple-element.59), channel_id=1, source_target_pairs={{0,1},{1,2},{2,3},{3,4},{4,5},{5,6},{6,7},{7,8},{8,9},{9,10},{10,1... | collective-permute-start | bytes 233480 | tf_op jit(solution)/shard_map/ppermute | solution.py:23
  20.4 16.7 %collective-permute-start.1 = (f32[19,1024]{1,0:T(8,128)S(1)}, f32[19,1024]{1,0:T(8,128)S(1)}, u32[]{:S(2)}, u32[]{:S(2)}) collective-permute-start(f32[19,1024]{1,0:T(8,128)S(1)} %get-tuple-element.60), channel_id=1, source_target_pairs={{1,0},{2,1},{3,2},{4,3},{5,4},{6,5},{7,6},{8,7},{9,8},{10,9},{11,1... | collective-permute-start | bytes 233480 | tf_op jit(solution)/shard_map/ppermute | solution.py:26
  26.8 4.6 %copy-start.14 = (s32[32,32]{1,0:T(8,128)S(1)}, s32[32,32]{1,0:T(8,128)}, u32[]{:S(2)}) copy-start(s32[32,32]{1,0:T(8,128)} %param.18) | copy-start | bytes 12292
  32.6 113.2 %collective-permute-start.3 = (f32[32,2432]{1,0:T(8,128)S(1)}, f32[32,2432]{1,0:T(8,128)}, u32[]{:S(2)}, u32[]{:S(2)}) collective-permute-start(f32[32,2432]{1,0:T(8,128)S(1)} %reshape.470), channel_id=1, source_target_pairs={{0,2},{1,3},{2,0},{3,1},{4,6},{5,7},{6,4},{7,5},{8,10},{9,11},{10,... | collective-permute-start | bytes 933896 | tf_op jit(solution)/shard_map/ppermute | solution.py:32
  37.1 107.7 %collective-permute-start.2 = (f32[32,2432]{1,0:T(8,128)S(1)}, f32[32,2432]{1,0:T(8,128)}, u32[]{:S(2)}, u32[]{:S(2)}) collective-permute-start(f32[32,2432]{1,0:T(8,128)S(1)} %reshape.470), channel_id=1, source_target_pairs={{0,1},{1,0},{2,3},{3,2},{4,5},{5,4},{6,7},{7,6},{8,9},{9,8},{10,11... | collective-permute-start | bytes 933896 | tf_op jit(solution)/shard_map/ppermute | solution.py:32
  144.8 5.1 %copy-start.2 = (f32[32,16,192]{2,1,0:T(8,128)S(1)}, f32[32,16,192]{2,1,0:T(8,128)}, u32[]{:S(2)}) copy-start(f32[32,16,192]{2,1,0:T(8,128)} %fusion.85) | copy-start | bytes 1179652
  169.4 11.7 %copy-start.6 = (f32[152,152]{1,0:T(8,128)S(1)}, f32[152,152]{1,0:T(8,128)}, u32[]{:S(2)}) copy-start(f32[152,152]{1,0:T(8,128)} %param.22) | copy-start | bytes 277252
  169.4 12.3 %copy-start.9 = (f32[32,152]{1,0:T(8,128)S(1)}, f32[32,152]{1,0:T(8,128)}, u32[]{:S(2)}) copy-start(f32[32,152]{1,0:T(8,128)} %copy-done.8) | copy-start | bytes 58372
  169.5 12.3 %copy-start.11 = (f32[32,152]{1,0:T(8,128)S(1)}, f32[32,152]{1,0:T(8,128)}, u32[]{:S(2)}) copy-start(f32[32,152]{1,0:T(8,128)} %copy-done.10) | copy-start | bytes 58372
  169.5 12.3 %copy-start.13 = (f32[32,152]{1,0:T(8,128)S(1)}, f32[32,152]{1,0:T(8,128)}, u32[]{:S(2)}) copy-start(f32[32,152]{1,0:T(8,128)} %copy-done.12) | copy-start | bytes 58372
  169.5 12.3 %copy-start.17 = (f32[32,128]{1,0:T(8,128)S(1)}, f32[32,128]{1,0:T(8,128)}, u32[]{:S(2)}) copy-start(f32[32,128]{1,0:T(8,128)} %copy-done.16) | copy-start | bytes 49156
  169.5 12.3 %copy-start.19 = (f32[32,128]{1,0:T(8,128)S(1)}, f32[32,128]{1,0:T(8,128)}, u32[]{:S(2)}) copy-start(f32[32,128]{1,0:T(8,128)} %copy-done.18) | copy-start | bytes 49156
  169.5 12.3 %copy-start.21 = (f32[32,128]{1,0:T(8,128)S(1)}, f32[32,128]{1,0:T(8,128)}, u32[]{:S(2)}) copy-start(f32[32,128]{1,0:T(8,128)} %copy-done.20) | copy-start | bytes 49156
  169.5 12.3 %copy-start.23 = (f32[32,128]{1,0:T(8,128)S(1)}, f32[32,128]{1,0:T(8,128)}, u32[]{:S(2)}) copy-start(f32[32,128]{1,0:T(8,128)} %copy-done.22) | copy-start | bytes 49156
  181.8 6.0 %copy-start.1 = (f32[152,152]{1,0:T(8,128)S(1)}, f32[152,152]{1,0:T(8,128)}, u32[]{:S(2)}) copy-start(f32[152,152]{1,0:T(8,128)} %param.21) | copy-start | bytes 277252
  (2 other events, 3.2 us)
where the time goes:
time: 189 us; the launch traced here: 188 us
  matrix products  97.2 us (51%)
  local copies, waits for them, and re-layouts  72 us (38%)
  starting transfers between devices  14.3 us (8%)
  other arithmetic  3.34 us (2%)
    dot_general x4, matrix products, one_group(): return jnp.einsum('gpn,gqn->gqp', tiles, sch, precision=highest)  65.1 us
    reshape x1, local copies, waits for them, and re-layouts, shards(): by_type = by_type.reshape(local_leaves, kinds_count, probes, equiv)  13.4 us
    ppermute x5, starting transfers between devices, from_partner(): lax.ppermute(array, axis, [(i, i ^ 1 << bit) for i in range(lax.axis_size...  11.7 us
    dot_general x1, matrix products, shards(): downcheck = jnp.einsum('ltqj,itj->lqi', by_type, m2l_ops, precision=highest)  11.6 us
    gather x2, local copies, waits for them, and re-layouts, shards(): near_src = ghost_leaves[:, local_ids]  11 us
    another operation x1, local copies, waits for them, and re-layouts, near_field(): src_chg.reshape(blocks, group, src_chg.shape[1], src_chg.shape[2])  9.14 us
    squeeze x8, local copies, waits for them, and re-layouts, near_field(): lax.map(one_group, (targets.reshape(blocks, group, targets.shape[1], targ...  6.99 us
    dot_general x1, matrix products, upward(): potent = jnp.einsum('ljp,qlp->lqj', tiles, masked, precision=highest)  6.83 us
  transfers between devices with their start and end apart: 7, of which 0 were waited for; matrix products, arithmetic and copies ran while one was open for 66% of the time, Pallas kernels for 0%

commit v1 on v0

--- a/solution.py
+++ b/solution.py
@@ -4,9 +4,12 @@
 import jax.numpy as jnp
 import numpy as np
 from jax import lax
+from jax.experimental import pallas as pl
+from jax.experimental.pallas import tpu as pltpu
 from jax.sharding import PartitionSpec as P
 
 GHOST = 8
+PTS = 128
 
 
 soften = 0.01
@@ -15,17 +18,13 @@
 highest = lax.Precision.HIGHEST
 
 
-def with_halo(block, sides, width):
-    for axis, dim in sides:
-        count = lax.axis_size(axis)
-        forward = [(i, i + 1) for i in range(count - 1)]
-        backward = [(target, source) for source, target in forward]
-        low = lax.ppermute(
-            lax.slice_in_dim(block, block.shape[dim] - width, None, axis=dim), axis, forward
-        )
-        high = lax.ppermute(lax.slice_in_dim(block, 0, width, axis=dim), axis, backward)
-        block = jnp.concatenate([low, block, high], axis=dim)
-    return block
+def halo(block, axis, width):
+    count = lax.axis_size(axis)
+    forward = [(i, i + 1) for i in range(count - 1)]
+    backward = [(target, source) for source, target in forward]
+    low = lax.ppermute(block[:, block.shape[1] - width:], axis, forward)
+    high = lax.ppermute(block[:, :width], axis, backward)
+    return low, high
 
 
 def from_partner(array, axis, bit):
@@ -71,25 +70,196 @@
     return jnp.einsum("lpj,lqj->qlp", tiles, downeq, precision=highest)
 
 
-def near_field(targets, src_pts, src_chg):
-    leaf_count = targets.shape[0]
-    group = math.gcd(leaf_count, 8)
-    blocks = leaf_count // group
-
-    def one_group(packed):
-        tgt, spt, sch = packed
-        tiles = jax.vmap(kernel)(tgt, spt)
-        return jnp.einsum("gpn,gqn->gqp", tiles, sch, precision=highest)
-
-    result = lax.map(
-        one_group,
-        (
-            targets.reshape(blocks, group, targets.shape[1], targets.shape[2]),
-            src_pts.reshape(blocks, group, src_pts.shape[1], src_pts.shape[2]),
-            src_chg.reshape(blocks, group, src_chg.shape[1], src_chg.shape[2]),
-        ),
-    )
-    return result.reshape(leaf_count, src_chg.shape[1], targets.shape[2])
+def near_kernel(first_ref, counts_ref, own_ref, low_ref, high_ref, ulist_ref, out_ref,
+                lanes_ref, chg_ref, src_ref, mult_ref, res_ref, start_ref, leaf_ref, from_ref, to_ref):
+    f32, bf16, i32 = jnp.float32, jnp.bfloat16, jnp.int32
+    local = out_ref.shape[1] // PTS
+    every = local + 2 * GHOST
+    probes = out_ref.shape[0]
+    base = GHOST * PTS
+    lane = lax.broadcasted_iota(i32, (1, PTS), 1)
+
+    first = first_ref[0]
+    centre = []
+    for axis in range(3):
+        low = high = jnp.int32(0)
+        for digit in range(10):
+            low = low + (((first >> (3 * digit + axis)) & 1) << digit)
+            high = high + ((((first + local - 1) >> (3 * digit + axis)) & 1) << digit)
+        centre.append((low + high + 1).astype(f32) * 0.5)
+    sub = lax.broadcasted_iota(i32, (8, PTS), 0)
+    shift_by = jnp.where(sub == 0, centre[0], jnp.where(sub == 1, centre[1], jnp.where(sub == 2, centre[2], 0.0)))
+
+    def units(n):
+        return ((n + 15) // 16) * 16
+
+    def ghost_count(ref, e):
+        return jnp.max(ref[3:4, e * PTS:(e + 1) * PTS]).astype(i32)
+
+    starts = [None] * (every + 1)
+    starts[GHOST] = jnp.int32(base)
+    for e in range(GHOST - 1, -1, -1):
+        starts[e] = starts[e + 1] - units(ghost_count(low_ref, e))
+    for e in range(GHOST, GHOST + local):
+        starts[e + 1] = starts[e] + units(counts_ref[e - GHOST])
+    for e in range(GHOST + local, every):
+        starts[e + 1] = starts[e] + units(ghost_count(high_ref, e - GHOST - local))
+    for e in range(every + 1):
+        start_ref[e] = starts[e]
+
+    for i in range(8):
+        leaf_ref[jnp.maximum((starts[0] >> 4) - 8 + i, 0)] = 0
+    for e in range(every):
+        for i in range(8 if e < every - 1 else 48):
+            leaf_ref[(starts[e] >> 4) + i] = e
+
+    for e in range(GHOST, GHOST + local):
+        head = starts[e] - base
+        tail = starts[e + 1] - base - 1
+        @pl.when(tail >= head)
+        def _():
+            h, t = head >> 8, tail >> 8
+
+            @pl.when((head & 255) == 0)
+            def _():
+                from_ref[h] = e
+
+            @pl.when(t > h)
+            def _():
+                from_ref[t] = e
+
+            to_ref[h] = e
+            to_ref[t] = e
+
+    ids = ulist_ref[...] - (first - GHOST)
+    which = lax.broadcasted_iota(i32, (local, every), 1)
+    tally = jnp.zeros((local, every), f32)
+    for u in range(ids.shape[1]):
+        tally = tally + (ids[:, u:u + 1] == which).astype(f32)
+    tally = tally.T
+
+    lanes_ref[...] = jnp.zeros_like(lanes_ref)
+    for e in range(every):
+        if e < GHOST:
+            block = low_ref[:, e * PTS:(e + 1) * PTS]
+        elif e < GHOST + local:
+            block = own_ref[:, (e - GHOST) * PTS:(e - GHOST + 1) * PTS]
+        else:
+            at = e - GHOST - local
+            block = high_ref[:, at * PTS:(at + 1) * PTS]
+        block = jnp.concatenate([block[:8] - shift_by, block[8:]], 0)
+        shift = starts[e] & (PTS - 1)
+        here = pl.multiple_of((starts[e] >> 7) << 7, PTS)
+        after = pl.multiple_of(((starts[e] >> 7) + 1) << 7, PTS)
+        rolled = pltpu.roll(block, shift, 1)
+        keep = lane >= shift
+        lanes_ref[:, pl.ds(here, PTS)] = jnp.where(keep, rolled, lanes_ref[:, pl.ds(here, PTS)])
+        lanes_ref[:, pl.ds(after, PTS)] = jnp.where(keep, 0.0, rolled)
+        if GHOST <= e < GHOST + local:
+            col = jnp.broadcast_to(tally[:, e - GHOST:e - GHOST + 1], (every, PTS))
+            here = pl.multiple_of(here - base, PTS)
+            after = pl.multiple_of(after - base, PTS)
+            mult_ref[:, pl.ds(here, PTS)] = jnp.where(keep, col, mult_ref[:, pl.ds(here, PTS)])
+            mult_ref[:, pl.ds(after, PTS)] = col
+
+    group = 4 * PTS
+    head = starts[0] >> 7
+    tail = (starts[every] + 127) >> 7
+
+    def spread(i, _):
+        at = pl.multiple_of((head + 4 * i) * PTS, PTS)
+        pos = lanes_ref[0:8, pl.ds(at, group)]
+        norm = pos[0:1] * pos[0:1] + pos[1:2] * pos[1:2] + pos[2:3] * pos[2:3]
+        feats = jnp.concatenate([-2.0 * pos[0:3], norm + soften, pos[4:8]], 0)
+        lanes_ref[3:4, pl.ds(at, group)] = norm
+        turned = feats.T
+        for k in range(4):
+            src_ref[k, pl.ds(at, group), :] = jnp.broadcast_to(turned[:, k:k + 1], (group, PTS))
+        chg = lanes_ref[8:8 + probes, pl.ds(at, group)]
+        hi = chg.astype(bf16)
+        chg_ref[0:probes, pl.ds(at, group)] = hi
+        chg_ref[probes:2 * probes, pl.ds(at, group)] = (chg - hi.astype(f32)).astype(bf16)
+        return 0
+
+    lax.fori_loop(0, (tail - head + 3) // 4 + 1, spread, 0)
+
+    def target_block(t, _):
+        where = pl.multiple_of(t * 256, 256)
+        tgt = lanes_ref[0:8, pl.ds(pl.multiple_of(base + where, 256), 256)]
+        lo_row = (start_ref[from_ref[t] - GHOST] >> 7) << 7
+        hi_row = start_ref[to_ref[t] + GHOST + 1]
+
+        def chunk(row, size, carry):
+            first_sum, second_sum = carry
+            row = pl.multiple_of(row, PTS)
+            his, los = [], []
+            for r in range(size // 16):
+                at = pl.multiple_of(row + 16 * r, 16)
+                leaf = leaf_ref[(row >> 4) + r]
+                weight = mult_ref[pl.ds(leaf, 1), pl.ds(where, 256)]
+                hi_pair, lo_pair = [], []
+                for half in range(2):
+                    x = tgt[:, half * 128:(half + 1) * 128]
+                    s = (src_ref[3, pl.ds(at, 16), :] + x[3:4]) + src_ref[0, pl.ds(at, 16), :] * x[0:1]
+                    s = s + (src_ref[1, pl.ds(at, 16), :] * x[1:2] + src_ref[2, pl.ds(at, 16), :] * x[2:3])
+                    k = lax.rsqrt(s) * weight[:, half * 128:(half + 1) * 128]
+                    hi = k.astype(bf16)
+                    hi_pair.append(hi)
+                    lo_pair.append((k - hi.astype(f32)).astype(bf16))
+                his.append(jnp.concatenate(hi_pair, 1))
+                los.append(jnp.concatenate(lo_pair, 1))
+            chg = chg_ref[:, pl.ds(row, size)]
+            first_sum = first_sum + jnp.dot(chg, jnp.concatenate(his, 0), preferred_element_type=f32)
+            second_sum = second_sum + jnp.dot(chg[:probes], jnp.concatenate(los, 0), preferred_element_type=f32)
+            return first_sum, second_sum
+
+        sums = (jnp.zeros((2 * probes, 256), f32), jnp.zeros((probes, 256), f32))
+        size = 512
+        sums = lax.fori_loop(0, (hi_row - lo_row + size - 1) // size, lambda i, c: chunk(lo_row + size * i, size, c), sums)
+        res_ref[:, pl.ds(where, 256)] = sums[0][:probes] + sums[0][probes:] + sums[1]
+        return 0
+
+    lax.fori_loop(0, (starts[GHOST + local] - base + 255) // 256, target_block, 0)
+
+    for g in range(local):
+        at = starts[g + GHOST] - base
+        shift = at & (PTS - 1)
+        here = pl.multiple_of((at >> 7) << 7, PTS)
+        after = pl.multiple_of(((at >> 7) + 1) << 7, PTS)
+        back = (PTS - shift) & (PTS - 1)
+        value = jnp.where(lane < PTS - shift, pltpu.roll(res_ref[:, pl.ds(here, PTS)], back, 1),
+                          pltpu.roll(res_ref[:, pl.ds(after, PTS)], back, 1))
+        out_ref[:, g * PTS:(g + 1) * PTS] = jnp.where(lane < counts_ref[g], value * inv_four_pi, 0.0)
+
+
+def near_call(first, counts, own, low, high, u_list):
+    local = counts.shape[0]
+    probes = own.shape[0] - 8
+    every = local + 2 * GHOST
+    width = every * PTS + 8 * PTS + 512
+    targets = local * PTS + 512
+    smem = pl.BlockSpec(memory_space=pltpu.SMEM)
+    vmem = pl.BlockSpec(memory_space=pltpu.VMEM)
+    return pl.pallas_call(
+        near_kernel,
+        out_shape=jax.ShapeDtypeStruct((probes, local * PTS), jnp.float32),
+        in_specs=[smem, smem, vmem, vmem, vmem, vmem],
+        out_specs=vmem,
+        scratch_shapes=[
+            pltpu.VMEM((8 + probes, width), jnp.float32),
+            pltpu.VMEM((2 * probes, width), jnp.bfloat16),
+            pltpu.VMEM((4, width, PTS), jnp.float32),
+            pltpu.VMEM((every, targets), jnp.float32),
+            pltpu.VMEM((probes, targets), jnp.float32),
+            pltpu.SMEM((every + 1,), jnp.int32),
+            pltpu.SMEM((width // 16 + 64,), jnp.int32),
+            pltpu.SMEM((local * PTS // 256 + 1,), jnp.int32),
+            pltpu.SMEM((local * PTS // 256 + 1,), jnp.int32),
+        ],
+        compiler_params=pltpu.CompilerParams(vmem_limit_bytes=48 << 20),
+        cost_estimate=pl.CostEstimate(flops=4_000_000_000, bytes_accessed=2_000_000, transcendentals=4_000_000),
+        name="near",
+    )(first, counts, own, low, high, u_list)
 
 
 def shards(offsets, charges, counts, u_list, v_src, v_type, wanted, m2l, uc2e, dc2e):
@@ -109,14 +279,17 @@
     centers = corners + 0.5
     points = offsets.reshape(3, local_leaves, per_leaf) + corners[:, :, None]
     masked = charges.reshape(probes, local_leaves, per_leaf) * inside[None]
-    stacked = jnp.concatenate(
+    held = jnp.broadcast_to(counts.astype(jnp.float32)[:, None], (local_leaves, per_leaf))
+    own = jnp.concatenate(
         [
             points.reshape(3, local_leaves * per_leaf),
+            held.reshape(1, local_leaves * per_leaf),
+            jnp.zeros((4, local_leaves * per_leaf), jnp.float32),
             masked.reshape(probes, local_leaves * per_leaf),
         ],
         0,
     )
-    extended = with_halo(stacked, (("cube", 1),), GHOST * per_leaf)
+    low, high = halo(own, "cube", GHOST * per_leaf)
     up_flat = upward(points, masked, centers, surface, uc2e).reshape(local_leaves, probes * equiv)
     pieces = []
     for bit_num in range(bits):
@@ -139,18 +312,9 @@
     by_type = by_type.reshape(local_leaves, kinds_count, probes, equiv)
     downcheck = jnp.einsum("ltqj,itj->lqi", by_type, m2l_ops, precision=highest)
     far = downward(points, centers, surface, downcheck, dc2e)
-    ghost_leaves = extended.reshape(3 + probes, local_leaves + 2 * GHOST, per_leaf)
-    local_ids = u_list - (first - GHOST)
-    near_src = ghost_leaves[:, local_ids]
-    src_pts = (
-        near_src[:3].transpose(1, 0, 2, 3).reshape(local_leaves, 3, u_list.shape[1] * per_leaf)
-    )
-    src_chg = (
-        near_src[3:].transpose(1, 0, 2, 3).reshape(local_leaves, probes, u_list.shape[1] * per_leaf)
-    )
-    near = near_field(points.transpose(1, 0, 2), src_pts, src_chg).transpose(1, 0, 2)
-    potential = (near + far) * inside[None]
-    return potential.reshape(probes, local_leaves * per_leaf)
+    near = near_call(first.reshape(1).astype(jnp.int32), counts, own, low, high, u_list)
+    potential = near + (far * inside[None]).reshape(probes, local_leaves * per_leaf)
+    return potential
 
 
 def solution(mesh):

time: 189 us -> 96.4 us (0.51)
  the two profiles are of different devices: /device:TPU:0 before, /device:TPU:8 now
where the time goes in v1:
time: 96.4 us; the launch traced here: 95.8 us
  matrix products  30.2 us (31%)
  local copies, waits for them, and re-layouts  27.1 us (28%)
  Pallas kernels  21.1 us (22%)
  starting transfers between devices  13.5 us (14%)
  other arithmetic  3.48 us (4%)
    pallas_call x1, Pallas kernels, near_call(): pl.pallas_call(near_kernel, out_shape=jax.ShapeDtypeStruct((probes, local...  21.1 us
    reshape x1, local copies, waits for them, and re-layouts, shards(): by_type = by_type.reshape(local_leaves, kinds_count, probes, equiv)  13.4 us
    dot_general x1, matrix products, shards(): downcheck = jnp.einsum('ltqj,itj->lqi', by_type, m2l_ops, precision=highest)  9.59 us
    dot_general x1, matrix products, upward(): potent = jnp.einsum('ljp,qlp->lqj', tiles, masked, precision=highest)  6.73 us
    dot_general x1, matrix products, shards(): by_type = jnp.einsum('ltr,rc->ltc', tally, table, precision=highest)  6.12 us
    ppermute x5, starting transfers between devices, from_partner(): lax.ppermute(array, axis, [(i, i ^ 1 << bit) for i in range(lax.axis_size...  6.1 us
    ppermute x1, starting transfers between devices, halo(): high = lax.ppermute(block[:, :width], axis, backward)  5.44 us
    dot_general x1, matrix products, downward(): return jnp.einsum('lpj,lqj->qlp', tiles, downeq, precision=highest)  5.14 us
  transfers between devices with their start and end apart: 7, of which 0 were waited for; matrix products, arithmetic and copies ran while one was open for 13% of the time, Pallas kernels for 22%

profile of v1, /device:TPU:8, one launch (start us, length us, event | category | flops | bytes accessed | tf_op | source)
XLA Modules:
  0.0 95.8 jit_solution(11296318384977162875)
XLA Ops:
  0.1 0.9 bitcast_add_fusion.2
  1.0 0.8 broadcast_add_fusion
  1.9 0.7 fusion.63
  2.6 1.0 %copy.21 = f32[2,8,32,128]{3,2,1,0:T(8,128)S(1)} copy(f32[2,8,32,128]{3,1,2,0:T(8,128)} %bitcast.58) | data formatting | bytes 524288
  3.7 6.7 %fusion.12 = f32[32,16,152]{2,1,0:T(8,128)S(1)} fusion(f32[32,128]{1,0:T(8,128)S(1)} %get-tuple-element.11, f32[32,152]{1,0:T(8,128)S(1)} %get-tuple-element.8, f32[32,128]{1,0:T(8,128)S(1)} %get-tuple-element.12, f32[32,152]{1,0:T(8,128)S(1)} %get-tuple-element.9, f32[32,128]{1,0:T(8,128)S(1)} %get-tuple-element.10, f32[32,152]{1,0:T(8,128)S(1)} %get-tuple-element.7, ...), kind=kOutput, calls=%fused_computation.13 | convolution fusion | flops 125763584 | bytes 680960 | tf_op jit(solution)/shard_map/ljp,qlp->lqj/dot_general | solution.py:62
  10.5 0.6 fusion.54
  11.1 1.0 %reshape.464 = f32[32,2432]{1,0:T(8,128)} reshape(f32[32,16,152]{2,1,0:T(8,128)S(1)} %fusion.54) | data formatting | bytes 622592 | tf_op jit(solution)/shard_map/reshape | solution.py:293
  12.1 1.5 %collective-permute-start.3 = (f32[32,2432]{1,0:T(8,128)}, f32[32,2432]{1,0:T(8,128)}, u32[]{:S(2)}, u32[]{:S(2)}) collective-permute-start(f32[32,2432]{1,0:T(8,128)} %reshape.464), channel_id=1, source_target_pairs={{0,2},{1,3},{2,0},{3,1},{4,6},{5,7},{6,4},{7,5},{8,10},{9,11},{10,... | collective-permute-start | bytes 933896 | tf_op jit(solution)/shard_map/ppermute | solution.py:31
  13.6 1.5 %collective-permute-start.4 = (f32[32,2432]{1,0:T(8,128)}, f32[32,2432]{1,0:T(8,128)}, u32[]{:S(2)}, u32[]{:S(2)}) collective-permute-start(f32[32,2432]{1,0:T(8,128)} %reshape.464), channel_id=1, source_target_pairs={{0,4},{1,5},{2,6},{3,7},{4,0},{5,1},{6,2},{7,3},{8,12},{9,13},{10,... | collective-permute-start | bytes 933896 | tf_op jit(solution)/shard_map/ppermute | solution.py:31
  15.2 0.1 lt.42
  15.3 0.1 pad.2.clone
  15.5 0.1 pad_maximum_fusion.own_ref
  15.6 1.9 %collective-permute-start = (f32[24,1024]{1,0:T(8,128)S(1)}, f32[24,1024]{1,0:T(8,128)S(1)}, u32[]{:S(2)}, u32[]{:S(2)}) collective-permute-start(f32[24,1024]{1,0:T(8,128)S(1)} %get-tuple-element.6), channel_id=1, source_target_pairs={{0,1},{1,2},{2,3},{3,4},{4,5},{5,6},{6,7},{7,8},{8,9},{9,10},{10,1... | collective-permute-start | bytes 294920 | tf_op jit(solution)/shard_map/ppermute | solution.py:25
  17.5 5.4 %collective-permute-start.1 = (f32[24,1024]{1,0:T(8,128)S(1)}, f32[24,1024]{1,0:T(8,128)S(1)}, u32[]{:S(2)}, u32[]{:S(2)}) collective-permute-start(f32[24,1024]{1,0:T(8,128)S(1)} %get-tuple-element.5), channel_id=1, source_target_pairs={{1,0},{2,1},{3,2},{4,3},{5,4},{6,5},{7,6},{8,7},{9,8},{10,9},{11,1... | collective-permute-start | bytes 294920 | tf_op jit(solution)/shard_map/ppermute | solution.py:26
  23.0 0.1 reshape.468
  23.1 4.8 %gather_fusion = s32[1024]{0:T(1024)S(1)} fusion(s32[5,16]{1,0:T(8,128)S(1)} %bitcast.56, s32[1024]{0:T(1024)S(1)} %reshape.468), kind=kCustom, calls=%fused_computation | custom fusion | bytes 16384 | tf_op jit(solution)/shard_map/gather | solution.py:300
  28.0 0.1 reshape.471
  28.1 1.4 %fusion.48 = f32[32,16,192]{2,1,0:T(8,128)} fusion(s32[32,32]{1,0:T(8,128)S(1)} %add_select_fusion.2, s32[32,32]{1,0:T(8,128)S(1)} %copy-done.14), kind=kOutput, calls=%fused_computation.47 | convolution fusion | flops 6504448 | bytes 401408 | tf_op jit(solution)/shard_map/lvr,lvt->ltr/dot_general | solution.py:310
  29.5 2.2 %copy.17 = f32[152,2432]{0,1:T(8,128)S(1)} copy(f32[152,2432]{1,0:T(8,128)} %param.18) | data formatting | bytes 2957312 | tf_op jit(solution)/shard_map/reshape | solution.py:271
  31.7 0.1 collective-permute-start.5
  31.8 3.0 %collective-permute-start.6 = (f32[32,2432]{1,0:T(8,128)}, f32[32,2432]{1,0:T(8,128)S(1)}, u32[]{:S(2)}, u32[]{:S(2)}) collective-permute-start(f32[32,2432]{1,0:T(8,128)} %reshape.464), channel_id=1, source_target_pairs={{0,16},{1,17},{2,18},{3,19},{4,20},{5,21},{6,22},{7,23},{8,24},{9,... | collective-permute-start | bytes 933896 | tf_op jit(solution)/shard_map/ppermute | solution.py:31
  34.8 21.1 %near.1 = f32[16,4096]{1,0:T(8,128)S(1)} custom-call(s32[1]{0:T(128)} %bitcast.first_ref, s32[32]{0:T(128)S(1)} %copy-done.1, f32[24,4096]{1,0:T(8,128)S(1)} %pad_maximum_fusion.own_ref, f32[24,1024]{1,0:T(8,128)S(1)} %collective-permute-done.low_ref, f32[24,1024]{1,0:T(8,128)S(1)} %collective-permute-done.1.high_ref, s32[32,27]{1,0:T(8,128)S(1)} %copy-done.2), custom_call_target="tpu_custom_call" | custom-call | flops 4000000000 | bytes 2000000 | tf_op jit(solution)/shard_map/near/pallas_call | solution.py:243
  56.0 1.0 %constant_dynamic-update-slice_fusion.5 = f32[192,2432]{1,0:T(8,128)S(1)} fusion(f32[32,2432]{1,0:T(8,128)} %collective-permute-done.2), kind=kLoop, calls=%fused_computation.95 | loop fusion | bytes 622592
  57.0 1.0 %constant_dynamic-update-slice_fusion.4 = f32[192,2432]{1,0:T(8,128)S(1)} fusion(f32[192,2432]{1,0:T(8,128)S(1)} %constant_dynamic-update-slice_fusion.5, f32[32,2432]{1,0:T(8,128)} %collective-permute-done.3), kind=kLoop, calls=%fused_computation.94 | loop fusion | bytes 622592
  58.0 1.0 %constant_dynamic-update-slice_fusion.3 = f32[192,2432]{1,0:T(8,128)S(1)} fusion(f32[192,2432]{1,0:T(8,128)S(1)} %constant_dynamic-update-slice_fusion.4, f32[32,2432]{1,0:T(8,128)} %collective-permute-done.4), kind=kLoop, calls=%fused_computation.93 | loop fusion | bytes 622592
  59.1 1.0 %constant_dynamic-update-slice_fusion = f32[192,2432]{1,0:T(8,128)S(1)} fusion(f32[192,2432]{1,0:T(8,128)S(1)} %constant_dynamic-update-slice_fusion.1, f32[32,2432]{1,0:T(8,128)} %reshape.464), kind=kLoop, calls=%fused_computation.90 | loop fusion | bytes 622592 | tf_op jit(solution)/shard_map/concatenate | solution.py:297
  60.1 6.1 %fusion.24 = f32[32,16,2432]{2,1,0:T(8,128)} fusion(f32[32,16,192]{2,1,0:T(8,128)S(1)} %copy-done.3, f32[192,2432]{1,0:T(8,128)S(1)} %constant_dynamic-update-slice_fusion), kind=kOutput, calls=%fused_computation.25 | convolution fusion | flops 2868903936 | bytes 7241728 | tf_op jit(solution)/shard_map/ltr,rc->ltc/dot_general | solution.py:311
  66.2 13.4 %reshape.465 = f32[32,16,16,152]{3,2,1,0:T(8,128)} reshape(f32[32,16,2432]{2,1,0:T(8,128)} %fusion.24) | data formatting | bytes 9961472 | tf_op jit(solution)/shard_map/reshape | solution.py:312
  79.7 9.6 %convolution_bitcast_fusion = f32[32,16,152]{2,1,0:T(8,128)S(1)} fusion(f32[32,16,16,152]{3,2,1,0:T(8,128)} %reshape.465, f32[152,16,152,1]{0,2,1,3:T(8,128)S(1)} %bitcast.57), kind=kOutput, calls=%fused_computation.43 | convolution fusion | flops 2271215616 | bytes 6770688 | tf_op jit(solution)/shard_map/ltqj,itj->lqi/dot_general | solution.py:313
  89.3 0.6 fusion.52
  90.0 5.1 %fusion.45 = f32[32,2,8,128]{3,2,1,0:T(8,128)S(1)} fusion(f32[32,16,152]{2,1,0:T(8,128)S(1)} %fusion.52, f32[32,152]{1,0:T(8,128)S(1)} %copy-done.11, f32[32,128]{1,0:T(8,128)S(1)} %copy-done.16, f32[32,152]{1,0:T(8,128)S(1)} %copy-done.13, f32[32,128]{1,0:T(8,128)S(1)} %copy-done.18, f32[32,152]{1,0:T(8,128)S(1)} %copy-done.9, ...), kind=kOutput, calls=%fused_computation.45 | convolution fusion | flops 125829120 | bytes 697344 | tf_op jit(solution)/shard_map/lpj,lqj->qlp/dot_general | solution.py:70
  95.1 0.7 bitcast_add_fusion
  (67 shorter events, 0.5 us)
Async XLA Ops:
  0.0 10.5 %copy-start = (f32[152,152]{1,0:T(8,128)S(1)}, f32[152,152]{1,0:T(8,128)}, u32[]{:S(2)}) copy-start(f32[152,152]{1,0:T(8,128)} %param.19) | copy-start | bytes 277252
  1.0 2.6 %copy-start.15 = (f32[32,128]{1,0:T(8,128)}, f32[32,128]{1,0:T(8,128)S(1)}, u32[]{:S(2)}) copy-start(f32[32,128]{1,0:T(8,128)S(1)} %get-tuple-element.11) | copy-start | bytes 49156
  1.0 2.6 %copy-start.17 = (f32[32,128]{1,0:T(8,128)}, f32[32,128]{1,0:T(8,128)S(1)}, u32[]{:S(2)}) copy-start(f32[32,128]{1,0:T(8,128)S(1)} %get-tuple-element.12) | copy-start | bytes 49156
  1.8 1.8 %copy-start.8 = (f32[32,152]{1,0:T(8,128)}, f32[32,152]{1,0:T(8,128)S(1)}, u32[]{:S(2)}) copy-start(f32[32,152]{1,0:T(8,128)S(1)} %get-tuple-element.7) | copy-start | bytes 58372
  1.8 1.8 %copy-start.10 = (f32[32,152]{1,0:T(8,128)}, f32[32,152]{1,0:T(8,128)S(1)}, u32[]{:S(2)}) copy-start(f32[32,152]{1,0:T(8,128)S(1)} %get-tuple-element.8) | copy-start | bytes 58372
  1.8 1.8 %copy-start.12 = (f32[32,152]{1,0:T(8,128)}, f32[32,152]{1,0:T(8,128)S(1)}, u32[]{:S(2)}) copy-start(f32[32,152]{1,0:T(8,128)S(1)} %get-tuple-element.9) | copy-start | bytes 58372
  3.7 11.4 %copy-start.1 = (s32[32]{0:T(128)S(1)}, s32[32]{0:T(128)}, u32[]{:S(2)}) copy-start(s32[32]{0:T(128)} %counts_ref.1) | copy-start | bytes 388
  3.7 11.4 %copy-start.5 = (f32[3,4096]{1,0:T(4,128)S(1)}, f32[3,4096]{1,0:T(4,128)}, u32[]{:S(2)}) copy-start(f32[3,4096]{1,0:T(4,128)} %param.11) | copy-start | bytes 147460
  3.7 11.6 %copy-start.4 = (f32[16,4096]{1,0:T(8,128)S(1)}, f32[16,4096]{1,0:T(8,128)}, u32[]{:S(2)}) copy-start(f32[16,4096]{1,0:T(8,128)} %param.12) | copy-start | bytes 786436
  10.5 12.5 %copy-start.7 = (s32[32,32]{1,0:T(8,128)S(1)}, s32[32,32]{1,0:T(8,128)}, u32[]{:S(2)}) copy-start(s32[32,32]{1,0:T(8,128)} %param.15) | copy-start | bytes 12292
  10.5 12.6 %copy-start.19 = (s32[1,5,16]{2,0,1:T(1,128)S(1)}, s32[1,5,16]{2,0,1:T(1,128)}, u32[]{:S(2)}) copy-start(s32[1,5,16]{2,0,1:T(1,128)} %param.17) | copy-start | bytes 964
  12.1 43.9 %collective-permute-start.2 = (f32[32,2432]{1,0:T(8,128)}, f32[32,2432]{1,0:T(8,128)}, u32[]{:S(2)}, u32[]{:S(2)}) collective-permute-start(f32[32,2432]{1,0:T(8,128)} %reshape.464), channel_id=1, source_target_pairs={{0,1},{1,0},{2,3},{3,2},{4,5},{5,4},{6,7},{7,6},{8,9},{9,8},{10,11... | collective-permute-start | bytes 933896 | tf_op jit(solution)/shard_map/ppermute | solution.py:31
  12.1 44.9 %collective-permute-start.3 = (f32[32,2432]{1,0:T(8,128)}, f32[32,2432]{1,0:T(8,128)}, u32[]{:S(2)}, u32[]{:S(2)}) collective-permute-start(f32[32,2432]{1,0:T(8,128)} %reshape.464), channel_id=1, source_target_pairs={{0,2},{1,3},{2,0},{3,1},{4,6},{5,7},{6,4},{7,5},{8,10},{9,11},{10,... | collective-permute-start | bytes 933896 | tf_op jit(solution)/shard_map/ppermute | solution.py:31
  13.6 44.4 %collective-permute-start.4 = (f32[32,2432]{1,0:T(8,128)}, f32[32,2432]{1,0:T(8,128)}, u32[]{:S(2)}, u32[]{:S(2)}) collective-permute-start(f32[32,2432]{1,0:T(8,128)} %reshape.464), channel_id=1, source_target_pairs={{0,4},{1,5},{2,6},{3,7},{4,0},{5,1},{6,2},{7,3},{8,12},{9,13},{10,... | collective-permute-start | bytes 933896 | tf_op jit(solution)/shard_map/ppermute | solution.py:31
  15.6 16.1 %collective-permute-start = (f32[24,1024]{1,0:T(8,128)S(1)}, f32[24,1024]{1,0:T(8,128)S(1)}, u32[]{:S(2)}, u32[]{:S(2)}) collective-permute-start(f32[24,1024]{1,0:T(8,128)S(1)} %get-tuple-element.6), channel_id=1, source_target_pairs={{0,1},{1,2},{2,3},{3,4},{4,5},{5,6},{6,7},{7,8},{8,9},{9,10},{10,1... | collective-permute-start | bytes 294920 | tf_op jit(solution)/shard_map/ppermute | solution.py:25
  17.5 14.3 %collective-permute-start.1 = (f32[24,1024]{1,0:T(8,128)S(1)}, f32[24,1024]{1,0:T(8,128)S(1)}, u32[]{:S(2)}, u32[]{:S(2)}) collective-permute-start(f32[24,1024]{1,0:T(8,128)S(1)} %get-tuple-element.5), channel_id=1, source_target_pairs={{1,0},{2,1},{3,2},{4,3},{5,4},{6,5},{7,6},{8,7},{9,8},{10,9},{11,1... | collective-permute-start | bytes 294920 | tf_op jit(solution)/shard_map/ppermute | solution.py:26
  23.1 5.0 %copy-start.14 = (s32[32,32]{1,0:T(8,128)S(1)}, s32[32,32]{1,0:T(8,128)}, u32[]{:S(2)}) copy-start(s32[32,32]{1,0:T(8,128)} %param.16) | copy-start | bytes 12292
  28.0 6.9 %copy-start.2 = (s32[32,27]{1,0:T(8,128)S(1)}, s32[32,27]{1,0:T(8,128)}, u32[]{:S(2)}) copy-start(s32[32,27]{1,0:T(8,128)} %ulist_ref.1) | copy-start | bytes 10372
  31.7 27.3 %collective-permute-start.5 = (f32[32,2432]{1,0:T(8,128)}, f32[32,2432]{1,0:T(8,128)S(1)}, u32[]{:S(2)}, u32[]{:S(2)}) collective-permute-start(f32[32,2432]{1,0:T(8,128)} %reshape.464), channel_id=1, source_target_pairs={{0,8},{1,9},{2,10},{3,11},{4,12},{5,13},{6,14},{7,15},{8,0},{9,1},... | collective-permute-start | bytes 933896 | tf_op jit(solution)/shard_map/ppermute | solution.py:31
  31.8 27.3 %collective-permute-start.6 = (f32[32,2432]{1,0:T(8,128)}, f32[32,2432]{1,0:T(8,128)S(1)}, u32[]{:S(2)}, u32[]{:S(2)}) collective-permute-start(f32[32,2432]{1,0:T(8,128)} %reshape.464), channel_id=1, source_target_pairs={{0,16},{1,17},{2,18},{3,19},{4,20},{5,21},{6,22},{7,23},{8,24},{9,... | collective-permute-start | bytes 933896 | tf_op jit(solution)/shard_map/ppermute | solution.py:31
  56.0 4.2 %copy-start.3 = (f32[32,16,192]{2,1,0:T(8,128)S(1)}, f32[32,16,192]{2,1,0:T(8,128)}, u32[]{:S(2)}) copy-start(f32[32,16,192]{2,1,0:T(8,128)} %fusion.48) | copy-start | bytes 1179652
  79.7 9.6 %copy-start.6 = (f32[152,152]{1,0:T(8,128)S(1)}, f32[152,152]{1,0:T(8,128)}, u32[]{:S(2)}) copy-start(f32[152,152]{1,0:T(8,128)} %param.20) | copy-start | bytes 277252
  79.7 10.2 %copy-start.9 = (f32[32,152]{1,0:T(8,128)S(1)}, f32[32,152]{1,0:T(8,128)}, u32[]{:S(2)}) copy-start(f32[32,152]{1,0:T(8,128)} %copy-done.8) | copy-start | bytes 58372
  79.7 10.2 %copy-start.11 = (f32[32,152]{1,0:T(8,128)S(1)}, f32[32,152]{1,0:T(8,128)}, u32[]{:S(2)}) copy-start(f32[32,152]{1,0:T(8,128)} %copy-done.10) | copy-start | bytes 58372
  79.7 10.3 %copy-start.13 = (f32[32,152]{1,0:T(8,128)S(1)}, f32[32,152]{1,0:T(8,128)}, u32[]{:S(2)}) copy-start(f32[32,152]{1,0:T(8,128)} %copy-done.12) | copy-start | bytes 58372
  79.7 10.3 %copy-start.16 = (f32[32,128]{1,0:T(8,128)S(1)}, f32[32,128]{1,0:T(8,128)}, u32[]{:S(2)}) copy-start(f32[32,128]{1,0:T(8,128)} %copy-done.15) | copy-start | bytes 49156
  79.7 10.3 %copy-start.18 = (f32[32,128]{1,0:T(8,128)S(1)}, f32[32,128]{1,0:T(8,128)}, u32[]{:S(2)}) copy-start(f32[32,128]{1,0:T(8,128)} %copy-done.17) | copy-start | bytes 49156

commit v2 on v1

--- a/solution.py
+++ b/solution.py
@@ -18,15 +18,6 @@
 highest = lax.Precision.HIGHEST
 
 
-def halo(block, axis, width):
-    count = lax.axis_size(axis)
-    forward = [(i, i + 1) for i in range(count - 1)]
-    backward = [(target, source) for source, target in forward]
-    low = lax.ppermute(block[:, block.shape[1] - width:], axis, forward)
-    high = lax.ppermute(block[:, :width], axis, backward)
-    return low, high
-
-
 def from_partner(array, axis, bit):
     return lax.ppermute(array, axis, [(i, i ^ 1 << bit) for i in range(lax.axis_size(axis))])
 
@@ -37,37 +28,6 @@
     coords = (coords - 2.5) / 2.5
     on_face = np.max(np.abs(coords), axis=0) > 0.99
     return coords[:, on_face].astype(np.float32)
-
-
-def leaf_corner(leaf_ids):
-    corners = []
-    for axis_num in range(3):
-        summed = jnp.zeros_like(leaf_ids)
-        for digit_num in range(10):
-            summed = summed + ((leaf_ids >> 3 * digit_num + axis_num & 1) << digit_num)
-        corners.append(summed)
-    return jnp.stack(corners, 0).astype(jnp.float32)
-
-
-def kernel(targets, sources):
-    squared = jnp.zeros((targets.shape[-1], sources.shape[-1]), jnp.float32)
-    for axis_num in range(3):
-        squared = squared + (targets[axis_num][:, None] - sources[axis_num][None, :]) ** 2
-    return inv_four_pi * lax.rsqrt(squared + soften)
-
-
-def upward(points, masked, centers, surface, uc2e):
-    checks = centers[:, :, None] + surface_radius * surface[:, None, :]
-    tiles = jax.vmap(kernel, in_axes=(1, 1))(checks, points)
-    potent = jnp.einsum("ljp,qlp->lqj", tiles, masked, precision=highest)
-    return jnp.einsum("lqj,ij->lqi", potent, uc2e, precision=highest)
-
-
-def downward(points, centers, surface, downcheck, dc2e):
-    downeq = jnp.einsum("lqi,ji->lqj", downcheck, dc2e, precision=highest)
-    equivs = centers[:, :, None] + surface_radius * surface[:, None, :]
-    tiles = jax.vmap(kernel, in_axes=(1, 1))(points, equivs)
-    return jnp.einsum("lpj,lqj->qlp", tiles, downeq, precision=highest)
 
 
 def near_kernel(first_ref, counts_ref, own_ref, low_ref, high_ref, ulist_ref, out_ref,
@@ -262,59 +222,297 @@
     )(first, counts, own, low, high, u_list)
 
 
+def split(value):
+    high = value.astype(jnp.bfloat16)
+    return high, (value - high.astype(jnp.float32)).astype(jnp.bfloat16)
+
+
+def dot(left, right):
+    return jnp.dot(left, right, preferred_element_type=jnp.float32)
+
+
+def dot_t(left, right):
+    return lax.dot_general(left, right, (((1,), (1,)), ((), ())), preferred_element_type=jnp.float32)
+
+
+def dot_t3(left, right):
+    left_hi, left_lo = split(left)
+    right_hi, right_lo = split(right)
+    return dot_t(left_hi, right_hi) + (dot_t(left_hi, right_lo) + dot_t(left_lo, right_hi))
+
+
+def corner_of(leaf, axis):
+    summed = jnp.int32(0)
+    for digit in range(10):
+        summed = summed + (((leaf >> (3 * digit + axis)) & 1) << digit)
+    return summed.astype(jnp.float32)
+
+
+def surface_tile(local, surface):
+    norm = local[0:1] * local[0:1] + (local[1:2] * local[1:2] + local[2:3] * local[2:3])
+    s = (norm + surface[:, 3:4]) + surface[:, 0:1] * local[0:1]
+    s = s + (surface[:, 1:2] * local[1:2] + surface[:, 2:3] * local[2:3])
+    return lax.rsqrt(s)
+
+
+def surface_rows():
+    points = surface_radius * surface_table().astype(np.float64)
+    count = points.shape[1]
+    rows = np.zeros((-(-count // 16) * 16, 8), np.float32)
+    rows[:count, :3] = -2.0 * points.T
+    rows[:count, 3] = (points ** 2).sum(0) + soften
+    rows[count:, 3] = 1.0
+    return rows
+
+
+def padded(ref, rows, lanes):
+    value = ref[...]
+    if value.shape[1] < lanes:
+        value = jnp.concatenate([value, jnp.zeros((value.shape[0], lanes - value.shape[1]), value.dtype)], 1)
+    if value.shape[0] < rows:
+        value = jnp.concatenate([value, jnp.zeros((rows - value.shape[0], lanes), value.dtype)], 0)
+    return value
+
+
+def up_kernel(first_ref, counts_ref, offsets_ref, charges_ref, uc2e_ref, surface_ref,
+              own_ref, low_ref, high_ref, up_ref, check_ref):
+    f32, i32 = jnp.float32, jnp.int32
+    probes, points = charges_ref.shape
+    local = points // PTS
+    lane = lax.broadcasted_iota(i32, (1, PTS), 1)
+    sub = lax.broadcasted_iota(i32, (8, PTS), 0)
+    first = first_ref[0]
+    surface = surface_ref[...]
+    zero = jnp.zeros((probes, PTS), jnp.bfloat16)
+
+    for g in range(0, local, 2):
+        parts = []
+        for h in (g, g + 1):
+            at = slice(h * PTS, (h + 1) * PTS)
+            corner = [corner_of(first + h, axis) for axis in range(3)]
+            held = counts_ref[h]
+            xyz = jnp.concatenate([offsets_ref[:, at], jnp.zeros((5, PTS), f32)], 0)
+            move = jnp.where(sub == 0, corner[0], jnp.where(sub == 1, corner[1], jnp.where(sub == 2, corner[2],
+                   jnp.where(sub == 3, held.astype(f32), 0.0))))
+            own_ref[0:8, at] = xyz + move
+            masked = jnp.where(lane < held, charges_ref[:, at], 0.0)
+            own_ref[8:8 + probes, at] = masked
+            parts.append(split(masked))
+        both = offsets_ref[:, g * PTS:(g + 2) * PTS] - 0.5
+        tile_hi, tile_lo = split(surface_tile(both, surface))
+        left = jnp.concatenate([parts[0][0], zero], 1), jnp.concatenate([zero, parts[1][0]], 1)
+        small = jnp.concatenate([parts[0][1], zero], 1), jnp.concatenate([zero, parts[1][1]], 1)
+        large = dot_t(jnp.concatenate(left + small, 0), tile_hi)
+        fine = dot_t(jnp.concatenate(left, 0), tile_lo)
+        value = (large[:2 * probes] + (large[2 * probes:] + fine)) * inv_four_pi
+        gap = jnp.zeros((2 * probes, 2 * PTS - value.shape[1]), f32)
+        value = jnp.concatenate([value, gap], 1)
+        for half in range(2):
+            at = slice(half * PTS, (half + 1) * PTS)
+            check_ref[half, pl.ds(g, probes, stride=local), :] = value[:probes, at]
+            check_ref[half, pl.ds(g + 1, probes, stride=local), :] = value[probes:, at]
+    low_ref[...] = own_ref[:, points - GHOST * PTS:]
+    high_ref[...] = own_ref[:, :GHOST * PTS]
+
+    equiv = uc2e_ref.shape[0]
+    up = dot_t3(jnp.concatenate([check_ref[0], check_ref[1]], 1), padded(uc2e_ref, 2 * PTS, 2 * PTS))
+    rows = probes * local
+    up_ref[:rows] = up[:, :PTS]
+    rest = rows // 4
+    tail = up[:rest, PTS:]
+    for k in range(1, 4):
+        tail = tail + pltpu.roll(up[k * rest:(k + 1) * rest, PTS:], 32 * k, 1)
+    up_ref[rows:] = tail
+
+
+def up_call(first, counts, offsets, charges, uc2e):
+    local = counts.shape[0]
+    probes, points = charges.shape
+    smem = pl.BlockSpec(memory_space=pltpu.SMEM)
+    vmem = pl.BlockSpec(memory_space=pltpu.VMEM)
+    f32 = jnp.float32
+    return pl.pallas_call(
+        up_kernel,
+        out_shape=(
+            jax.ShapeDtypeStruct((8 + probes, points), f32),
+            jax.ShapeDtypeStruct((8 + probes, GHOST * PTS), f32),
+            jax.ShapeDtypeStruct((8 + probes, GHOST * PTS), f32),
+            jax.ShapeDtypeStruct((probes * local * 5 // 4, PTS), f32),
+        ),
+        in_specs=[smem, smem, vmem, vmem, vmem, vmem],
+        out_specs=(vmem, vmem, vmem, vmem),
+        scratch_shapes=[pltpu.VMEM((2, probes * local, PTS), f32)],
+        compiler_params=pltpu.CompilerParams(vmem_limit_bytes=32 << 20),
+        cost_estimate=pl.CostEstimate(flops=500_000_000, bytes_accessed=1_500_000, transcendentals=600_000),
+        name="upward",
+    )(first, counts, offsets, charges, uc2e, jnp.asarray(surface_rows()))
+
+
+def far_kernel(counts_ref, wanted_ref, offsets_ref, near_ref, vsrc_ref, vtype_ref, m2l_ref, dc2e_ref, surface_ref,
+               *refs):
+    f32, bf16, i32 = jnp.float32, jnp.bfloat16, jnp.int32
+    pieces = refs[:-9]
+    out_ref, code_ref, tally_ref, table_ref, x_hi_ref, x_lo_ref, w_hi_ref, w_lo_ref, eq_ref = refs[-9:]
+    probes, points = out_ref.shape
+    local = points // PTS
+    bits, cap = wanted_ref.shape
+    depth = len(pieces) * local
+    equiv = m2l_ref.shape[0]
+    kinds = m2l_ref.shape[1] // equiv
+    rest = equiv - PTS
+    rows = probes * local
+    lane = lax.broadcasted_iota(i32, (1, PTS), 1)
+
+    w_hi_ref[...] = jnp.zeros_like(w_hi_ref)
+    w_lo_ref[...] = jnp.zeros_like(w_lo_ref)
+    grown = w_hi_ref.shape[0]
+    fill = jnp.zeros((grown - equiv, PTS), f32)
+    for t in range(kinds):
+        main = jnp.concatenate([m2l_ref[:, t * equiv:t * equiv + PTS], fill], 0)
+        w_hi_ref[:, t * PTS:(t + 1) * PTS], w_lo_ref[:, t * PTS:(t + 1) * PTS] = split(main)
+    gap = jnp.zeros((equiv, 32 - rest), f32)
+    for t in range(0, kinds, 4):
+        row = []
+        for k in range(4):
+            row += [m2l_ref[:, (t + k) * equiv + PTS:(t + k + 1) * equiv], gap]
+        tail = jnp.concatenate([jnp.concatenate(row, 1), fill], 0)
+        at = kinds * PTS + t * 32
+        w_hi_ref[:, at:at + PTS], w_lo_ref[:, at:at + PTS] = split(tail)
+
+    codes = vsrc_ref[...]
+    slots = codes.shape[1]
+    found = codes - bits * cap + bits * local
+    for b in range(bits):
+        for s in range(cap):
+            found = jnp.where(codes == b * cap + s, b * local + wanted_ref[b, s], found)
+    code_ref[...] = jnp.full(code_ref.shape, -1.0, f32)
+    code_ref[0:local, 0:slots] = found.astype(f32)
+    code_ref[local:, 0:slots] = vtype_ref[...].astype(f32)
+
+    per = PTS // slots
+    spot = lax.broadcasted_iota(i32, (8, 8 * slots), 1) // slots == lax.broadcasted_iota(i32, (8, 8 * slots), 0)
+
+    def flat(value):
+        wide = jnp.where(lane < slots, value, 0.0)
+        total = wide
+        for k in range(1, per):
+            total = total + pltpu.roll(wide, slots * k, 1)
+        total = jnp.concatenate([total] * (8 // per), 1)
+        return jnp.sum(jnp.where(spot, total, 0.0), 0, keepdims=True)
+
+    row_id = lax.broadcasted_iota(i32, (8 * kinds, 8 * slots), 0)
+    mine = lax.broadcasted_iota(i32, (8 * kinds, 8 * slots), 1) // slots == row_id % 8
+    kind = (row_id // 8).astype(f32)
+    table_row = lax.broadcasted_iota(i32, (depth, 8 * slots), 0).astype(f32)
+    for g in range(0, local, 8):
+        take = flat(code_ref[g:g + 8, :])
+        sort = flat(code_ref[local + g:local + g + 8, :])
+        pick = jnp.where(mine & (sort == kind), 1.0, 0.0).astype(bf16)
+        hit = jnp.where(take == table_row, 1.0, 0.0).astype(bf16)
+        count = dot_t(pick, hit)
+        for t in range(kinds):
+            tally_ref[t * local + g:t * local + g + 8, :] = count[8 * t:8 * t + 8]
+    tally = tally_ref[...].astype(bf16)
+
+    blocks = pieces[0].shape[0] // local
+    for b, piece in enumerate(pieces):
+        for n in range(blocks):
+            hi, lo = split(piece[n * local:(n + 1) * local, :])
+            table_ref[b * local:(b + 1) * local, n * PTS:(n + 1) * PTS] = hi
+            table_ref[depth + b * local:depth + (b + 1) * local, n * PTS:(n + 1) * PTS] = lo
+
+    twice = jnp.concatenate([tally, tally], 1)
+    group = lane // 32
+    quarter = probes // 4
+    for n in range(0, blocks, 2):
+        both = dot(twice, table_ref[:, n * PTS:(n + 2) * PTS])
+        for half in range(2):
+            q = n + half
+            part = both[:, half * PTS:(half + 1) * PTS]
+            if q < probes:
+                hi, lo = split(part)
+                for t in range(kinds):
+                    x_hi_ref[q * local:(q + 1) * local, t * PTS:(t + 1) * PTS] = hi[t * local:(t + 1) * local]
+                    x_lo_ref[q * local:(q + 1) * local, t * PTS:(t + 1) * PTS] = lo[t * local:(t + 1) * local]
+            else:
+                for k in range(4):
+                    to = (q - probes + quarter * k) * local
+                    for t in range(0, kinds, 4):
+                        value = jnp.zeros((local, PTS), f32)
+                        for i in range(4):
+                            moved = part[(t + i) * local:(t + i + 1) * local]
+                            if i != k:
+                                moved = pltpu.roll(moved, (32 * (i - k)) % PTS, 1)
+                            value = jnp.where(group == i, moved, value)
+                        at = kinds * PTS + t * 32
+                        x_hi_ref[to:to + local, at:at + PTS], x_lo_ref[to:to + local, at:at + PTS] = split(value)
+
+    down = dot_t(x_hi_ref[...], w_hi_ref[...]) + (dot_t(x_hi_ref[...], w_lo_ref[...]) + dot_t(x_lo_ref[...], w_hi_ref[...]))
+    equivs = dot_t3(down, padded(dc2e_ref, 2 * PTS, 2 * PTS))
+    eq_ref[0], eq_ref[1] = equivs[:, :PTS], equivs[:, PTS:]
+
+    surface = surface_ref[...]
+    reach = surface.shape[0]
+    for g in range(0, local, 2):
+        at = slice(g * PTS, (g + 2) * PTS)
+        tile_hi, tile_lo = split(surface_tile(offsets_ref[:, at] - 0.5, surface))
+        parts = []
+        for h in (g, g + 1):
+            value = jnp.concatenate([eq_ref[half, pl.ds(h, probes, stride=local), :] for half in range(2)], 1)[:, :reach]
+            parts.append(split(value))
+        left = parts[0][0], parts[1][0]
+        large = dot(jnp.concatenate(left + (parts[0][1], parts[1][1]), 0), tile_hi)
+        value = large[:2 * probes] + (large[2 * probes:] + dot(jnp.concatenate(left, 0), tile_lo))
+        for i in range(2):
+            h = g + i
+            to = slice(h * PTS, (h + 1) * PTS)
+            part = value[i * probes:(i + 1) * probes, i * PTS:(i + 1) * PTS] * inv_four_pi
+            out_ref[:, to] = jnp.where(lane < counts_ref[h], near_ref[:, to] + part, 0.0)
+
+
+def far_call(counts, wanted, offsets, near, v_src, v_type, m2l, dc2e, pieces):
+    local = counts.shape[0]
+    probes, points = near.shape
+    equiv = dc2e.shape[0]
+    kinds = m2l.shape[1] // equiv
+    smem = pl.BlockSpec(memory_space=pltpu.SMEM)
+    vmem = pl.BlockSpec(memory_space=pltpu.VMEM)
+    f32, bf16 = jnp.float32, jnp.bfloat16
+    rows = probes * local
+    wide = kinds * (PTS + 32)
+    return pl.pallas_call(
+        far_kernel,
+        out_shape=jax.ShapeDtypeStruct((probes, points), f32),
+        in_specs=[smem, smem] + [vmem] * (7 + len(pieces)),
+        out_specs=vmem,
+        scratch_shapes=[
+            pltpu.VMEM((2 * local, PTS), f32),
+            pltpu.VMEM((kinds * local, len(pieces) * local), f32),
+            pltpu.VMEM((2 * len(pieces) * local, pieces[0].shape[0] // local * PTS), bf16),
+            pltpu.VMEM((rows, wide), bf16),
+            pltpu.VMEM((rows, wide), bf16),
+            pltpu.VMEM((2 * PTS, wide), bf16),
+            pltpu.VMEM((2 * PTS, wide), bf16),
+            pltpu.VMEM((2, rows, PTS), f32),
+        ],
+        compiler_params=pltpu.CompilerParams(vmem_limit_bytes=40 << 20),
+        cost_estimate=pl.CostEstimate(flops=4_000_000_000, bytes_accessed=4_000_000, transcendentals=600_000),
+        name="far",
+    )(counts, wanted, offsets, near, v_src, v_type, m2l, dc2e, jnp.asarray(surface_rows()), *pieces)
+
+
 def shards(offsets, charges, counts, u_list, v_src, v_type, wanted, m2l, uc2e, dc2e):
     local_leaves = counts.shape[0]
-    per_leaf = offsets.shape[1] // local_leaves
-    probes = charges.shape[0]
-    equiv = uc2e.shape[0]
-    kinds_count = m2l.shape[1] // equiv
-    m2l_ops = m2l.reshape(equiv, kinds_count, equiv)
-    bits = lax.axis_size("cube").bit_length() - 1
-    read_cap = wanted.shape[2]
-    surface = jnp.asarray(surface_table())
-    first = lax.axis_index("cube") * local_leaves
-    leaf_ids = first + jnp.arange(local_leaves, dtype=jnp.int32)
-    inside = (jnp.arange(per_leaf, dtype=jnp.int32)[None, :] < counts[:, None]).astype(jnp.float32)
-    corners = leaf_corner(leaf_ids)
-    centers = corners + 0.5
-    points = offsets.reshape(3, local_leaves, per_leaf) + corners[:, :, None]
-    masked = charges.reshape(probes, local_leaves, per_leaf) * inside[None]
-    held = jnp.broadcast_to(counts.astype(jnp.float32)[:, None], (local_leaves, per_leaf))
-    own = jnp.concatenate(
-        [
-            points.reshape(3, local_leaves * per_leaf),
-            held.reshape(1, local_leaves * per_leaf),
-            jnp.zeros((4, local_leaves * per_leaf), jnp.float32),
-            masked.reshape(probes, local_leaves * per_leaf),
-        ],
-        0,
-    )
-    low, high = halo(own, "cube", GHOST * per_leaf)
-    up_flat = upward(points, masked, centers, surface, uc2e).reshape(local_leaves, probes * equiv)
-    pieces = []
-    for bit_num in range(bits):
-        pieces.append(from_partner(up_flat, "cube", bit_num))
-    table = jnp.concatenate(pieces + [up_flat], 0)
-    bit_part = jnp.minimum(v_src // read_cap, bits - 1)
-    slot_part = v_src % read_cap
-    remote_leaf = wanted[0][bit_part, slot_part]
-    rows = jnp.where(
-        v_src >= bits * read_cap,
-        bits * local_leaves + v_src - bits * read_cap,
-        bit_part * local_leaves + remote_leaf,
-    )
-    row_ids = jnp.arange(table.shape[0], dtype=jnp.int32)
-    type_ids = jnp.arange(kinds_count, dtype=jnp.int32)
-    onehot_rows = (rows[:, :, None] == row_ids[None, None, :]).astype(jnp.float32)
-    onehot_types = (v_type[:, :, None] == type_ids[None, None, :]).astype(jnp.float32)
-    tally = jnp.einsum("lvr,lvt->ltr", onehot_rows, onehot_types)
-    by_type = jnp.einsum("ltr,rc->ltc", tally, table, precision=highest)
-    by_type = by_type.reshape(local_leaves, kinds_count, probes, equiv)
-    downcheck = jnp.einsum("ltqj,itj->lqi", by_type, m2l_ops, precision=highest)
-    far = downward(points, centers, surface, downcheck, dc2e)
-    near = near_call(first.reshape(1).astype(jnp.int32), counts, own, low, high, u_list)
-    potential = near + (far * inside[None]).reshape(probes, local_leaves * per_leaf)
-    return potential
+    first = (lax.axis_index("cube") * local_leaves).astype(jnp.int32).reshape(1)
+    own, to_next, to_last, up = up_call(first, counts, offsets, charges, uc2e)
+    count = lax.axis_size("cube")
+    forward = [(i, i + 1) for i in range(count - 1)]
+    backward = [(target, source) for source, target in forward]
+    low = lax.ppermute(to_next, "cube", forward)
+    high = lax.ppermute(to_last, "cube", backward)
+    pieces = [from_partner(up, "cube", bit) for bit in range(count.bit_length() - 1)] + [up]
+    near = near_call(first, counts, own, low, high, u_list)
+    return far_call(counts, wanted[0], offsets, near, v_src, v_type, m2l, dc2e, pieces)
 
 
 def solution(mesh):

time: 96.4 us -> 52.8 us (0.55)
  the two profiles are of different devices: /device:TPU:8 before, /device:TPU:15 now
where the time goes in v2:
time: 52.8 us; the launch traced here: 52.3 us
  Pallas kernels  32 us (61%)
  starting transfers between devices  8.68 us (16%)
  waiting for transfers between devices  7.15 us (14%)
  local copies, waits for them, and re-layouts  4.32 us (8%)
    pallas_call x1, Pallas kernels, near_call(): pl.pallas_call(near_kernel, out_shape=jax.ShapeDtypeStruct((probes, local...  19.3 us
    pallas_call x1, Pallas kernels, far_call(): pl.pallas_call(far_kernel, out_shape=jax.ShapeDtypeStruct((probes, points...  10.1 us
    ppermute x1, waiting for transfers between devices, shards(): high = lax.ppermute(to_last, 'cube', backward)  7.13 us
    unnamed x29, local copies, waits for them, and re-layouts  4.32 us
    ppermute x1, starting transfers between devices, shards(): low = lax.ppermute(to_next, 'cube', forward)  3.67 us
    ppermute x5, starting transfers between devices, from_partner(): lax.ppermute(array, axis, [(i, i ^ 1 << bit) for i in range(lax.axis_size...  3.09 us
    pallas_call x1, Pallas kernels, up_call(): pl.pallas_call(up_kernel, out_shape=(jax.ShapeDtypeStruct((8 + probes, po...  2.64 us
    ppermute x1, starting transfers between devices, shards(): high = lax.ppermute(to_last, 'cube', backward)  1.92 us
  transfers between devices with their start and end apart: 7, of which 1 were waited for; matrix products, arithmetic and copies ran while one was open for 0% of the time, Pallas kernels for 37%

profile of v2, /device:TPU:15, one launch (start us, length us, event | category | flops | bytes accessed | tf_op | source)
XLA Modules:
  0.0 52.3 jit_solution(7042103973691346374)
XLA Ops:
  0.0 1.0 %copy-done.1 = f32[16,4096]{1,0:T(8,128)S(1)} copy-done((f32[16,4096]{1,0:T(8,128)S(1)}, f32[16,4096]{1,0:T(8,128)}, u32[]{:S(2)}) %copy-start.1) | copy-done | bytes 262168
  1.0 0.9 %copy-done.2 = f32[152,152]{1,0:T(8,128)S(1)} copy-done((f32[152,152]{1,0:T(8,128)S(1)}, f32[152,152]{1,0:T(8,128)}, u32[]{:S(2)}) %copy-start.2) | copy-done | bytes 92440
  1.9 0.8 %copy-done.4 = f32[3,4096]{1,0:T(4,128)S(1)} copy-done((f32[3,4096]{1,0:T(4,128)S(1)}, f32[3,4096]{1,0:T(4,128)}, u32[]{:S(2)}) %copy-start.4) | copy-done | bytes 49176
  2.7 0.7 %copy-done.9 = s32[32]{0:T(128)S(1)} copy-done((s32[32]{0:T(128)S(1)}, s32[32]{0:T(128)}, u32[]{:S(2)}) %copy-start.9) | copy-done | bytes 152
  3.4 0.9 %copy-done.11 = f32[160,8]{1,0:T(8,128)S(1)} copy-done((f32[160,8]{1,0:T(8,128)S(1)}, f32[160,8]{1,0:T(8,128)}, u32[]{:S(2)}) %copy-start.11) | copy-done | bytes 5144
  4.3 2.6 %upward.1 = (f32[24,4096]{1,0:T(8,128)S(1)}, f32[24,1024]{1,0:T(8,128)S(1)}, f32[24,1024]{1,0:T(8,128)S(1)}, f32[640,128]{1,0:T(8,128)S(1)}) custom-call(s32[1]{0:T(128)} %bitcast.first_ref, s32[32]{0:T(128)S(1)} %copy-done.9, f32[3,4096]{1,0:T(4,128)S(1)} %copy-done.4, f32[16,4096]{1,0:T(8,128)S(1)} %copy-done.1, f32[152,152]{1,0:T(8,128)S(1)} %copy-done.2, ...), custom_call_target="tpu_custom_call" | custom-call | flops 500000000 | bytes 1500000 | tf_op jit(solution)/shard_map/upward/pallas_call | solution.py:334
  6.9 3.7 %collective-permute-start = (f32[24,1024]{1,0:T(8,128)S(1)}, f32[24,1024]{1,0:T(8,128)S(1)}, u32[]{:S(2)}, u32[]{:S(2)}) collective-permute-start(f32[24,1024]{1,0:T(8,128)S(1)} %get-tuple-element.10), channel_id=1, source_target_pairs={{0,1},{1,2},{2,3},{3,4},{4,5},{5,6},{6,7},{7,8},{8,9},{9,10},{10,1... | collective-permute-start | bytes 294920 | tf_op jit(solution)/shard_map/ppermute | solution.py:511
  10.6 1.9 %collective-permute-start.1 = (f32[24,1024]{1,0:T(8,128)S(1)}, f32[24,1024]{1,0:T(8,128)S(1)}, u32[]{:S(2)}, u32[]{:S(2)}) collective-permute-start(f32[24,1024]{1,0:T(8,128)S(1)} %get-tuple-element.11), channel_id=1, source_target_pairs={{1,0},{2,1},{3,2},{4,3},{5,4},{6,5},{7,6},{8,7},{9,8},{10,9},{11,1... | collective-permute-start | bytes 294920 | tf_op jit(solution)/shard_map/ppermute | solution.py:512
  12.5 1.3 %collective-permute-start.6 = (f32[640,128]{1,0:T(8,128)S(1)}, f32[640,128]{1,0:T(8,128)S(1)}, u32[]{:S(2)}, u32[]{:S(2)}) collective-permute-start(f32[640,128]{1,0:T(8,128)S(1)} %get-tuple-element.12.refs_5_), channel_id=1, source_target_pairs={{0,16},{1,17},{2,18},{3,19},{4,20},{5,21},{6,22},{7,23},{8,24},{9,... | collective-permute-start | bytes 983048 | tf_op jit(solution)/shard_map/ppermute | solution.py:22
  13.8 1.3 %collective-permute-start.5 = (f32[640,128]{1,0:T(8,128)S(1)}, f32[640,128]{1,0:T(8,128)S(1)}, u32[]{:S(2)}, u32[]{:S(2)}) collective-permute-start(f32[640,128]{1,0:T(8,128)S(1)} %get-tuple-element.12.refs_5_), channel_id=1, source_target_pairs={{0,8},{1,9},{2,10},{3,11},{4,12},{5,13},{6,14},{7,15},{8,0},{9,1},... | collective-permute-start | bytes 983048 | tf_op jit(solution)/shard_map/ppermute | solution.py:22
  15.1 0.2 collective-permute-start.4
  15.3 0.0 copy-done.13
  15.3 0.0 collective-permute-done.low_ref
  15.3 0.3 collective-permute-start.3
  15.6 7.1 %collective-permute-done.1.high_ref = f32[24,1024]{1,0:T(8,128)S(1)} collective-permute-done((f32[24,1024]{1,0:T(8,128)S(1)}, f32[24,1024]{1,0:T(8,128)S(1)}, u32[]{:S(2)}, u32[]{:S(2)}) %collective-permute-start.1) | collective-permute-done | bytes 98336 | tf_op jit(solution)/shard_map/ppermute | solution.py:512
  22.8 0.0 collective-permute-start.2
  22.8 0.0 copy-done.10
  22.8 0.0 copy-done.6
  22.8 0.0 copy-start
  22.8 0.0 copy-start.3
  22.8 0.0 copy-start.5
  22.8 0.0 copy-start.7
  22.8 0.0 copy-start.8
  22.8 0.0 copy-start.12
  22.9 19.3 %near.1.near_ref = f32[16,4096]{1,0:T(8,128)S(1)} custom-call(s32[1]{0:T(128)} %bitcast.first_ref, s32[32]{0:T(128)S(1)} %copy-done.10, f32[24,4096]{1,0:T(8,128)S(1)} %get-tuple-element.9.own_ref, f32[24,1024]{1,0:T(8,128)S(1)} %collective-permute-done.low_ref, f32[24,1024]{1,0:T(8,128)S(1)} %collective-permute-done.1.high_ref, s32[32,27]{1,0:T(8,128)S(1)} %copy-done.6), custom_call_target="tpu_custom_call" | custom-call | flops 4000000000 | bytes 2000000 | tf_op jit(solution)/shard_map/near/pallas_call | solution.py:203
  42.1 0.0 collective-permute-done.6.refs_4_
  42.1 0.0 collective-permute-done.5.refs_3_
  42.1 0.0 collective-permute-done.4.refs_2_
  42.1 0.0 collective-permute-done.3.refs_1_
  42.2 0.0 collective-permute-done.2.refs_0_
  42.2 0.0 copy-done
  42.2 10.1 %far.1 = f32[16,4096]{1,0:T(8,128)} custom-call(s32[32]{0:T(128)S(1)} %copy-done.10, s32[5,16]{1,0:T(8,128)S(1)} %bitcast.4, f32[3,4096]{1,0:T(4,128)S(1)} %copy-done.5, f32[16,4096]{1,0:T(8,128)S(1)} %near.1.near_ref, s32[32,32]{1,0:T(8,128)S(1)} %copy-done.7, s32[32,32]{1,0:T(8,128)S(1)} %copy-done.8, f32[152,2432]{1,0:T(8,128)S(1)} %copy-done, ...), custom_call_target="tpu_custom_call" | custom-call | flops 4000000000 | bytes 4000000 | tf_op jit(solution)/shard_map/far/pallas_call | solution.py:483
  (14 shorter events, 0.0 us)
Async XLA Ops:
  0.0 22.8 %copy-start.10 = (s32[32]{0:T(128)S(1)}, s32[32]{0:T(128)}, u32[]{:S(2)}) copy-start(s32[32]{0:T(128)} %counts_ref.5) | copy-start | bytes 388
  0.0 15.3 %copy-start.13 = (s32[1,5,16]{2,0,1:T(1,128)S(1)}, s32[1,5,16]{2,0,1:T(1,128)}, u32[]{:S(2)}) copy-start(s32[1,5,16]{2,0,1:T(1,128)} %param.18) | copy-start | bytes 964
  0.0 1.0 %copy-start.1 = (f32[16,4096]{1,0:T(8,128)S(1)}, f32[16,4096]{1,0:T(8,128)}, u32[]{:S(2)}) copy-start(f32[16,4096]{1,0:T(8,128)} %charges_ref.1) | copy-start | bytes 786436
  1.0 0.9 %copy-start.2 = (f32[152,152]{1,0:T(8,128)S(1)}, f32[152,152]{1,0:T(8,128)}, u32[]{:S(2)}) copy-start(f32[152,152]{1,0:T(8,128)} %uc2e_ref.1) | copy-start | bytes 277252
  1.9 0.8 %copy-start.4 = (f32[3,4096]{1,0:T(4,128)S(1)}, f32[3,4096]{1,0:T(4,128)}, u32[]{:S(2)}) copy-start(f32[3,4096]{1,0:T(4,128)} %offsets_ref.3) | copy-start | bytes 147460
  2.7 0.7 %copy-start.9 = (s32[32]{0:T(128)S(1)}, s32[32]{0:T(128)}, u32[]{:S(2)}) copy-start(s32[32]{0:T(128)} %counts_ref.5) | copy-start | bytes 388
  3.4 0.9 %copy-start.11 = (f32[160,8]{1,0:T(8,128)S(1)}, f32[160,8]{1,0:T(8,128)}, u32[]{:S(2)}) copy-start(f32[160,8]{1,0:T(8,128)} %constant.8.clone.surface_ref) | copy-start | bytes 15364
  4.3 18.5 %copy-start.6 = (s32[32,27]{1,0:T(8,128)S(1)}, s32[32,27]{1,0:T(8,128)}, u32[]{:S(2)}) copy-start(s32[32,27]{1,0:T(8,128)} %ulist_ref.1) | copy-start | bytes 10372
  6.9 8.4 %collective-permute-start = (f32[24,1024]{1,0:T(8,128)S(1)}, f32[24,1024]{1,0:T(8,128)S(1)}, u32[]{:S(2)}, u32[]{:S(2)}) collective-permute-start(f32[24,1024]{1,0:T(8,128)S(1)} %get-tuple-element.10), channel_id=1, source_target_pairs={{0,1},{1,2},{2,3},{3,4},{4,5},{5,6},{6,7},{7,8},{8,9},{9,10},{10,1... | collective-permute-start | bytes 294920 | tf_op jit(solution)/shard_map/ppermute | solution.py:511
  10.6 12.2 %collective-permute-start.1 = (f32[24,1024]{1,0:T(8,128)S(1)}, f32[24,1024]{1,0:T(8,128)S(1)}, u32[]{:S(2)}, u32[]{:S(2)}) collective-permute-start(f32[24,1024]{1,0:T(8,128)S(1)} %get-tuple-element.11), channel_id=1, source_target_pairs={{1,0},{2,1},{3,2},{4,3},{5,4},{6,5},{7,6},{8,7},{9,8},{10,9},{11,1... | collective-permute-start | bytes 294920 | tf_op jit(solution)/shard_map/ppermute | solution.py:512
  12.5 29.6 %collective-permute-start.6 = (f32[640,128]{1,0:T(8,128)S(1)}, f32[640,128]{1,0:T(8,128)S(1)}, u32[]{:S(2)}, u32[]{:S(2)}) collective-permute-start(f32[640,128]{1,0:T(8,128)S(1)} %get-tuple-element.12.refs_5_), channel_id=1, source_target_pairs={{0,16},{1,17},{2,18},{3,19},{4,20},{5,21},{6,22},{7,23},{8,24},{9,... | collective-permute-start | bytes 983048 | tf_op jit(solution)/shard_map/ppermute | solution.py:22
  13.8 28.3 %collective-permute-start.5 = (f32[640,128]{1,0:T(8,128)S(1)}, f32[640,128]{1,0:T(8,128)S(1)}, u32[]{:S(2)}, u32[]{:S(2)}) collective-permute-start(f32[640,128]{1,0:T(8,128)S(1)} %get-tuple-element.12.refs_5_), channel_id=1, source_target_pairs={{0,8},{1,9},{2,10},{3,11},{4,12},{5,13},{6,14},{7,15},{8,0},{9,1},... | collective-permute-start | bytes 983048 | tf_op jit(solution)/shard_map/ppermute | solution.py:22
  15.1 27.1 %collective-permute-start.4 = (f32[640,128]{1,0:T(8,128)S(1)}, f32[640,128]{1,0:T(8,128)S(1)}, u32[]{:S(2)}, u32[]{:S(2)}) collective-permute-start(f32[640,128]{1,0:T(8,128)S(1)} %get-tuple-element.12.refs_5_), channel_id=1, source_target_pairs={{0,4},{1,5},{2,6},{3,7},{4,0},{5,1},{6,2},{7,3},{8,12},{9,13},{10,... | collective-permute-start | bytes 983048 | tf_op jit(solution)/shard_map/ppermute | solution.py:22
  15.3 26.8 %collective-permute-start.3 = (f32[640,128]{1,0:T(8,128)S(1)}, f32[640,128]{1,0:T(8,128)S(1)}, u32[]{:S(2)}, u32[]{:S(2)}) collective-permute-start(f32[640,128]{1,0:T(8,128)S(1)} %get-tuple-element.12.refs_5_), channel_id=1, source_target_pairs={{0,2},{1,3},{2,0},{3,1},{4,6},{5,7},{6,4},{7,5},{8,10},{9,11},{10,... | collective-permute-start | bytes 983048 | tf_op jit(solution)/shard_map/ppermute | solution.py:22
  22.8 19.4 %collective-permute-start.2 = (f32[640,128]{1,0:T(8,128)S(1)}, f32[640,128]{1,0:T(8,128)S(1)}, u32[]{:S(2)}, u32[]{:S(2)}) collective-permute-start(f32[640,128]{1,0:T(8,128)S(1)} %get-tuple-element.12.refs_5_), channel_id=1, source_target_pairs={{0,1},{1,0},{2,3},{3,2},{4,5},{5,4},{6,7},{7,6},{8,9},{9,8},{10,11... | collective-permute-start | bytes 983048 | tf_op jit(solution)/shard_map/ppermute | solution.py:22
  22.8 19.4 %copy-start = (f32[152,2432]{1,0:T(8,128)S(1)}, f32[152,2432]{1,0:T(8,128)}, u32[]{:S(2)}) copy-start(f32[152,2432]{1,0:T(8,128)} %m2l_ref.1) | copy-start | bytes 4435972
  22.8 19.4 %copy-start.3 = (f32[152,152]{1,0:T(8,128)S(1)}, f32[152,152]{1,0:T(8,128)}, u32[]{:S(2)}) copy-start(f32[152,152]{1,0:T(8,128)} %dc2e_ref.1) | copy-start | bytes 277252
  22.8 19.4 %copy-start.5 = (f32[3,4096]{1,0:T(4,128)S(1)}, f32[3,4096]{1,0:T(4,128)}, u32[]{:S(2)}) copy-start(f32[3,4096]{1,0:T(4,128)} %offsets_ref.3) | copy-start | bytes 147460
  22.8 19.4 %copy-start.7 = (s32[32,32]{1,0:T(8,128)S(1)}, s32[32,32]{1,0:T(8,128)}, u32[]{:S(2)}) copy-start(s32[32,32]{1,0:T(8,128)} %vsrc_ref.1) | copy-start | bytes 12292
  22.8 19.4 %copy-start.8 = (s32[32,32]{1,0:T(8,128)S(1)}, s32[32,32]{1,0:T(8,128)}, u32[]{:S(2)}) copy-start(s32[32,32]{1,0:T(8,128)} %vtype_ref.1) | copy-start | bytes 12292
  22.8 19.4 %copy-start.12 = (f32[160,8]{1,0:T(8,128)S(1)}, f32[160,8]{1,0:T(8,128)}, u32[]{:S(2)}) copy-start(f32[160,8]{1,0:T(8,128)} %constant.8.clone.surface_ref) | copy-start | bytes 15364

commit v3 on v2

--- a/solution.py
+++ b/solution.py
@@ -10,6 +10,9 @@
 
 GHOST = 8
 PTS = 128
+UNIT = 8
+UNIT_LOG = 3
+SIDE = 3
 
 
 soften = 0.01
@@ -30,8 +33,17 @@
     return coords[:, on_face].astype(np.float32)
 
 
-def near_kernel(first_ref, counts_ref, own_ref, low_ref, high_ref, ulist_ref, out_ref,
-                lanes_ref, chg_ref, src_ref, mult_ref, res_ref, start_ref, leaf_ref, from_ref, to_ref):
+def corner_of(leaf, axis):
+    summed = jnp.int32(0)
+    for digit in range(10):
+        summed = summed + (((leaf >> (3 * digit + axis)) & 1) << digit)
+    return summed.astype(jnp.float32)
+
+
+def near_kernel(first_ref, counts_ref, offsets_ref, charges_ref, pair_ref, odd_ref, ulist_ref, out_ref,
+                ghost_ref,
+                lanes_ref, chg_ref, src_ref, tgt_ref, square_ref, hi_ref, lo_ref, acc_ref,
+                mult_ref, res_ref, start_ref, leaf_ref, from_ref, to_ref, open_ref, shut_ref):
     f32, bf16, i32 = jnp.float32, jnp.bfloat16, jnp.int32
     local = out_ref.shape[1] // PTS
     every = local + 2 * GHOST
@@ -51,45 +63,42 @@
     shift_by = jnp.where(sub == 0, centre[0], jnp.where(sub == 1, centre[1], jnp.where(sub == 2, centre[2], 0.0)))
 
     def units(n):
-        return ((n + 15) // 16) * 16
-
-    def ghost_count(ref, e):
-        return jnp.max(ref[3:4, e * PTS:(e + 1) * PTS]).astype(i32)
+        return ((n + UNIT - 1) >> UNIT_LOG) << UNIT_LOG
+
+    deep = 8 + probes
+    even = lax.rem(lax.div(first, local), 2) == 0
+    skip = pair_ref.shape[0] - GHOST * deep
+    odd, pair = odd_ref[...], pair_ref[skip:]
+    ghost_ref[0] = jnp.where(even, odd, pair)
+    ghost_ref[1] = jnp.where(even, pair, odd)
+
+    def ghost_count(side, e):
+        return jnp.max(ghost_ref[side, e * deep + 3:e * deep + 4, :]).astype(i32)
 
     starts = [None] * (every + 1)
     starts[GHOST] = jnp.int32(base)
     for e in range(GHOST - 1, -1, -1):
-        starts[e] = starts[e + 1] - units(ghost_count(low_ref, e))
+        starts[e] = starts[e + 1] - units(ghost_count(0, e))
     for e in range(GHOST, GHOST + local):
         starts[e + 1] = starts[e] + units(counts_ref[e - GHOST])
     for e in range(GHOST + local, every):
-        starts[e + 1] = starts[e] + units(ghost_count(high_ref, e - GHOST - local))
+        starts[e + 1] = starts[e] + units(ghost_count(1, e - GHOST - local))
     for e in range(every + 1):
         start_ref[e] = starts[e]
 
-    for i in range(8):
-        leaf_ref[jnp.maximum((starts[0] >> 4) - 8 + i, 0)] = 0
+    per = PTS // UNIT
+    for i in range(per):
+        leaf_ref[jnp.maximum((starts[0] >> UNIT_LOG) - per + i, 0)] = 0
     for e in range(every):
-        for i in range(8 if e < every - 1 else 48):
-            leaf_ref[(starts[e] >> 4) + i] = e
-
+        for i in range(per if e < every - 1 else 6 * per):
+            leaf_ref[(starts[e] >> UNIT_LOG) + i] = e
+
+    for e in range(GHOST + local - 1, GHOST - 1, -1):
+        from_ref[(starts[e + 1] - base - 1) >> 8] = e
+        from_ref[(starts[e] - base) >> 8] = e
     for e in range(GHOST, GHOST + local):
-        head = starts[e] - base
-        tail = starts[e + 1] - base - 1
-        @pl.when(tail >= head)
-        def _():
-            h, t = head >> 8, tail >> 8
-
-            @pl.when((head & 255) == 0)
-            def _():
-                from_ref[h] = e
-
-            @pl.when(t > h)
-            def _():
-                from_ref[t] = e
-
-            to_ref[h] = e
-            to_ref[t] = e
+        to_ref[(starts[e] - base) >> 8] = e
+        to_ref[(starts[e + 1] - base - 1) >> 8] = e
 
     ids = ulist_ref[...] - (first - GHOST)
     which = lax.broadcasted_iota(i32, (local, every), 1)
@@ -101,12 +110,17 @@
     lanes_ref[...] = jnp.zeros_like(lanes_ref)
     for e in range(every):
         if e < GHOST:
-            block = low_ref[:, e * PTS:(e + 1) * PTS]
+            block = ghost_ref[0, e * deep:(e + 1) * deep, :]
         elif e < GHOST + local:
-            block = own_ref[:, (e - GHOST) * PTS:(e - GHOST + 1) * PTS]
+            h = e - GHOST
+            at = slice(h * PTS, (h + 1) * PTS)
+            corner = [corner_of(first + h, axis) for axis in range(3)]
+            move = jnp.where(sub == 0, corner[0], jnp.where(sub == 1, corner[1], corner[2]))
+            xyz = jnp.concatenate([offsets_ref[:, at], jnp.zeros((5, PTS), f32)], 0)
+            block = jnp.concatenate([xyz + move, jnp.where(lane < counts_ref[h], charges_ref[:, at], 0.0)], 0)
         else:
             at = e - GHOST - local
-            block = high_ref[:, at * PTS:(at + 1) * PTS]
+            block = ghost_ref[1, at * deep:(at + 1) * deep, :]
         block = jnp.concatenate([block[:8] - shift_by, block[8:]], 0)
         shift = starts[e] & (PTS - 1)
         here = pl.multiple_of((starts[e] >> 7) << 7, PTS)
@@ -117,69 +131,123 @@
         lanes_ref[:, pl.ds(after, PTS)] = jnp.where(keep, 0.0, rolled)
         if GHOST <= e < GHOST + local:
             col = jnp.broadcast_to(tally[:, e - GHOST:e - GHOST + 1], (every, PTS))
-            here = pl.multiple_of(here - base, PTS)
-            after = pl.multiple_of(after - base, PTS)
-            mult_ref[:, pl.ds(here, PTS)] = jnp.where(keep, col, mult_ref[:, pl.ds(here, PTS)])
-            mult_ref[:, pl.ds(after, PTS)] = col
+            here = pl.multiple_of(((starts[e] - base) >> 7) * every, 8)
+            after = pl.multiple_of((((starts[e] - base) >> 7) + 1) * every, 8)
+            mult_ref[pl.ds(here, every), :] = jnp.where(keep, col, mult_ref[pl.ds(here, every), :])
+            mult_ref[pl.ds(after, every), :] = col
 
     group = 4 * PTS
     head = starts[0] >> 7
     tail = (starts[every] + 127) >> 7
+    row_id = lax.broadcasted_iota(i32, (8, group), 0)
 
     def spread(i, _):
         at = pl.multiple_of((head + 4 * i) * PTS, PTS)
-        pos = lanes_ref[0:8, pl.ds(at, group)]
-        norm = pos[0:1] * pos[0:1] + pos[1:2] * pos[1:2] + pos[2:3] * pos[2:3]
-        feats = jnp.concatenate([-2.0 * pos[0:3], norm + soften, pos[4:8]], 0)
-        lanes_ref[3:4, pl.ds(at, group)] = norm
-        turned = feats.T
-        for k in range(4):
-            src_ref[k, pl.ds(at, group), :] = jnp.broadcast_to(turned[:, k:k + 1], (group, PTS))
+        pos = jnp.where(row_id < 3, lanes_ref[0:8, pl.ds(at, group)], 0.0)
+        pos_hi = pos.astype(bf16).astype(f32)
+        pos_lo = (pos - pos_hi).astype(bf16).astype(f32)
+        used = pos_hi + pos_lo
+        norm = jnp.sum(used * used, 0, keepdims=True)
+
+        def rows(blocks, total, three, four):
+            parts = []
+            for block in blocks[:3]:
+                piece = total.astype(bf16).astype(f32)
+                total = total - piece
+                extra = jnp.where(row_id == three, piece, jnp.where(row_id == four, 1.0, 0.0))
+                parts.append(jnp.where(row_id < 3, block, extra))
+            return jnp.concatenate(parts + [blocks[3]], 0)
+
+        src = rows((-2.0 * pos_hi, -2.0 * pos_hi, -2.0 * pos_lo, -2.0 * pos_lo), norm + soften, 3, 4)
+        tgt = rows((pos_hi, pos_lo, pos_hi, pos_lo), norm, 4, 3)
+        src_ref[pl.ds(at, group), :] = src.T.astype(bf16)
+        tgt_ref[:, pl.ds(at, group)] = tgt.astype(bf16)
         chg = lanes_ref[8:8 + probes, pl.ds(at, group)]
         hi = chg.astype(bf16)
         chg_ref[0:probes, pl.ds(at, group)] = hi
         chg_ref[probes:2 * probes, pl.ds(at, group)] = (chg - hi.astype(f32)).astype(bf16)
         return 0
 
-    lax.fori_loop(0, (tail - head + 3) // 4 + 1, spread, 0)
-
-    def target_block(t, _):
+    lax.fori_loop(0, (tail - head + 5) // 4, spread, 0)
+
+    acc_ref[...] = jnp.zeros_like(acc_ref)
+    blocks = (starts[GHOST + local] - base + 255) >> 8
+    steps = jnp.int32(0)
+    for t in range(local * PTS // 256 + 1):
+        real = t < blocks
+        opens = (start_ref[jnp.where(real, from_ref[t], GHOST) - GHOST] >> 7) << 7
+        shuts = jnp.where(real, start_ref[jnp.where(real, to_ref[t], GHOST) + GHOST + 1], 0)
+        open_ref[t] = opens
+        shut_ref[t] = shuts
+        steps = steps + jnp.where(real, (shuts - opens + 255) >> 8, 0)
+
+    def advance(step):
+        t, row = step
+        done = row + 256 >= shut_ref[t]
+        after = jnp.minimum(jnp.where(done, t + 1, t), blocks)
+        return after, jnp.where(done, open_ref[after], row + 256)
+
+    def square(step, slot):
+        t, row = step
+        tgt = tgt_ref[:, pl.ds(pl.multiple_of(base + t * 256, 256), 256)]
+        square_ref[slot] = jnp.dot(src_ref[pl.ds(pl.multiple_of(row, PTS), 256), :], tgt, preferred_element_type=f32)
+
+    def weigh(step, slot):
+        t, row = step
+        left = t * (2 * every)
+        for r in range(16):
+            k = lax.rsqrt(square_ref[slot, 16 * r:16 * r + 16, :])
+            parts = []
+            for half in range(2):
+                leaf = left + leaf_ref[(row >> UNIT_LOG) + 2 * r + half]
+                weight = jnp.concatenate([mult_ref[pl.ds(leaf, 1), :], mult_ref[pl.ds(leaf + every, 1), :]], 1)
+                parts.append(k[8 * half:8 * half + 8] * weight)
+            k = jnp.concatenate(parts, 0)
+            at = slice(16 * r, 16 * r + 16)
+            hi = k.astype(bf16)
+            hi_ref[slot, at, :] = hi
+            lo_ref[slot, at, :] = (k - hi.astype(f32)).astype(bf16)
+
+    def gather(step, slot):
+        t, row = step
         where = pl.multiple_of(t * 256, 256)
-        tgt = lanes_ref[0:8, pl.ds(pl.multiple_of(base + where, 256), 256)]
-        lo_row = (start_ref[from_ref[t] - GHOST] >> 7) << 7
-        hi_row = start_ref[to_ref[t] + GHOST + 1]
-
-        def chunk(row, size, carry):
-            first_sum, second_sum = carry
-            row = pl.multiple_of(row, PTS)
-            his, los = [], []
-            for r in range(size // 16):
-                at = pl.multiple_of(row + 16 * r, 16)
-                leaf = leaf_ref[(row >> 4) + r]
-                weight = mult_ref[pl.ds(leaf, 1), pl.ds(where, 256)]
-                hi_pair, lo_pair = [], []
-                for half in range(2):
-                    x = tgt[:, half * 128:(half + 1) * 128]
-                    s = (src_ref[3, pl.ds(at, 16), :] + x[3:4]) + src_ref[0, pl.ds(at, 16), :] * x[0:1]
-                    s = s + (src_ref[1, pl.ds(at, 16), :] * x[1:2] + src_ref[2, pl.ds(at, 16), :] * x[2:3])
-                    k = lax.rsqrt(s) * weight[:, half * 128:(half + 1) * 128]
-                    hi = k.astype(bf16)
-                    hi_pair.append(hi)
-                    lo_pair.append((k - hi.astype(f32)).astype(bf16))
-                his.append(jnp.concatenate(hi_pair, 1))
-                los.append(jnp.concatenate(lo_pair, 1))
-            chg = chg_ref[:, pl.ds(row, size)]
-            first_sum = first_sum + jnp.dot(chg, jnp.concatenate(his, 0), preferred_element_type=f32)
-            second_sum = second_sum + jnp.dot(chg[:probes], jnp.concatenate(los, 0), preferred_element_type=f32)
-            return first_sum, second_sum
-
-        sums = (jnp.zeros((2 * probes, 256), f32), jnp.zeros((probes, 256), f32))
-        size = 512
-        sums = lax.fori_loop(0, (hi_row - lo_row + size - 1) // size, lambda i, c: chunk(lo_row + size * i, size, c), sums)
-        res_ref[:, pl.ds(where, 256)] = sums[0][:probes] + sums[0][probes:] + sums[1]
-        return 0
-
-    lax.fori_loop(0, (starts[GHOST + local] - base + 255) // 256, target_block, 0)
+        chg = chg_ref[:, pl.ds(pl.multiple_of(row, PTS), 256)]
+        return (where, jnp.dot(chg, hi_ref[slot], preferred_element_type=f32),
+                jnp.dot(chg[:probes], lo_ref[slot], preferred_element_type=f32))
+
+    def add(where, first_sum, second_sum):
+        acc_ref[0:2 * probes, pl.ds(where, 256)] += first_sum
+        acc_ref[2 * probes:, pl.ds(where, 256)] += second_sum
+
+    step = (jnp.int32(0), open_ref[0])
+    order = [step]
+    for _ in range(2 * SIDE - 1):
+        step = advance(step)
+        order.append(step)
+    for c in range(SIDE):
+        square(order[c], c)
+    for c in range(SIDE):
+        weigh(order[c], c)
+    for c in range(SIDE):
+        square(order[SIDE + c], c)
+
+    def several(_, order):
+        later = []
+        step = order[-1]
+        for c in range(SIDE):
+            step = advance(step)
+            later.append(step)
+        sums = [gather(order[c], c) for c in range(SIDE)]
+        for c in range(SIDE):
+            weigh(order[SIDE + c], c)
+        for c in range(SIDE):
+            square(later[c], c)
+        for each in sums:
+            add(*each)
+        return (*order[SIDE:], *later)
+
+    lax.fori_loop(0, (steps + SIDE - 1) // SIDE, several, tuple(order))
+    res_ref[...] = acc_ref[0:probes] + acc_ref[probes:2 * probes] + acc_ref[2 * probes:]
 
     for g in range(local):
         at = starts[g + GHOST] - base
@@ -192,9 +260,9 @@
         out_ref[:, g * PTS:(g + 1) * PTS] = jnp.where(lane < counts_ref[g], value * inv_four_pi, 0.0)
 
 
-def near_call(first, counts, own, low, high, u_list):
+def near_call(first, counts, offsets, charges, pair, odd, u_list):
     local = counts.shape[0]
-    probes = own.shape[0] - 8
+    probes = charges.shape[0]
     every = local + 2 * GHOST
     width = every * PTS + 8 * PTS + 512
     targets = local * PTS + 512
@@ -203,23 +271,31 @@
     return pl.pallas_call(
         near_kernel,
         out_shape=jax.ShapeDtypeStruct((probes, local * PTS), jnp.float32),
-        in_specs=[smem, smem, vmem, vmem, vmem, vmem],
+        in_specs=[smem, smem, vmem, vmem, vmem, vmem, vmem],
         out_specs=vmem,
         scratch_shapes=[
+            pltpu.VMEM((2, GHOST * (8 + probes), PTS), jnp.float32),
             pltpu.VMEM((8 + probes, width), jnp.float32),
             pltpu.VMEM((2 * probes, width), jnp.bfloat16),
-            pltpu.VMEM((4, width, PTS), jnp.float32),
-            pltpu.VMEM((every, targets), jnp.float32),
+            pltpu.VMEM((width, 32), jnp.bfloat16),
+            pltpu.VMEM((32, width), jnp.bfloat16),
+            pltpu.VMEM((SIDE, 256, 256), jnp.float32),
+            pltpu.VMEM((SIDE, 256, 256), jnp.bfloat16),
+            pltpu.VMEM((SIDE, 256, 256), jnp.bfloat16),
+            pltpu.VMEM((3 * probes, targets), jnp.float32),
+            pltpu.VMEM((targets // PTS * every, PTS), jnp.float32),
             pltpu.VMEM((probes, targets), jnp.float32),
             pltpu.SMEM((every + 1,), jnp.int32),
-            pltpu.SMEM((width // 16 + 64,), jnp.int32),
+            pltpu.SMEM((width // UNIT + 64,), jnp.int32),
+            pltpu.SMEM((local * PTS // 256 + 1,), jnp.int32),
+            pltpu.SMEM((local * PTS // 256 + 1,), jnp.int32),
             pltpu.SMEM((local * PTS // 256 + 1,), jnp.int32),
             pltpu.SMEM((local * PTS // 256 + 1,), jnp.int32),
         ],
-        compiler_params=pltpu.CompilerParams(vmem_limit_bytes=48 << 20),
+        compiler_params=pltpu.CompilerParams(vmem_limit_bytes=24 << 20),
         cost_estimate=pl.CostEstimate(flops=4_000_000_000, bytes_accessed=2_000_000, transcendentals=4_000_000),
         name="near",
-    )(first, counts, own, low, high, u_list)
+    )(first, counts, offsets, charges, pair, odd, u_list)
 
 
 def split(value):
@@ -239,13 +315,6 @@
     left_hi, left_lo = split(left)
     right_hi, right_lo = split(right)
     return dot_t(left_hi, right_hi) + (dot_t(left_hi, right_lo) + dot_t(left_lo, right_hi))
-
-
-def corner_of(leaf, axis):
-    summed = jnp.int32(0)
-    for digit in range(10):
-        summed = summed + (((leaf >> (3 * digit + axis)) & 1) << digit)
-    return summed.astype(jnp.float32)
 
 
 def surface_tile(local, surface):
@@ -274,32 +343,36 @@
     return value
 
 
-def up_kernel(first_ref, counts_ref, offsets_ref, charges_ref, uc2e_ref, surface_ref,
-              own_ref, low_ref, high_ref, up_ref, check_ref):
+def up_kernel(first_ref, counts_hbm, offsets_hbm, charges_hbm, uc2e_hbm, surface_hbm,
+              odd_ref, pair_ref, up_ref, tile_hi_hbm, tile_lo_hbm,
+              tile_hi_ref, tile_lo_ref, counts_ref, offsets_ref, charges_ref, uc2e_ref, surface_ref, check_ref, sems):
     f32, i32 = jnp.float32, jnp.int32
+    copies = []
+    for n, (source, target) in enumerate(((counts_hbm, counts_ref), (offsets_hbm, offsets_ref),
+                                          (surface_hbm, surface_ref), (charges_hbm, charges_ref),
+                                          (uc2e_hbm, uc2e_ref))):
+        copies.append(pltpu.make_async_copy(source, target, sems.at[n]))
+        copies[n].start()
     probes, points = charges_ref.shape
     local = points // PTS
     lane = lax.broadcasted_iota(i32, (1, PTS), 1)
     sub = lax.broadcasted_iota(i32, (8, PTS), 0)
     first = first_ref[0]
+    zero = jnp.zeros((probes, PTS), jnp.bfloat16)
+    for copy in copies[:4]:
+        copy.wait()
     surface = surface_ref[...]
-    zero = jnp.zeros((probes, PTS), jnp.bfloat16)
-
+
+    leaving = []
     for g in range(0, local, 2):
         parts = []
         for h in (g, g + 1):
             at = slice(h * PTS, (h + 1) * PTS)
-            corner = [corner_of(first + h, axis) for axis in range(3)]
-            held = counts_ref[h]
-            xyz = jnp.concatenate([offsets_ref[:, at], jnp.zeros((5, PTS), f32)], 0)
-            move = jnp.where(sub == 0, corner[0], jnp.where(sub == 1, corner[1], jnp.where(sub == 2, corner[2],
-                   jnp.where(sub == 3, held.astype(f32), 0.0))))
-            own_ref[0:8, at] = xyz + move
-            masked = jnp.where(lane < held, charges_ref[:, at], 0.0)
-            own_ref[8:8 + probes, at] = masked
-            parts.append(split(masked))
-        both = offsets_ref[:, g * PTS:(g + 2) * PTS] - 0.5
-        tile_hi, tile_lo = split(surface_tile(both, surface))
+            parts.append(split(jnp.where(lane < counts_ref[h], charges_ref[:, at], 0.0)))
+        both = slice(g * PTS, (g + 2) * PTS)
+        tile_hi, tile_lo = split(surface_tile(offsets_ref[:, both] - 0.5, surface))
+        tile_hi_ref[:, both] = tile_hi
+        tile_lo_ref[:, both] = tile_lo
         left = jnp.concatenate([parts[0][0], zero], 1), jnp.concatenate([zero, parts[1][0]], 1)
         small = jnp.concatenate([parts[0][1], zero], 1), jnp.concatenate([zero, parts[1][1]], 1)
         large = dot_t(jnp.concatenate(left + small, 0), tile_hi)
@@ -311,18 +384,38 @@
             at = slice(half * PTS, (half + 1) * PTS)
             check_ref[half, pl.ds(g, probes, stride=local), :] = value[:probes, at]
             check_ref[half, pl.ds(g + 1, probes, stride=local), :] = value[probes:, at]
-    low_ref[...] = own_ref[:, points - GHOST * PTS:]
-    high_ref[...] = own_ref[:, :GHOST * PTS]
-
-    equiv = uc2e_ref.shape[0]
+        if (g + 2) % 8 == 0:
+            done = slice((g - 6) * PTS, (g + 2) * PTS)
+            for source, target in ((tile_hi_ref, tile_hi_hbm), (tile_lo_ref, tile_lo_hbm)):
+                leaving.append(pltpu.make_async_copy(source.at[:, done], target.at[:, done], sems.at[5]))
+                leaving[-1].start()
+
+    rows = probes * local
+    even = lax.rem(lax.div(first, local), 2) == 0
+    deep = 8 + probes
+    for e in range(GHOST):
+        leaf = jnp.where(even, e, local - GHOST + e), jnp.where(even, local - GHOST + e, e)
+        for h, ref, skip in ((leaf[0], odd_ref, 0), (leaf[1], pair_ref, rows * 5 // 4)):
+            at = pl.multiple_of(h * PTS, PTS)
+            corner = [corner_of(first + h, axis) for axis in range(3)]
+            held = counts_ref[h]
+            xyz = jnp.concatenate([offsets_ref[:, pl.ds(at, PTS)], jnp.zeros((5, PTS), f32)], 0)
+            move = jnp.where(sub == 0, corner[0], jnp.where(sub == 1, corner[1], jnp.where(sub == 2, corner[2],
+                   jnp.where(sub == 3, held.astype(f32), 0.0))))
+            ref[skip + e * deep:skip + e * deep + 8] = xyz + move
+            ref[skip + e * deep + 8:skip + (e + 1) * deep] = jnp.where(lane < held, charges_ref[:, pl.ds(at, PTS)], 0.0)
+
+    copies[4].wait()
     up = dot_t3(jnp.concatenate([check_ref[0], check_ref[1]], 1), padded(uc2e_ref, 2 * PTS, 2 * PTS))
-    rows = probes * local
-    up_ref[:rows] = up[:, :PTS]
     rest = rows // 4
     tail = up[:rest, PTS:]
     for k in range(1, 4):
         tail = tail + pltpu.roll(up[k * rest:(k + 1) * rest, PTS:], 32 * k, 1)
-    up_ref[rows:] = tail
+    for target in (up_ref, pair_ref):
+        target[:rows] = up[:, :PTS]
+        target[rows:rows + rest] = tail
+    for copy in leaving:
+        copy.wait()
 
 
 def up_call(first, counts, offsets, charges, uc2e):
@@ -330,28 +423,48 @@
     probes, points = charges.shape
     smem = pl.BlockSpec(memory_space=pltpu.SMEM)
     vmem = pl.BlockSpec(memory_space=pltpu.VMEM)
-    f32 = jnp.float32
+    hbm = pl.BlockSpec(memory_space=pltpu.HBM)
+    f32, bf16 = jnp.float32, jnp.bfloat16
+    surface = surface_rows()
+    sent = probes * local * 5 // 4
+    ghost = GHOST * (8 + probes)
     return pl.pallas_call(
         up_kernel,
         out_shape=(
-            jax.ShapeDtypeStruct((8 + probes, points), f32),
-            jax.ShapeDtypeStruct((8 + probes, GHOST * PTS), f32),
-            jax.ShapeDtypeStruct((8 + probes, GHOST * PTS), f32),
-            jax.ShapeDtypeStruct((probes * local * 5 // 4, PTS), f32),
+            jax.ShapeDtypeStruct((ghost, PTS), f32),
+            jax.ShapeDtypeStruct((sent + ghost, PTS), f32),
+            jax.ShapeDtypeStruct((sent, PTS), f32),
+            jax.ShapeDtypeStruct((surface.shape[0], points), bf16),
+            jax.ShapeDtypeStruct((surface.shape[0], points), bf16),
         ),
-        in_specs=[smem, smem, vmem, vmem, vmem, vmem],
-        out_specs=(vmem, vmem, vmem, vmem),
-        scratch_shapes=[pltpu.VMEM((2, probes * local, PTS), f32)],
-        compiler_params=pltpu.CompilerParams(vmem_limit_bytes=32 << 20),
+        in_specs=[smem, hbm, hbm, hbm, hbm, hbm],
+        out_specs=(vmem, vmem, vmem, hbm, hbm),
+        scratch_shapes=[
+            pltpu.VMEM((surface.shape[0], points), bf16),
+            pltpu.VMEM((surface.shape[0], points), bf16),
+            pltpu.SMEM(counts.shape, jnp.int32),
+            pltpu.VMEM(offsets.shape, f32),
+            pltpu.VMEM(charges.shape, f32),
+            pltpu.VMEM(uc2e.shape, f32),
+            pltpu.VMEM(surface.shape, f32),
+            pltpu.VMEM((2, probes * local, PTS), f32),
+            pltpu.SemaphoreType.DMA((6,)),
+        ],
+        compiler_params=pltpu.CompilerParams(vmem_limit_bytes=60 << 20),
         cost_estimate=pl.CostEstimate(flops=500_000_000, bytes_accessed=1_500_000, transcendentals=600_000),
         name="upward",
-    )(first, counts, offsets, charges, uc2e, jnp.asarray(surface_rows()))
-
-
-def far_kernel(counts_ref, wanted_ref, offsets_ref, near_ref, vsrc_ref, vtype_ref, m2l_ref, dc2e_ref, surface_ref,
+    )(first, counts, offsets, charges, uc2e, jnp.asarray(surface))
+
+
+def send_order(count):
+    return [count - 1, 1, *range(count - 2, 1, -1), 0]
+
+
+def far_kernel(counts_ref, wanted_ref, tile_hi_ref, tile_lo_ref, near_ref, vsrc_ref, vtype_ref, m2l_ref, dc2e_ref,
                *refs):
     f32, bf16, i32 = jnp.float32, jnp.bfloat16, jnp.int32
-    pieces = refs[:-9]
+    sent = refs[:-9]
+    pieces = [sent[i] for i in np.argsort(send_order(len(sent)))]
     out_ref, code_ref, tally_ref, table_ref, x_hi_ref, x_lo_ref, w_hi_ref, w_lo_ref, eq_ref = refs[-9:]
     probes, points = out_ref.shape
     local = points // PTS
@@ -414,7 +527,7 @@
             tally_ref[t * local + g:t * local + g + 8, :] = count[8 * t:8 * t + 8]
     tally = tally_ref[...].astype(bf16)
 
-    blocks = pieces[0].shape[0] // local
+    blocks = probes * 5 // 4
     for b, piece in enumerate(pieces):
         for n in range(blocks):
             hi, lo = split(piece[n * local:(n + 1) * local, :])
@@ -451,11 +564,10 @@
     equivs = dot_t3(down, padded(dc2e_ref, 2 * PTS, 2 * PTS))
     eq_ref[0], eq_ref[1] = equivs[:, :PTS], equivs[:, PTS:]
 
-    surface = surface_ref[...]
-    reach = surface.shape[0]
+    reach = tile_hi_ref.shape[0]
     for g in range(0, local, 2):
         at = slice(g * PTS, (g + 2) * PTS)
-        tile_hi, tile_lo = split(surface_tile(offsets_ref[:, at] - 0.5, surface))
+        tile_hi, tile_lo = tile_hi_ref[:, at], tile_lo_ref[:, at]
         parts = []
         for h in (g, g + 1):
             value = jnp.concatenate([eq_ref[half, pl.ds(h, probes, stride=local), :] for half in range(2)], 1)[:, :reach]
@@ -470,7 +582,7 @@
             out_ref[:, to] = jnp.where(lane < counts_ref[h], near_ref[:, to] + part, 0.0)
 
 
-def far_call(counts, wanted, offsets, near, v_src, v_type, m2l, dc2e, pieces):
+def far_call(counts, wanted, tiles, near, v_src, v_type, m2l, dc2e, pieces):
     local = counts.shape[0]
     probes, points = near.shape
     equiv = dc2e.shape[0]
@@ -488,31 +600,30 @@
         scratch_shapes=[
             pltpu.VMEM((2 * local, PTS), f32),
             pltpu.VMEM((kinds * local, len(pieces) * local), f32),
-            pltpu.VMEM((2 * len(pieces) * local, pieces[0].shape[0] // local * PTS), bf16),
+            pltpu.VMEM((2 * len(pieces) * local, probes * 5 // 4 * PTS), bf16),
             pltpu.VMEM((rows, wide), bf16),
             pltpu.VMEM((rows, wide), bf16),
             pltpu.VMEM((2 * PTS, wide), bf16),
             pltpu.VMEM((2 * PTS, wide), bf16),
             pltpu.VMEM((2, rows, PTS), f32),
         ],
-        compiler_params=pltpu.CompilerParams(vmem_limit_bytes=40 << 20),
+        compiler_params=pltpu.CompilerParams(vmem_limit_bytes=32 << 20),
         cost_estimate=pl.CostEstimate(flops=4_000_000_000, bytes_accessed=4_000_000, transcendentals=600_000),
         name="far",
-    )(counts, wanted, offsets, near, v_src, v_type, m2l, dc2e, jnp.asarray(surface_rows()), *pieces)
+    )(counts, wanted, *tiles, near, v_src, v_type, m2l, dc2e, *(pieces[i] for i in send_order(len(pieces))))
 
 
 def shards(offsets, charges, counts, u_list, v_src, v_type, wanted, m2l, uc2e, dc2e):
     local_leaves = counts.shape[0]
     first = (lax.axis_index("cube") * local_leaves).astype(jnp.int32).reshape(1)
-    own, to_next, to_last, up = up_call(first, counts, offsets, charges, uc2e)
+    odd, pair, up, tile_hi, tile_lo = up_call(first, counts, offsets, charges, uc2e)
     count = lax.axis_size("cube")
-    forward = [(i, i + 1) for i in range(count - 1)]
-    backward = [(target, source) for source, target in forward]
-    low = lax.ppermute(to_next, "cube", forward)
-    high = lax.ppermute(to_last, "cube", backward)
-    pieces = [from_partner(up, "cube", bit) for bit in range(count.bit_length() - 1)] + [up]
-    near = near_call(first, counts, own, low, high, u_list)
-    return far_call(counts, wanted[0], offsets, near, v_src, v_type, m2l, dc2e, pieces)
+    odd = lax.ppermute(odd, "cube", [(i, i + 1 if i % 2 else i - 1) for i in range(1, count - 1)])
+    pieces = [from_partner(up, "cube", bit) for bit in range(count.bit_length() - 2, 0, -1)]
+    pair = from_partner(pair, "cube", 0)
+    pieces = [pair] + pieces[::-1] + [up]
+    near = near_call(first, counts, offsets, charges, pair, odd, u_list)
+    return far_call(counts, wanted[0], (tile_hi, tile_lo), near, v_src, v_type, m2l, dc2e, pieces)
 
 
 def solution(mesh):

time: 52.8 us -> 43.5 us (0.82)
  the two profiles are of different devices: /device:TPU:15 before, /device:TPU:11 now
where the time goes in v3:
time: 43.5 us; the launch traced here: 44.3 us
  Pallas kernels  27.1 us (62%)
  starting transfers between devices  14.8 us (34%)
  waiting for transfers between devices  2.15 us (5%)
    pallas_call x1, Pallas kernels, near_call(): pl.pallas_call(near_kernel, out_shape=jax.ShapeDtypeStruct((probes, local...  12.7 us
    ppermute x5, starting transfers between devices, from_partner(): lax.ppermute(array, axis, [(i, i ^ 1 << bit) for i in range(lax.axis_size...  11.7 us
    pallas_call x1, Pallas kernels, far_call(): pl.pallas_call(far_kernel, out_shape=jax.ShapeDtypeStruct((probes, points...  9.62 us
    pallas_call x1, Pallas kernels, up_call(): pl.pallas_call(up_kernel, out_shape=(jax.ShapeDtypeStruct((ghost, PTS), f...  4.75 us
    ppermute x1, starting transfers between devices, shards(): lax.ppermute(odd, 'cube', [(i, i + 1 if i % 2 else i - 1) for i in range(...  3.02 us
    ppermute x1, waiting for transfers between devices, shards(): lax.ppermute(odd, 'cube', [(i, i + 1 if i % 2 else i - 1) for i in range(...  2.13 us
  transfers between devices with their start and end apart: 6, of which 1 were waited for; matrix products, arithmetic and copies ran while one was open for 0% of the time, Pallas kernels for 29%

profile of v3, /device:TPU:11, one launch (start us, length us, event | category | flops | bytes accessed | tf_op | source)
XLA Modules:
  0.0 44.3 jit_solution(3560395666833695984)
XLA Ops:
  0.0 0.0 copy-start.11
  0.0 0.0 copy-start.5
  0.0 4.8 %upward.1 = (f32[192,128]{1,0:T(8,128)}, f32[832,128]{1,0:T(8,128)}, f32[640,128]{1,0:T(8,128)}, bf16[160,4096]{1,0:T(8,128)(2,1)}, bf16[160,4096]{1,0:T(8,128)(2,1)}) custom-call(s32[1]{0:T(128)} %bitcast.first_ref, s32[32]{0:T(128)} %counts_ref.3, f32[3,4096]{1,0:T(4,128)} %offsets_ref.1, f32[16,4096]{1,0:T(8,128)} %charges_ref.1, f32[152,152]{1,0:T(8,128)} %uc2e_hbm.1, ...), custom_call_target="tpu_custom_call" | custom-call | flops 500000000 | bytes 1500000 | tf_op jit(solution)/shard_map/upward/pallas_call | solution.py:431
  4.8 0.7 %collective-permute-start = (f32[832,128]{1,0:T(8,128)}, f32[832,128]{1,0:T(8,128)S(1)}, u32[]{:S(2)}, u32[]{:S(2)}) collective-permute-start(f32[832,128]{1,0:T(8,128)} %get-tuple-element.12), channel_id=1, source_target_pairs={{0,1},{1,0},{2,3},{3,2},{4,5},{5,4},{6,7},{7,6},{8,9},{9,8},{10,11... | collective-permute-start | bytes 1277960 | tf_op jit(solution)/shard_map/ppermute | solution.py:25
  5.5 3.0 %collective-permute-start.1 = (f32[192,128]{1,0:T(8,128)}, f32[192,128]{1,0:T(8,128)S(1)}, u32[]{:S(2)}, u32[]{:S(2)}) collective-permute-start(f32[192,128]{1,0:T(8,128)} %get-tuple-element.13), channel_id=1, source_target_pairs={{1,2},{2,1},{3,4},{4,3},{5,6},{6,5},{7,8},{8,7},{9,10},{10,9},{11,... | collective-permute-start | bytes 294920 | tf_op jit(solution)/shard_map/ppermute | solution.py:621
  8.6 0.3 collective-permute-start.2
  8.9 2.3 %collective-permute-start.3 = (f32[640,128]{1,0:T(8,128)}, f32[640,128]{1,0:T(8,128)S(1)}, u32[]{:S(2)}, u32[]{:S(2)}) collective-permute-start(f32[640,128]{1,0:T(8,128)} %get-tuple-element.14.refs_0_), channel_id=1, source_target_pairs={{0,16},{1,17},{2,18},{3,19},{4,20},{5,21},{6,22},{7,23},{8,24},{9,... | collective-permute-start | bytes 983048 | tf_op jit(solution)/shard_map/ppermute | solution.py:25
  11.2 0.2 collective-permute-start.4
  11.4 0.0 copy-done.11
  11.4 0.0 copy-start.3
  11.4 0.0 copy-start.6
  11.4 0.0 copy-start.7
  11.4 0.0 copy-start.9
  11.4 0.0 copy-start.10
  11.4 2.1 %collective-permute-done.1.odd_ref = f32[192,128]{1,0:T(8,128)S(1)} collective-permute-done((f32[192,128]{1,0:T(8,128)}, f32[192,128]{1,0:T(8,128)S(1)}, u32[]{:S(2)}, u32[]{:S(2)}) %collective-permute-start.1) | collective-permute-done | bytes 98336 | tf_op jit(solution)/shard_map/ppermute | solution.py:621
  13.6 8.2 %collective-permute-start.5 = (f32[640,128]{1,0:T(8,128)}, f32[640,128]{1,0:T(8,128)S(1)}, u32[]{:S(2)}, u32[]{:S(2)}) collective-permute-start(f32[640,128]{1,0:T(8,128)} %get-tuple-element.14.refs_0_), channel_id=1, source_target_pairs={{0,4},{1,5},{2,6},{3,7},{4,0},{5,1},{6,2},{7,3},{8,12},{9,13},{10,... | collective-permute-start | bytes 983048 | tf_op jit(solution)/shard_map/ppermute | solution.py:25
  21.8 0.0 collective-permute-done.pair_ref.refs_5_
  21.8 0.0 copy-done.4
  21.8 0.0 copy-done.2
  21.8 0.0 copy-done.8
  21.8 0.0 copy-done.5
  21.8 12.7 %near.1.near_ref = f32[16,4096]{1,0:T(8,128)S(1)} custom-call(s32[1]{0:T(128)} %bitcast.first_ref, s32[32]{0:T(128)S(1)} %copy-done.8, f32[3,4096]{1,0:T(4,128)S(1)} %copy-done.4, f32[16,4096]{1,0:T(8,128)S(1)} %copy-done.2, f32[832,128]{1,0:T(8,128)S(1)} %collective-permute-done.pair_ref.refs_5_, f32[192,128]{1,0:T(8,128)S(1)} %collective-permute-done.1.odd_ref, ...), custom_call_target="tpu_custom_call" | custom-call | flops 4000000000 | bytes 2000000 | tf_op jit(solution)/shard_map/near/pallas_call | solution.py:271
  34.5 0.0 collective-permute-done.2.refs_1_
  34.6 0.0 collective-permute-done.3.refs_2_
  34.6 0.0 collective-permute-done.4.refs_3_
  34.6 0.0 collective-permute-done.5.refs_4_
  34.6 0.0 copy-done
  34.6 0.0 copy-done.1
  34.6 0.0 copy-done.3
  34.6 0.0 copy-done.6
  34.6 0.0 copy-done.7
  34.7 9.6 %far.1 = f32[16,4096]{1,0:T(8,128)} custom-call(s32[32]{0:T(128)S(1)} %copy-done.8, s32[5,16]{1,0:T(8,128)S(1)} %bitcast.4, bf16[160,4096]{1,0:T(8,128)(2,1)S(1)} %copy-done.9, bf16[160,4096]{1,0:T(8,128)(2,1)S(1)} %copy-done.10, f32[16,4096]{1,0:T(8,128)S(1)} %near.1.near_ref, s32[32,32]{1,0:T(8,128)S(1)} %copy-done.6, s32[32,32]{1,0:T(8,128)S(1)} %copy-done.7, ...), custom_call_target="tpu_custom_call" | custom-call | flops 4000000000 | bytes 4000000 | tf_op jit(solution)/shard_map/far/pallas_call | solution.py:595
  (8 shorter events, 0.0 us)
Async XLA Ops:
  0.0 21.8 %copy-start.4 = (f32[3,4096]{1,0:T(4,128)S(1)}, f32[3,4096]{1,0:T(4,128)}, u32[]{:S(2)}) copy-start(f32[3,4096]{1,0:T(4,128)} %offsets_ref.1) | copy-start | bytes 147460
  0.0 21.8 %copy-start.2 = (f32[16,4096]{1,0:T(8,128)S(1)}, f32[16,4096]{1,0:T(8,128)}, u32[]{:S(2)}) copy-start(f32[16,4096]{1,0:T(8,128)} %charges_ref.1) | copy-start | bytes 786436
  0.0 21.8 %copy-start.8 = (s32[32]{0:T(128)S(1)}, s32[32]{0:T(128)}, u32[]{:S(2)}) copy-start(s32[32]{0:T(128)} %counts_ref.3) | copy-start | bytes 388
  0.0 11.4 %copy-start.11 = (s32[1,5,16]{2,0,1:T(1,128)S(1)}, s32[1,5,16]{2,0,1:T(1,128)}, u32[]{:S(2)}) copy-start(s32[1,5,16]{2,0,1:T(1,128)} %param.17) | copy-start | bytes 964
  0.0 21.8 %copy-start.5 = (s32[32,27]{1,0:T(8,128)S(1)}, s32[32,27]{1,0:T(8,128)}, u32[]{:S(2)}) copy-start(s32[32,27]{1,0:T(8,128)} %ulist_ref.1) | copy-start | bytes 10372
  4.8 17.0 %collective-permute-start = (f32[832,128]{1,0:T(8,128)}, f32[832,128]{1,0:T(8,128)S(1)}, u32[]{:S(2)}, u32[]{:S(2)}) collective-permute-start(f32[832,128]{1,0:T(8,128)} %get-tuple-element.12), channel_id=1, source_target_pairs={{0,1},{1,0},{2,3},{3,2},{4,5},{5,4},{6,7},{7,6},{8,9},{9,8},{10,11... | collective-permute-start | bytes 1277960 | tf_op jit(solution)/shard_map/ppermute | solution.py:25
  5.5 8.0 %collective-permute-start.1 = (f32[192,128]{1,0:T(8,128)}, f32[192,128]{1,0:T(8,128)S(1)}, u32[]{:S(2)}, u32[]{:S(2)}) collective-permute-start(f32[192,128]{1,0:T(8,128)} %get-tuple-element.13), channel_id=1, source_target_pairs={{1,2},{2,1},{3,4},{4,3},{5,6},{6,5},{7,8},{8,7},{9,10},{10,9},{11,... | collective-permute-start | bytes 294920 | tf_op jit(solution)/shard_map/ppermute | solution.py:621
  8.6 26.0 %collective-permute-start.2 = (f32[640,128]{1,0:T(8,128)}, f32[640,128]{1,0:T(8,128)S(1)}, u32[]{:S(2)}, u32[]{:S(2)}) collective-permute-start(f32[640,128]{1,0:T(8,128)} %get-tuple-element.14.refs_0_), channel_id=1, source_target_pairs={{0,2},{1,3},{2,0},{3,1},{4,6},{5,7},{6,4},{7,5},{8,10},{9,11},{10,... | collective-permute-start | bytes 983048 | tf_op jit(solution)/shard_map/ppermute | solution.py:25
  8.9 25.7 %collective-permute-start.3 = (f32[640,128]{1,0:T(8,128)}, f32[640,128]{1,0:T(8,128)S(1)}, u32[]{:S(2)}, u32[]{:S(2)}) collective-permute-start(f32[640,128]{1,0:T(8,128)} %get-tuple-element.14.refs_0_), channel_id=1, source_target_pairs={{0,16},{1,17},{2,18},{3,19},{4,20},{5,21},{6,22},{7,23},{8,24},{9,... | collective-permute-start | bytes 983048 | tf_op jit(solution)/shard_map/ppermute | solution.py:25
  11.2 23.4 %collective-permute-start.4 = (f32[640,128]{1,0:T(8,128)}, f32[640,128]{1,0:T(8,128)S(1)}, u32[]{:S(2)}, u32[]{:S(2)}) collective-permute-start(f32[640,128]{1,0:T(8,128)} %get-tuple-element.14.refs_0_), channel_id=1, source_target_pairs={{0,8},{1,9},{2,10},{3,11},{4,12},{5,13},{6,14},{7,15},{8,0},{9,1},... | collective-permute-start | bytes 983048 | tf_op jit(solution)/shard_map/ppermute | solution.py:25
  11.4 23.2 %copy-start = (f32[152,2432]{1,0:T(8,128)S(1)}, f32[152,2432]{1,0:T(8,128)}, u32[]{:S(2)}) copy-start(f32[152,2432]{1,0:T(8,128)} %m2l_ref.1) | copy-start | bytes 4435972
  11.4 23.2 %copy-start.1 = (f32[640,128]{1,0:T(8,128)S(1)}, f32[640,128]{1,0:T(8,128)}, u32[]{:S(2)}) copy-start(f32[640,128]{1,0:T(8,128)} %get-tuple-element.14.refs_0_) | copy-start | bytes 983044
  11.4 23.2 %copy-start.3 = (f32[152,152]{1,0:T(8,128)S(1)}, f32[152,152]{1,0:T(8,128)}, u32[]{:S(2)}) copy-start(f32[152,152]{1,0:T(8,128)} %dc2e_ref.1) | copy-start | bytes 277252
  11.4 23.2 %copy-start.6 = (s32[32,32]{1,0:T(8,128)S(1)}, s32[32,32]{1,0:T(8,128)}, u32[]{:S(2)}) copy-start(s32[32,32]{1,0:T(8,128)} %vsrc_ref.1) | copy-start | bytes 12292
  11.4 23.2 %copy-start.7 = (s32[32,32]{1,0:T(8,128)S(1)}, s32[32,32]{1,0:T(8,128)}, u32[]{:S(2)}) copy-start(s32[32,32]{1,0:T(8,128)} %vtype_ref.1) | copy-start | bytes 12292
  11.4 23.2 %copy-start.9 = (bf16[160,4096]{1,0:T(8,128)(2,1)S(1)}, bf16[160,4096]{1,0:T(8,128)(2,1)}, u32[]{:S(2)}) copy-start(bf16[160,4096]{1,0:T(8,128)(2,1)} %get-tuple-element.10.tile_hi_ref) | copy-start | bytes 3932164
  11.4 23.2 %copy-start.10 = (bf16[160,4096]{1,0:T(8,128)(2,1)S(1)}, bf16[160,4096]{1,0:T(8,128)(2,1)}, u32[]{:S(2)}) copy-start(bf16[160,4096]{1,0:T(8,128)(2,1)} %get-tuple-element.11.tile_lo_ref) | copy-start | bytes 3932164
  13.6 21.0 %collective-permute-start.5 = (f32[640,128]{1,0:T(8,128)}, f32[640,128]{1,0:T(8,128)S(1)}, u32[]{:S(2)}, u32[]{:S(2)}) collective-permute-start(f32[640,128]{1,0:T(8,128)} %get-tuple-element.14.refs_0_), channel_id=1, source_target_pairs={{0,4},{1,5},{2,6},{3,7},{4,0},{5,1},{6,2},{7,3},{8,12},{9,13},{10,... | collective-permute-start | bytes 983048 | tf_op jit(solution)/shard_map/ppermute | solution.py:25

commit v4 on v3

--- a/solution.py
+++ b/solution.py
@@ -40,8 +40,84 @@
     return summed.astype(jnp.float32)
 
 
-def near_kernel(first_ref, counts_ref, offsets_ref, charges_ref, pair_ref, odd_ref, ulist_ref, out_ref,
-                ghost_ref,
+def prepare(m2l_ref, vsrc_ref, vtype_ref, w_hi_ref, w_lo_ref, twice_ref, code_ref, tally_ref):
+    f32, bf16, i32 = jnp.float32, jnp.bfloat16, jnp.int32
+    local = vsrc_ref.shape[0]
+    equiv = m2l_ref.shape[0]
+    kinds = m2l_ref.shape[1] // equiv
+    depth = twice_ref.shape[1] // 2
+    rest = equiv - PTS
+    lane = lax.broadcasted_iota(i32, (1, PTS), 1)
+
+    grown = w_hi_ref.shape[0]
+    fill = jnp.zeros((grown - equiv, PTS), f32)
+
+    def lanes_from(at, count):
+        block, shift = at // PTS, at % PTS
+        part = m2l_ref[:, block * PTS:(block + 1) * PTS]
+        if shift:
+            part = pltpu.roll(part, PTS - shift, 1)
+            if shift + count > PTS:
+                after = pltpu.roll(m2l_ref[:, (block + 1) * PTS:(block + 2) * PTS], PTS - shift, 1)
+                part = jnp.where(lane < PTS - shift, part, after)
+        return part
+
+    def tail_from(at, to):
+        block, shift = at // PTS, at % PTS
+        part = pltpu.roll(m2l_ref[:, block * PTS:(block + 1) * PTS], (to - shift) % PTS, 1)
+        if shift + rest > PTS:
+            after = pltpu.roll(m2l_ref[:, (block + 1) * PTS:(block + 2) * PTS], (to - shift) % PTS, 1)
+            part = jnp.where(lane < to + PTS - shift, part, after)
+        return part
+
+    def operators(first):
+        for t in range(first, first + 4):
+            main = jnp.concatenate([lanes_from(t * equiv, PTS), fill], 0)
+            w_hi_ref[:, t * PTS:(t + 1) * PTS], w_lo_ref[:, t * PTS:(t + 1) * PTS] = split(main)
+        tail = jnp.zeros((equiv, PTS), f32)
+        for k in range(4):
+            mine = (lane >= 32 * k) & (lane < 32 * k + rest)
+            tail = jnp.where(mine, tail_from((first + k) * equiv + PTS, 32 * k), tail)
+        tail = jnp.concatenate([tail, fill], 0)
+        at = kinds * PTS + first * 32
+        w_hi_ref[:, at:at + PTS], w_lo_ref[:, at:at + PTS] = split(tail)
+
+    for first in range(0, kinds, 4):
+        operators(first)
+    slots = vsrc_ref.shape[1]
+    code_ref[...] = jnp.full(code_ref.shape, -1.0, f32)
+    code_ref[0:local, 0:slots] = vsrc_ref[...].astype(f32)
+    code_ref[local:, 0:slots] = vtype_ref[...].astype(f32)
+
+    per = PTS // slots
+    spot = lax.broadcasted_iota(i32, (8, 8 * slots), 1) // slots == lax.broadcasted_iota(i32, (8, 8 * slots), 0)
+
+    def flat(value):
+        wide = jnp.where(lane < slots, value, 0.0)
+        total = wide
+        for k in range(1, per):
+            total = total + pltpu.roll(wide, slots * k, 1)
+        total = jnp.concatenate([total] * (8 // per), 1)
+        return jnp.sum(jnp.where(spot, total, 0.0), 0, keepdims=True)
+
+    row_id = lax.broadcasted_iota(i32, (8 * kinds, 8 * slots), 0)
+    mine = lax.broadcasted_iota(i32, (8 * kinds, 8 * slots), 1) // slots == row_id % 8
+    kind = (row_id // 8).astype(f32)
+    table_row = lax.broadcasted_iota(i32, (2 * depth, 8 * slots), 0)
+    table_row = jnp.where(table_row < depth, table_row, table_row - depth).astype(f32)
+    for g in range(0, local, 8):
+        take = flat(code_ref[g:g + 8, :])
+        sort = flat(code_ref[local + g:local + g + 8, :])
+        pick = jnp.where(mine & (sort == kind), 1.0, 0.0).astype(bf16)
+        hit = jnp.where(take == table_row, 1.0, 0.0).astype(bf16)
+        count = dot_t(pick, hit)
+        for t in range(kinds):
+            tally_ref[t * local + g:t * local + g + 8, :] = count[8 * t:8 * t + 8]
+    twice_ref[...] = tally_ref[...].astype(bf16)
+
+
+def near_kernel(first_ref, counts_ref, offsets_ref, charges_ref, pair_ref, odd_ref, ulist_ref, m2l_ref, vsrc_ref, vtype_ref,
+                out_ref, w_hi_ref, w_lo_ref, twice_ref, code_ref, tally_ref, ghost_ref,
                 lanes_ref, chg_ref, src_ref, tgt_ref, square_ref, hi_ref, lo_ref, acc_ref,
                 mult_ref, res_ref, start_ref, leaf_ref, from_ref, to_ref, open_ref, shut_ref):
     f32, bf16, i32 = jnp.float32, jnp.bfloat16, jnp.int32
@@ -136,6 +212,8 @@
             mult_ref[pl.ds(here, every), :] = jnp.where(keep, col, mult_ref[pl.ds(here, every), :])
             mult_ref[pl.ds(after, every), :] = col
 
+    prepare(m2l_ref, vsrc_ref, vtype_ref, w_hi_ref, w_lo_ref, twice_ref, code_ref, tally_ref)
+
     group = 4 * PTS
     head = starts[0] >> 7
     tail = (starts[every] + 127) >> 7
@@ -260,9 +338,10 @@
         out_ref[:, g * PTS:(g + 1) * PTS] = jnp.where(lane < counts_ref[g], value * inv_four_pi, 0.0)
 
 
-def near_call(first, counts, offsets, charges, pair, odd, u_list):
+def near_call(first, counts, offsets, charges, pair, odd, u_list, m2l, v_src, v_type, depth):
     local = counts.shape[0]
     probes = charges.shape[0]
+    kinds = m2l.shape[1] // m2l.shape[0]
     every = local + 2 * GHOST
     width = every * PTS + 8 * PTS + 512
     targets = local * PTS + 512
@@ -270,10 +349,17 @@
     vmem = pl.BlockSpec(memory_space=pltpu.VMEM)
     return pl.pallas_call(
         near_kernel,
-        out_shape=jax.ShapeDtypeStruct((probes, local * PTS), jnp.float32),
-        in_specs=[smem, smem, vmem, vmem, vmem, vmem, vmem],
-        out_specs=vmem,
+        out_shape=(
+            jax.ShapeDtypeStruct((probes, local * PTS), jnp.float32),
+            jax.ShapeDtypeStruct((2 * PTS, kinds * (PTS + 32)), jnp.bfloat16),
+            jax.ShapeDtypeStruct((2 * PTS, kinds * (PTS + 32)), jnp.bfloat16),
+            jax.ShapeDtypeStruct((kinds * local, 2 * depth), jnp.bfloat16),
+        ),
+        in_specs=[smem, smem] + [vmem] * 8,
+        out_specs=(vmem,) * 4,
         scratch_shapes=[
+            pltpu.VMEM((2 * local, PTS), jnp.float32),
+            pltpu.VMEM((kinds * local, 2 * depth), jnp.float32),
             pltpu.VMEM((2, GHOST * (8 + probes), PTS), jnp.float32),
             pltpu.VMEM((8 + probes, width), jnp.float32),
             pltpu.VMEM((2 * probes, width), jnp.bfloat16),
@@ -295,7 +381,7 @@
         compiler_params=pltpu.CompilerParams(vmem_limit_bytes=24 << 20),
         cost_estimate=pl.CostEstimate(flops=4_000_000_000, bytes_accessed=2_000_000, transcendentals=4_000_000),
         name="near",
-    )(first, counts, offsets, charges, pair, odd, u_list)
+    )(first, counts, offsets, charges, pair, odd, u_list, m2l, v_src, v_type)
 
 
 def split(value):
@@ -457,110 +543,80 @@
 
 
 def send_order(count):
-    return [count - 1, 1, *range(count - 2, 1, -1), 0]
-
-
-def far_kernel(counts_ref, wanted_ref, tile_hi_ref, tile_lo_ref, near_ref, vsrc_ref, vtype_ref, m2l_ref, dc2e_ref,
+    half = count // 2
+    return [count - 1, *range(half, count - 1), *range(half - 1, 0, -1), 0]
+
+
+def far_kernel(counts_ref, wanted_ref, tile_hi_ref, tile_lo_ref, near_ref, w_hi_ref, w_lo_ref, twice_ref, dc2e_ref,
                *refs):
     f32, bf16, i32 = jnp.float32, jnp.bfloat16, jnp.int32
-    sent = refs[:-9]
+    sent = refs[:-6]
     pieces = [sent[i] for i in np.argsort(send_order(len(sent)))]
-    out_ref, code_ref, tally_ref, table_ref, x_hi_ref, x_lo_ref, w_hi_ref, w_lo_ref, eq_ref = refs[-9:]
+    out_ref, pick_ref, table_ref, x_hi_ref, x_lo_ref, eq_ref = refs[-6:]
     probes, points = out_ref.shape
     local = points // PTS
     bits, cap = wanted_ref.shape
-    depth = len(pieces) * local
-    equiv = m2l_ref.shape[0]
-    kinds = m2l_ref.shape[1] // equiv
-    rest = equiv - PTS
+    depth = bits * cap + local
+    kinds = w_hi_ref.shape[1] // (PTS + 32)
+    twice = twice_ref[...]
     rows = probes * local
     lane = lax.broadcasted_iota(i32, (1, PTS), 1)
 
-    w_hi_ref[...] = jnp.zeros_like(w_hi_ref)
-    w_lo_ref[...] = jnp.zeros_like(w_lo_ref)
-    grown = w_hi_ref.shape[0]
-    fill = jnp.zeros((grown - equiv, PTS), f32)
-    for t in range(kinds):
-        main = jnp.concatenate([m2l_ref[:, t * equiv:t * equiv + PTS], fill], 0)
-        w_hi_ref[:, t * PTS:(t + 1) * PTS], w_lo_ref[:, t * PTS:(t + 1) * PTS] = split(main)
-    gap = jnp.zeros((equiv, 32 - rest), f32)
-    for t in range(0, kinds, 4):
-        row = []
-        for k in range(4):
-            row += [m2l_ref[:, (t + k) * equiv + PTS:(t + k + 1) * equiv], gap]
-        tail = jnp.concatenate([jnp.concatenate(row, 1), fill], 0)
-        at = kinds * PTS + t * 32
-        w_hi_ref[:, at:at + PTS], w_lo_ref[:, at:at + PTS] = split(tail)
-
-    codes = vsrc_ref[...]
-    slots = codes.shape[1]
-    found = codes - bits * cap + bits * local
+    blocks = probes * 5 // 4
     for b in range(bits):
-        for s in range(cap):
-            found = jnp.where(codes == b * cap + s, b * local + wanted_ref[b, s], found)
-    code_ref[...] = jnp.full(code_ref.shape, -1.0, f32)
-    code_ref[0:local, 0:slots] = found.astype(f32)
-    code_ref[local:, 0:slots] = vtype_ref[...].astype(f32)
-
-    per = PTS // slots
-    spot = lax.broadcasted_iota(i32, (8, 8 * slots), 1) // slots == lax.broadcasted_iota(i32, (8, 8 * slots), 0)
-
-    def flat(value):
-        wide = jnp.where(lane < slots, value, 0.0)
-        total = wide
-        for k in range(1, per):
-            total = total + pltpu.roll(wide, slots * k, 1)
-        total = jnp.concatenate([total] * (8 // per), 1)
-        return jnp.sum(jnp.where(spot, total, 0.0), 0, keepdims=True)
-
-    row_id = lax.broadcasted_iota(i32, (8 * kinds, 8 * slots), 0)
-    mine = lax.broadcasted_iota(i32, (8 * kinds, 8 * slots), 1) // slots == row_id % 8
-    kind = (row_id // 8).astype(f32)
-    table_row = lax.broadcasted_iota(i32, (depth, 8 * slots), 0).astype(f32)
-    for g in range(0, local, 8):
-        take = flat(code_ref[g:g + 8, :])
-        sort = flat(code_ref[local + g:local + g + 8, :])
-        pick = jnp.where(mine & (sort == kind), 1.0, 0.0).astype(bf16)
-        hit = jnp.where(take == table_row, 1.0, 0.0).astype(bf16)
-        count = dot_t(pick, hit)
-        for t in range(kinds):
-            tally_ref[t * local + g:t * local + g + 8, :] = count[8 * t:8 * t + 8]
-    tally = tally_ref[...].astype(bf16)
-
-    blocks = probes * 5 // 4
-    for b, piece in enumerate(pieces):
-        for n in range(blocks):
-            hi, lo = split(piece[n * local:(n + 1) * local, :])
-            table_ref[b * local:(b + 1) * local, n * PTS:(n + 1) * PTS] = hi
-            table_ref[depth + b * local:depth + (b + 1) * local, n * PTS:(n + 1) * PTS] = lo
-
-    twice = jnp.concatenate([tally, tally], 1)
+        for c in range(cap):
+            pick_ref[pl.ds(b * cap + c, blocks, stride=depth), :] = pieces[b][pl.ds(wanted_ref[b, c], blocks, stride=local), :]
+    for n in range(blocks):
+        pick_ref[n * depth + bits * cap:(n + 1) * depth, :] = pieces[bits][n * local:(n + 1) * local, :]
+    for n in range(blocks):
+        hi, lo = split(pick_ref[n * depth:(n + 1) * depth, :])
+        table_ref[:depth, n * PTS:(n + 1) * PTS] = hi
+        table_ref[depth:, n * PTS:(n + 1) * PTS] = lo
+
     group = lane // 32
     quarter = probes // 4
-    for n in range(0, blocks, 2):
+    def spread(part, q):
+        hi, lo = split(part)
+        for t in range(kinds):
+            x_hi_ref[q * local:(q + 1) * local, t * PTS:(t + 1) * PTS] = hi[t * local:(t + 1) * local]
+            x_lo_ref[q * local:(q + 1) * local, t * PTS:(t + 1) * PTS] = lo[t * local:(t + 1) * local]
+
+    def spread_rest(part, q):
+        for t in range(0, kinds, 4):
+            kinds4 = [part[(t + i) * local:(t + i + 1) * local] for i in range(4)]
+
+            def mix(pick):
+                value = pick(3)
+                for i in range(3):
+                    value = jnp.where(group == i, pick(i), value)
+                return value
+
+            moved = []
+            for shift in range(4):
+                value = mix(lambda k: kinds4[(k + shift) % 4])
+                moved.append(pltpu.roll(value, 32 * shift, 1) if shift else value)
+            at = kinds * PTS + t * 32
+            for k in range(4):
+                to = (q + quarter * k) * local
+                value = mix(lambda i: moved[(i - k) % 4])
+                x_hi_ref[to:to + local, at:at + PTS], x_lo_ref[to:to + local, at:at + PTS] = split(value)
+
+    for n in range(0, probes, 2):
         both = dot(twice, table_ref[:, n * PTS:(n + 2) * PTS])
-        for half in range(2):
-            q = n + half
-            part = both[:, half * PTS:(half + 1) * PTS]
-            if q < probes:
-                hi, lo = split(part)
-                for t in range(kinds):
-                    x_hi_ref[q * local:(q + 1) * local, t * PTS:(t + 1) * PTS] = hi[t * local:(t + 1) * local]
-                    x_lo_ref[q * local:(q + 1) * local, t * PTS:(t + 1) * PTS] = lo[t * local:(t + 1) * local]
-            else:
-                for k in range(4):
-                    to = (q - probes + quarter * k) * local
-                    for t in range(0, kinds, 4):
-                        value = jnp.zeros((local, PTS), f32)
-                        for i in range(4):
-                            moved = part[(t + i) * local:(t + i + 1) * local]
-                            if i != k:
-                                moved = pltpu.roll(moved, (32 * (i - k)) % PTS, 1)
-                            value = jnp.where(group == i, moved, value)
-                        at = kinds * PTS + t * 32
-                        x_hi_ref[to:to + local, at:at + PTS], x_lo_ref[to:to + local, at:at + PTS] = split(value)
-
-    down = dot_t(x_hi_ref[...], w_hi_ref[...]) + (dot_t(x_hi_ref[...], w_lo_ref[...]) + dot_t(x_lo_ref[...], w_hi_ref[...]))
+        spread(both[:, :PTS], n)
+        spread(both[:, PTS:], n + 1)
+
+    def down_part(at):
+        x_hi, x_lo, w_hi, w_lo = x_hi_ref[:, at], x_lo_ref[:, at], w_hi_ref[:, at], w_lo_ref[:, at]
+        return dot_t(jnp.concatenate([x_hi, x_hi, x_lo], 1), jnp.concatenate([w_hi, w_lo, w_hi], 1))
+
+    down = None
+    for c in range(kinds // 4):
+        value = down_part(slice(4 * c * PTS, 4 * (c + 1) * PTS))
+        down = value if down is None else down + value
+        for q in range(c, quarter, kinds // 4):
+            spread_rest(dot(twice, table_ref[:, (probes + q) * PTS:(probes + q + 1) * PTS]), q)
+    down = down + down_part(slice(kinds * PTS, kinds * (PTS + 32)))
     equivs = dot_t3(down, padded(dc2e_ref, 2 * PTS, 2 * PTS))
     eq_ref[0], eq_ref[1] = equivs[:, :PTS], equivs[:, PTS:]
 
@@ -582,35 +638,32 @@
             out_ref[:, to] = jnp.where(lane < counts_ref[h], near_ref[:, to] + part, 0.0)
 
 
-def far_call(counts, wanted, tiles, near, v_src, v_type, m2l, dc2e, pieces):
+def far_call(counts, wanted, tiles, near, w_hi, w_lo, twice, dc2e, pieces):
     local = counts.shape[0]
     probes, points = near.shape
-    equiv = dc2e.shape[0]
-    kinds = m2l.shape[1] // equiv
+    kinds = w_hi.shape[1] // (PTS + 32)
     smem = pl.BlockSpec(memory_space=pltpu.SMEM)
     vmem = pl.BlockSpec(memory_space=pltpu.VMEM)
     f32, bf16 = jnp.float32, jnp.bfloat16
     rows = probes * local
     wide = kinds * (PTS + 32)
+    depth = wanted.shape[0] * wanted.shape[1] + local
     return pl.pallas_call(
         far_kernel,
         out_shape=jax.ShapeDtypeStruct((probes, points), f32),
         in_specs=[smem, smem] + [vmem] * (7 + len(pieces)),
         out_specs=vmem,
         scratch_shapes=[
-            pltpu.VMEM((2 * local, PTS), f32),
-            pltpu.VMEM((kinds * local, len(pieces) * local), f32),
-            pltpu.VMEM((2 * len(pieces) * local, probes * 5 // 4 * PTS), bf16),
+            pltpu.VMEM((probes * 5 // 4 * depth, PTS), f32),
+            pltpu.VMEM((2 * depth, probes * 5 // 4 * PTS), bf16),
             pltpu.VMEM((rows, wide), bf16),
             pltpu.VMEM((rows, wide), bf16),
-            pltpu.VMEM((2 * PTS, wide), bf16),
-            pltpu.VMEM((2 * PTS, wide), bf16),
             pltpu.VMEM((2, rows, PTS), f32),
         ],
         compiler_params=pltpu.CompilerParams(vmem_limit_bytes=32 << 20),
         cost_estimate=pl.CostEstimate(flops=4_000_000_000, bytes_accessed=4_000_000, transcendentals=600_000),
         name="far",
-    )(counts, wanted, *tiles, near, v_src, v_type, m2l, dc2e, *(pieces[i] for i in send_order(len(pieces))))
+    )(counts, wanted, *tiles, near, w_hi, w_lo, twice, dc2e, *(pieces[i] for i in send_order(len(pieces))))
 
 
 def shards(offsets, charges, counts, u_list, v_src, v_type, wanted, m2l, uc2e, dc2e):
@@ -622,8 +675,9 @@
     pieces = [from_partner(up, "cube", bit) for bit in range(count.bit_length() - 2, 0, -1)]
     pair = from_partner(pair, "cube", 0)
     pieces = [pair] + pieces[::-1] + [up]
-    near = near_call(first, counts, offsets, charges, pair, odd, u_list)
-    return far_call(counts, wanted[0], (tile_hi, tile_lo), near, v_src, v_type, m2l, dc2e, pieces)
+    depth = wanted.shape[1] * wanted.shape[2] + counts.shape[0]
+    near, w_hi, w_lo, twice = near_call(first, counts, offsets, charges, pair, odd, u_list, m2l, v_src, v_type, depth)
+    return far_call(counts, wanted[0], (tile_hi, tile_lo), near, w_hi, w_lo, twice, dc2e, pieces)
 
 
 def solution(mesh):

time: 43.5 us -> 38.7 us (0.89)
  the two profiles are of different devices: /device:TPU:11 before, /device:TPU:0 now
where the time goes in v4:
time: 38.7 us; the launch traced here: 38.6 us
  Pallas kernels  24 us (62%)
  starting transfers between devices  11.4 us (29%)
  waiting for transfers between devices  2.96 us (8%)
    pallas_call x1, Pallas kernels, near_call(): pl.pallas_call(near_kernel, out_shape=(jax.ShapeDtypeStruct((probes, loca...  11.3 us
    ppermute x5, starting transfers between devices, from_partner(): lax.ppermute(array, axis, [(i, i ^ 1 << bit) for i in range(lax.axis_size...  10.7 us
    pallas_call x1, Pallas kernels, far_call(): pl.pallas_call(far_kernel, out_shape=jax.ShapeDtypeStruct((probes, points...  7.89 us
    pallas_call x1, Pallas kernels, up_call(): pl.pallas_call(up_kernel, out_shape=(jax.ShapeDtypeStruct((ghost, PTS), f...  4.83 us
    ppermute x5, waiting for transfers between devices, from_partner(): lax.ppermute(array, axis, [(i, i ^ 1 << bit) for i in range(lax.axis_size...  2.96 us
  transfers between devices with their start and end apart: 6, of which 2 were waited for; matrix products, arithmetic and copies ran while one was open for 0% of the time, Pallas kernels for 29%

profile of v4, /device:TPU:0, one launch (start us, length us, event | category | flops | bytes accessed | tf_op | source)
XLA Modules:
  0.0 38.6 jit_solution(14958896424772907147)
XLA Ops:
  0.0 0.0 copy-start.7
  0.0 0.0 copy-start.6
  0.0 0.0 copy-start.5
  0.0 4.8 %upward.1 = (f32[192,128]{1,0:T(8,128)}, f32[832,128]{1,0:T(8,128)}, f32[640,128]{1,0:T(8,128)}, bf16[160,4096]{1,0:T(8,128)(2,1)}, bf16[160,4096]{1,0:T(8,128)(2,1)}) custom-call(s32[1]{0:T(128)} %bitcast.first_ref, s32[32]{0:T(128)} %counts_ref.3, f32[3,4096]{1,0:T(4,128)} %offsets_ref.1, f32[16,4096]{1,0:T(8,128)} %charges_ref.1, f32[152,152]{1,0:T(8,128)} %uc2e_hbm.1, ...), custom_call_target="tpu_custom_call" | custom-call | flops 500000000 | bytes 1500000 | tf_op jit(solution)/shard_map/upward/pallas_call | solution.py:517
  4.9 0.5 %collective-permute-start = (f32[832,128]{1,0:T(8,128)}, f32[832,128]{1,0:T(8,128)S(1)}, u32[]{:S(2)}, u32[]{:S(2)}) collective-permute-start(f32[832,128]{1,0:T(8,128)} %get-tuple-element.16), channel_id=1, source_target_pairs={{0,1},{1,0},{2,3},{3,2},{4,5},{5,4},{6,7},{7,6},{8,9},{9,8},{10,11... | collective-permute-start | bytes 1277960 | tf_op jit(solution)/shard_map/ppermute | solution.py:25
  5.4 0.7 %collective-permute-start.1 = (f32[192,128]{1,0:T(8,128)}, f32[192,128]{1,0:T(8,128)S(1)}, u32[]{:S(2)}, u32[]{:S(2)}) collective-permute-start(f32[192,128]{1,0:T(8,128)} %get-tuple-element.17), channel_id=1, source_target_pairs={{1,2},{2,1},{3,4},{4,3},{5,6},{6,5},{7,8},{8,7},{9,10},{10,9},{11,... | collective-permute-start | bytes 294920 | tf_op jit(solution)/shard_map/ppermute | solution.py:674
  6.1 3.8 %collective-permute-start.5 = (f32[640,128]{1,0:T(8,128)}, f32[640,128]{1,0:T(8,128)S(1)}, u32[]{:S(2)}, u32[]{:S(2)}) collective-permute-start(f32[640,128]{1,0:T(8,128)} %get-tuple-element.22.refs_0_), channel_id=1, source_target_pairs={{0,2},{1,3},{2,0},{3,1},{4,6},{5,7},{6,4},{7,5},{8,10},{9,11},{10,... | collective-permute-start | bytes 983048 | tf_op jit(solution)/shard_map/ppermute | solution.py:25
  9.9 2.1 %collective-permute-start.4 = (f32[640,128]{1,0:T(8,128)}, f32[640,128]{1,0:T(8,128)S(1)}, u32[]{:S(2)}, u32[]{:S(2)}) collective-permute-start(f32[640,128]{1,0:T(8,128)} %get-tuple-element.22.refs_0_), channel_id=1, source_target_pairs={{0,4},{1,5},{2,6},{3,7},{4,0},{5,1},{6,2},{7,3},{8,12},{9,13},{10,... | collective-permute-start | bytes 983048 | tf_op jit(solution)/shard_map/ppermute | solution.py:25
  12.0 2.6 %collective-permute-start.3 = (f32[640,128]{1,0:T(8,128)}, f32[640,128]{1,0:T(8,128)S(1)}, u32[]{:S(2)}, u32[]{:S(2)}) collective-permute-start(f32[640,128]{1,0:T(8,128)} %get-tuple-element.22.refs_0_), channel_id=1, source_target_pairs={{0,16},{1,17},{2,18},{3,19},{4,20},{5,21},{6,22},{7,23},{8,24},{9,... | collective-permute-start | bytes 983048 | tf_op jit(solution)/shard_map/ppermute | solution.py:25
  14.6 0.0 copy-done.11
  14.6 0.0 copy-start.9
  14.7 0.0 copy-start.10
  14.7 0.0 collective-permute-done.1.odd_ref
  14.7 1.6 %collective-permute-start.2 = (f32[640,128]{1,0:T(8,128)}, f32[640,128]{1,0:T(8,128)S(1)}, u32[]{:S(2)}, u32[]{:S(2)}) collective-permute-start(f32[640,128]{1,0:T(8,128)} %get-tuple-element.22.refs_0_), channel_id=1, source_target_pairs={{0,8},{1,9},{2,10},{3,11},{4,12},{5,13},{6,14},{7,15},{8,0},{9,1},... | collective-permute-start | bytes 983048 | tf_op jit(solution)/shard_map/ppermute | solution.py:25
  16.3 0.0 collective-permute-done.pair_ref.refs_5_
  16.3 0.0 copy-done.8
  16.3 0.0 copy-done.2
  16.3 0.0 copy-done.4
  16.3 0.0 copy-done
  16.3 0.0 copy-done.7
  16.4 0.0 copy-done.6
  16.4 0.0 copy-done.5
  16.4 11.3 %near.1 = (f32[16,4096]{1,0:T(8,128)S(1)}, bf16[256,2560]{1,0:T(8,128)(2,1)S(1)}, bf16[256,2560]{1,0:T(8,128)(2,1)S(1)}, bf16[512,224]{1,0:T(8,128)(2,1)S(1)}) custom-call(s32[1]{0:T(128)} %bitcast.first_ref, s32[32]{0:T(128)S(1)} %copy-done.8, f32[3,4096]{1,0:T(4,128)S(1)} %copy-done.4, f32[16,4096]{1,0:T(8,128)S(1)} %copy-done.2, ...), custom_call_target="tpu_custom_call" | custom-call | flops 4000000000 | bytes 2000000 | tf_op jit(solution)/shard_map/near/pallas_call | solution.py:350
  27.7 0.0 collective-permute-done.5.refs_4_
  27.7 0.0 collective-permute-done.4.refs_3_
  27.7 2.7 %collective-permute-done.3.refs_2_ = f32[640,128]{1,0:T(8,128)S(1)} collective-permute-done((f32[640,128]{1,0:T(8,128)}, f32[640,128]{1,0:T(8,128)S(1)}, u32[]{:S(2)}, u32[]{:S(2)}) %collective-permute-start.3) | collective-permute-done | bytes 327712 | tf_op jit(solution)/shard_map/ppermute | solution.py:25
  30.3 0.3 collective-permute-done.2.refs_1_
  30.6 0.0 copy-done.1
  30.6 0.0 copy-done.3
  30.6 0.0 copy-done.9
  30.6 0.0 copy-done.10
  30.7 7.9 %far.1 = f32[16,4096]{1,0:T(8,128)} custom-call(s32[32]{0:T(128)S(1)} %copy-done.8, s32[5,16]{1,0:T(8,128)S(1)} %bitcast.4, bf16[160,4096]{1,0:T(8,128)(2,1)S(1)} %copy-done.9, bf16[160,4096]{1,0:T(8,128)(2,1)S(1)} %copy-done.10, f32[16,4096]{1,0:T(8,128)S(1)} %get-tuple-element.18.near_ref, bf16[256,2560]{1,0:T(8,128)(2,1)S(1)} %get-tuple-element.19.w_hi_ref, ...), custom_call_target="tpu_custom_call" | custom-call | flops 4000000000 | bytes 4000000 | tf_op jit(solution)/shard_map/far/pallas_call | solution.py:651
  (8 shorter events, 0.0 us)
Async XLA Ops:
  0.0 16.3 %copy-start.8 = (s32[32]{0:T(128)S(1)}, s32[32]{0:T(128)}, u32[]{:S(2)}) copy-start(s32[32]{0:T(128)} %counts_ref.3) | copy-start | bytes 388
  0.0 16.3 %copy-start.2 = (f32[16,4096]{1,0:T(8,128)S(1)}, f32[16,4096]{1,0:T(8,128)}, u32[]{:S(2)}) copy-start(f32[16,4096]{1,0:T(8,128)} %charges_ref.1) | copy-start | bytes 786436
  0.0 16.3 %copy-start.4 = (f32[3,4096]{1,0:T(4,128)S(1)}, f32[3,4096]{1,0:T(4,128)}, u32[]{:S(2)}) copy-start(f32[3,4096]{1,0:T(4,128)} %offsets_ref.1) | copy-start | bytes 147460
  0.0 14.6 %copy-start.11 = (s32[1,5,16]{2,0,1:T(1,128)S(1)}, s32[1,5,16]{2,0,1:T(1,128)}, u32[]{:S(2)}) copy-start(s32[1,5,16]{2,0,1:T(1,128)} %param.17) | copy-start | bytes 964
  0.0 16.3 %copy-start = (f32[152,2432]{1,0:T(8,128)S(1)}, f32[152,2432]{1,0:T(8,128)}, u32[]{:S(2)}) copy-start(f32[152,2432]{1,0:T(8,128)} %m2l_ref.1) | copy-start | bytes 4435972
  0.0 16.3 %copy-start.7 = (s32[32,32]{1,0:T(8,128)S(1)}, s32[32,32]{1,0:T(8,128)}, u32[]{:S(2)}) copy-start(s32[32,32]{1,0:T(8,128)} %vtype_ref.1) | copy-start | bytes 12292
  0.0 16.3 %copy-start.6 = (s32[32,32]{1,0:T(8,128)S(1)}, s32[32,32]{1,0:T(8,128)}, u32[]{:S(2)}) copy-start(s32[32,32]{1,0:T(8,128)} %vsrc_ref.1) | copy-start | bytes 12292
  0.0 16.3 %copy-start.5 = (s32[32,27]{1,0:T(8,128)S(1)}, s32[32,27]{1,0:T(8,128)}, u32[]{:S(2)}) copy-start(s32[32,27]{1,0:T(8,128)} %ulist_ref.1) | copy-start | bytes 10372
  4.9 11.4 %collective-permute-start = (f32[832,128]{1,0:T(8,128)}, f32[832,128]{1,0:T(8,128)S(1)}, u32[]{:S(2)}, u32[]{:S(2)}) collective-permute-start(f32[832,128]{1,0:T(8,128)} %get-tuple-element.16), channel_id=1, source_target_pairs={{0,1},{1,0},{2,3},{3,2},{4,5},{5,4},{6,7},{7,6},{8,9},{9,8},{10,11... | collective-permute-start | bytes 1277960 | tf_op jit(solution)/shard_map/ppermute | solution.py:25
  5.4 9.2 %collective-permute-start.1 = (f32[192,128]{1,0:T(8,128)}, f32[192,128]{1,0:T(8,128)S(1)}, u32[]{:S(2)}, u32[]{:S(2)}) collective-permute-start(f32[192,128]{1,0:T(8,128)} %get-tuple-element.17), channel_id=1, source_target_pairs={{1,2},{2,1},{3,4},{4,3},{5,6},{6,5},{7,8},{8,7},{9,10},{10,9},{11,... | collective-permute-start | bytes 294920 | tf_op jit(solution)/shard_map/ppermute | solution.py:674
  6.1 21.6 %collective-permute-start.5 = (f32[640,128]{1,0:T(8,128)}, f32[640,128]{1,0:T(8,128)S(1)}, u32[]{:S(2)}, u32[]{:S(2)}) collective-permute-start(f32[640,128]{1,0:T(8,128)} %get-tuple-element.22.refs_0_), channel_id=1, source_target_pairs={{0,2},{1,3},{2,0},{3,1},{4,6},{5,7},{6,4},{7,5},{8,10},{9,11},{10,... | collective-permute-start | bytes 983048 | tf_op jit(solution)/shard_map/ppermute | solution.py:25
  9.9 17.8 %collective-permute-start.4 = (f32[640,128]{1,0:T(8,128)}, f32[640,128]{1,0:T(8,128)S(1)}, u32[]{:S(2)}, u32[]{:S(2)}) collective-permute-start(f32[640,128]{1,0:T(8,128)} %get-tuple-element.22.refs_0_), channel_id=1, source_target_pairs={{0,4},{1,5},{2,6},{3,7},{4,0},{5,1},{6,2},{7,3},{8,12},{9,13},{10,... | collective-permute-start | bytes 983048 | tf_op jit(solution)/shard_map/ppermute | solution.py:25
  12.0 18.3 %collective-permute-start.3 = (f32[640,128]{1,0:T(8,128)}, f32[640,128]{1,0:T(8,128)S(1)}, u32[]{:S(2)}, u32[]{:S(2)}) collective-permute-start(f32[640,128]{1,0:T(8,128)} %get-tuple-element.22.refs_0_), channel_id=1, source_target_pairs={{0,16},{1,17},{2,18},{3,19},{4,20},{5,21},{6,22},{7,23},{8,24},{9,... | collective-permute-start | bytes 983048 | tf_op jit(solution)/shard_map/ppermute | solution.py:25
  14.6 16.0 %copy-start.1 = (f32[640,128]{1,0:T(8,128)S(1)}, f32[640,128]{1,0:T(8,128)}, u32[]{:S(2)}) copy-start(f32[640,128]{1,0:T(8,128)} %get-tuple-element.22.refs_0_) | copy-start | bytes 983044
  14.6 16.0 %copy-start.3 = (f32[152,152]{1,0:T(8,128)S(1)}, f32[152,152]{1,0:T(8,128)}, u32[]{:S(2)}) copy-start(f32[152,152]{1,0:T(8,128)} %dc2e_ref.1) | copy-start | bytes 277252
  14.6 16.0 %copy-start.9 = (bf16[160,4096]{1,0:T(8,128)(2,1)S(1)}, bf16[160,4096]{1,0:T(8,128)(2,1)}, u32[]{:S(2)}) copy-start(bf16[160,4096]{1,0:T(8,128)(2,1)} %get-tuple-element.14.tile_hi_ref) | copy-start | bytes 3932164
  14.7 16.0 %copy-start.10 = (bf16[160,4096]{1,0:T(8,128)(2,1)S(1)}, bf16[160,4096]{1,0:T(8,128)(2,1)}, u32[]{:S(2)}) copy-start(bf16[160,4096]{1,0:T(8,128)(2,1)} %get-tuple-element.15.tile_lo_ref) | copy-start | bytes 3932164
  14.7 16.0 %collective-permute-start.2 = (f32[640,128]{1,0:T(8,128)}, f32[640,128]{1,0:T(8,128)S(1)}, u32[]{:S(2)}, u32[]{:S(2)}) collective-permute-start(f32[640,128]{1,0:T(8,128)} %get-tuple-element.22.refs_0_), channel_id=1, source_target_pairs={{0,8},{1,9},{2,10},{3,11},{4,12},{5,13},{6,14},{7,15},{8,0},{9,1},... | collective-permute-start | bytes 983048 | tf_op jit(solution)/shard_map/ppermute | solution.py:25

commit v5 on v4

--- a/solution.py
+++ b/solution.py
@@ -38,6 +38,17 @@
     for digit in range(10):
         summed = summed + (((leaf >> (3 * digit + axis)) & 1) << digit)
     return summed.astype(jnp.float32)
+
+
+def corners(first, local):
+    base = [corner_of(first, axis) for axis in range(3)]
+
+    def at(h, axis):
+        if local & (local - 1):
+            return corner_of(first + h, axis)
+        return base[axis] + float(sum(((h >> (3 * digit + axis)) & 1) << digit for digit in range(10)))
+
+    return at
 
 
 def prepare(m2l_ref, vsrc_ref, vtype_ref, w_hi_ref, w_lo_ref, twice_ref, code_ref, tally_ref):
@@ -117,7 +128,7 @@
 
 
 def near_kernel(first_ref, counts_ref, offsets_ref, charges_ref, pair_ref, odd_ref, ulist_ref, m2l_ref, vsrc_ref, vtype_ref,
-                out_ref, w_hi_ref, w_lo_ref, twice_ref, code_ref, tally_ref, ghost_ref,
+                surface_ref, out_ref, w_hi_ref, w_lo_ref, twice_ref, tile_hi_ref, tile_lo_ref, code_ref, tally_ref, ghost_ref,
                 lanes_ref, chg_ref, src_ref, tgt_ref, square_ref, hi_ref, lo_ref, acc_ref,
                 mult_ref, res_ref, start_ref, leaf_ref, from_ref, to_ref, open_ref, shut_ref):
     f32, bf16, i32 = jnp.float32, jnp.bfloat16, jnp.int32
@@ -128,13 +139,8 @@
     lane = lax.broadcasted_iota(i32, (1, PTS), 1)
 
     first = first_ref[0]
-    centre = []
-    for axis in range(3):
-        low = high = jnp.int32(0)
-        for digit in range(10):
-            low = low + (((first >> (3 * digit + axis)) & 1) << digit)
-            high = high + ((((first + local - 1) >> (3 * digit + axis)) & 1) << digit)
-        centre.append((low + high + 1).astype(f32) * 0.5)
+    corner_at = corners(first, local)
+    centre = [(corner_at(0, axis) + corner_at(local - 1, axis) + 1.0) * 0.5 for axis in range(3)]
     sub = lax.broadcasted_iota(i32, (8, PTS), 0)
     shift_by = jnp.where(sub == 0, centre[0], jnp.where(sub == 1, centre[1], jnp.where(sub == 2, centre[2], 0.0)))
 
@@ -190,7 +196,7 @@
         elif e < GHOST + local:
             h = e - GHOST
             at = slice(h * PTS, (h + 1) * PTS)
-            corner = [corner_of(first + h, axis) for axis in range(3)]
+            corner = [corner_at(h, axis) for axis in range(3)]
             move = jnp.where(sub == 0, corner[0], jnp.where(sub == 1, corner[1], corner[2]))
             xyz = jnp.concatenate([offsets_ref[:, at], jnp.zeros((5, PTS), f32)], 0)
             block = jnp.concatenate([xyz + move, jnp.where(lane < counts_ref[h], charges_ref[:, at], 0.0)], 0)
@@ -327,6 +333,20 @@
     lax.fori_loop(0, (steps + SIDE - 1) // SIDE, several, tuple(order))
     res_ref[...] = acc_ref[0:probes] + acc_ref[probes:2 * probes] + acc_ref[2 * probes:]
 
+    def tile(i, _):
+        for half in range(2):
+            at = pl.ds(pl.multiple_of((2 * i + half) * PTS, PTS), PTS)
+            x = offsets_ref[:, at] - 0.5
+            norm = x[0:1] * x[0:1] + (x[1:2] * x[1:2] + x[2:3] * x[2:3])
+            for r in range(0, tile_hi_ref.shape[0], 16):
+                rows = slice(r, r + 16)
+                s = (surface_ref[3, rows, :] + norm) + surface_ref[0, rows, :] * x[0:1]
+                s = s + (surface_ref[1, rows, :] * x[1:2] + surface_ref[2, rows, :] * x[2:3])
+                tile_hi_ref[rows, at], tile_lo_ref[rows, at] = split(lax.rsqrt(s))
+        return 0
+
+    lax.fori_loop(0, local // 2, tile, 0, unroll=2)
+
     for g in range(local):
         at = starts[g + GHOST] - base
         shift = at & (PTS - 1)
@@ -342,6 +362,8 @@
     local = counts.shape[0]
     probes = charges.shape[0]
     kinds = m2l.shape[1] // m2l.shape[0]
+    spread = np.ascontiguousarray(np.broadcast_to(surface_rows().T[:4, :, None], (4, surface_rows().shape[0], PTS)))
+    grown = -(-m2l.shape[0] // 16) * 16
     every = local + 2 * GHOST
     width = every * PTS + 8 * PTS + 512
     targets = local * PTS + 512
@@ -351,12 +373,14 @@
         near_kernel,
         out_shape=(
             jax.ShapeDtypeStruct((probes, local * PTS), jnp.float32),
-            jax.ShapeDtypeStruct((2 * PTS, kinds * (PTS + 32)), jnp.bfloat16),
-            jax.ShapeDtypeStruct((2 * PTS, kinds * (PTS + 32)), jnp.bfloat16),
+            jax.ShapeDtypeStruct((grown, kinds * (PTS + 32)), jnp.bfloat16),
+            jax.ShapeDtypeStruct((grown, kinds * (PTS + 32)), jnp.bfloat16),
             jax.ShapeDtypeStruct((kinds * local, 2 * depth), jnp.bfloat16),
+            jax.ShapeDtypeStruct((spread.shape[1], local * PTS), jnp.bfloat16),
+            jax.ShapeDtypeStruct((spread.shape[1], local * PTS), jnp.bfloat16),
         ),
-        in_specs=[smem, smem] + [vmem] * 8,
-        out_specs=(vmem,) * 4,
+        in_specs=[smem, smem] + [vmem] * 9,
+        out_specs=(vmem,) * 6,
         scratch_shapes=[
             pltpu.VMEM((2 * local, PTS), jnp.float32),
             pltpu.VMEM((kinds * local, 2 * depth), jnp.float32),
@@ -381,7 +405,7 @@
         compiler_params=pltpu.CompilerParams(vmem_limit_bytes=24 << 20),
         cost_estimate=pl.CostEstimate(flops=4_000_000_000, bytes_accessed=2_000_000, transcendentals=4_000_000),
         name="near",
-    )(first, counts, offsets, charges, pair, odd, u_list, m2l, v_src, v_type)
+    )(first, counts, offsets, charges, pair, odd, u_list, m2l, v_src, v_type, jnp.asarray(spread))
 
 
 def split(value):
@@ -430,8 +454,7 @@
 
 
 def up_kernel(first_ref, counts_hbm, offsets_hbm, charges_hbm, uc2e_hbm, surface_hbm,
-              odd_ref, pair_ref, up_ref, tile_hi_hbm, tile_lo_hbm,
-              tile_hi_ref, tile_lo_ref, counts_ref, offsets_ref, charges_ref, uc2e_ref, surface_ref, check_ref, sems):
+              odd_ref, pair_ref, up_ref, counts_ref, offsets_ref, charges_ref, uc2e_ref, surface_ref, check_ref, sems):
     f32, i32 = jnp.float32, jnp.int32
     copies = []
     for n, (source, target) in enumerate(((counts_hbm, counts_ref), (offsets_hbm, offsets_ref),
@@ -449,7 +472,6 @@
         copy.wait()
     surface = surface_ref[...]
 
-    leaving = []
     for g in range(0, local, 2):
         parts = []
         for h in (g, g + 1):
@@ -457,8 +479,6 @@
             parts.append(split(jnp.where(lane < counts_ref[h], charges_ref[:, at], 0.0)))
         both = slice(g * PTS, (g + 2) * PTS)
         tile_hi, tile_lo = split(surface_tile(offsets_ref[:, both] - 0.5, surface))
-        tile_hi_ref[:, both] = tile_hi
-        tile_lo_ref[:, both] = tile_lo
         left = jnp.concatenate([parts[0][0], zero], 1), jnp.concatenate([zero, parts[1][0]], 1)
         small = jnp.concatenate([parts[0][1], zero], 1), jnp.concatenate([zero, parts[1][1]], 1)
         large = dot_t(jnp.concatenate(left + small, 0), tile_hi)
@@ -470,20 +490,17 @@
             at = slice(half * PTS, (half + 1) * PTS)
             check_ref[half, pl.ds(g, probes, stride=local), :] = value[:probes, at]
             check_ref[half, pl.ds(g + 1, probes, stride=local), :] = value[probes:, at]
-        if (g + 2) % 8 == 0:
-            done = slice((g - 6) * PTS, (g + 2) * PTS)
-            for source, target in ((tile_hi_ref, tile_hi_hbm), (tile_lo_ref, tile_lo_hbm)):
-                leaving.append(pltpu.make_async_copy(source.at[:, done], target.at[:, done], sems.at[5]))
-                leaving[-1].start()
 
     rows = probes * local
     even = lax.rem(lax.div(first, local), 2) == 0
+    corner_at = corners(first, local)
     deep = 8 + probes
     for e in range(GHOST):
-        leaf = jnp.where(even, e, local - GHOST + e), jnp.where(even, local - GHOST + e, e)
-        for h, ref, skip in ((leaf[0], odd_ref, 0), (leaf[1], pair_ref, rows * 5 // 4)):
+        ends = e, local - GHOST + e
+        for ids, ref, skip in ((ends, odd_ref, 0), (ends[::-1], pair_ref, rows * 5 // 4)):
+            h = jnp.where(even, *ids)
             at = pl.multiple_of(h * PTS, PTS)
-            corner = [corner_of(first + h, axis) for axis in range(3)]
+            corner = [jnp.where(even, corner_at(ids[0], axis), corner_at(ids[1], axis)) for axis in range(3)]
             held = counts_ref[h]
             xyz = jnp.concatenate([offsets_ref[:, pl.ds(at, PTS)], jnp.zeros((5, PTS), f32)], 0)
             move = jnp.where(sub == 0, corner[0], jnp.where(sub == 1, corner[1], jnp.where(sub == 2, corner[2],
@@ -500,17 +517,15 @@
     for target in (up_ref, pair_ref):
         target[:rows] = up[:, :PTS]
         target[rows:rows + rest] = tail
-    for copy in leaving:
-        copy.wait()
 
 
 def up_call(first, counts, offsets, charges, uc2e):
     local = counts.shape[0]
-    probes, points = charges.shape
+    probes = charges.shape[0]
     smem = pl.BlockSpec(memory_space=pltpu.SMEM)
     vmem = pl.BlockSpec(memory_space=pltpu.VMEM)
     hbm = pl.BlockSpec(memory_space=pltpu.HBM)
-    f32, bf16 = jnp.float32, jnp.bfloat16
+    f32 = jnp.float32
     surface = surface_rows()
     sent = probes * local * 5 // 4
     ghost = GHOST * (8 + probes)
@@ -520,21 +535,17 @@
             jax.ShapeDtypeStruct((ghost, PTS), f32),
             jax.ShapeDtypeStruct((sent + ghost, PTS), f32),
             jax.ShapeDtypeStruct((sent, PTS), f32),
-            jax.ShapeDtypeStruct((surface.shape[0], points), bf16),
-            jax.ShapeDtypeStruct((surface.shape[0], points), bf16),
         ),
         in_specs=[smem, hbm, hbm, hbm, hbm, hbm],
-        out_specs=(vmem, vmem, vmem, hbm, hbm),
+        out_specs=(vmem,) * 3,
         scratch_shapes=[
-            pltpu.VMEM((surface.shape[0], points), bf16),
-            pltpu.VMEM((surface.shape[0], points), bf16),
             pltpu.SMEM(counts.shape, jnp.int32),
             pltpu.VMEM(offsets.shape, f32),
             pltpu.VMEM(charges.shape, f32),
             pltpu.VMEM(uc2e.shape, f32),
             pltpu.VMEM(surface.shape, f32),
             pltpu.VMEM((2, probes * local, PTS), f32),
-            pltpu.SemaphoreType.DMA((6,)),
+            pltpu.SemaphoreType.DMA((5,)),
         ],
         compiler_params=pltpu.CompilerParams(vmem_limit_bytes=60 << 20),
         cost_estimate=pl.CostEstimate(flops=500_000_000, bytes_accessed=1_500_000, transcendentals=600_000),
@@ -550,9 +561,9 @@
 def far_kernel(counts_ref, wanted_ref, tile_hi_ref, tile_lo_ref, near_ref, w_hi_ref, w_lo_ref, twice_ref, dc2e_ref,
                *refs):
     f32, bf16, i32 = jnp.float32, jnp.bfloat16, jnp.int32
-    sent = refs[:-6]
+    sent = refs[:-7]
     pieces = [sent[i] for i in np.argsort(send_order(len(sent)))]
-    out_ref, pick_ref, table_ref, x_hi_ref, x_lo_ref, eq_ref = refs[-6:]
+    out_ref, pick_ref, table_ref, x_hi_ref, x_lo_ref, eq_ref, down_ref = refs[-7:]
     probes, points = out_ref.shape
     local = points // PTS
     bits, cap = wanted_ref.shape
@@ -610,14 +621,18 @@
         x_hi, x_lo, w_hi, w_lo = x_hi_ref[:, at], x_lo_ref[:, at], w_hi_ref[:, at], w_lo_ref[:, at]
         return dot_t(jnp.concatenate([x_hi, x_hi, x_lo], 1), jnp.concatenate([w_hi, w_lo, w_hi], 1))
 
-    down = None
-    for c in range(kinds // 4):
-        value = down_part(slice(4 * c * PTS, 4 * (c + 1) * PTS))
-        down = value if down is None else down + value
-        for q in range(c, quarter, kinds // 4):
-            spread_rest(dot(twice, table_ref[:, (probes + q) * PTS:(probes + q + 1) * PTS]), q)
-    down = down + down_part(slice(kinds * PTS, kinds * (PTS + 32)))
-    equivs = dot_t3(down, padded(dc2e_ref, 2 * PTS, 2 * PTS))
+    for q in range(quarter):
+        spread_rest(dot(twice, table_ref[:, (probes + q) * PTS:(probes + q + 1) * PTS]), q)
+
+    def add_part(i, _):
+        down_ref[...] += down_part(pl.ds(pl.multiple_of(i * cut, PTS), cut))
+        return 0
+
+    cut = kinds * (PTS + 32) // 2
+    down_ref[...] = jnp.zeros_like(down_ref)
+    lax.fori_loop(0, 2, add_part, 0)
+    down = down_ref[...]
+    equivs = dot_t3(down, padded(dc2e_ref, 2 * PTS, down.shape[1]))
     eq_ref[0], eq_ref[1] = equivs[:, :PTS], equivs[:, PTS:]
 
     reach = tile_hi_ref.shape[0]
@@ -659,6 +674,7 @@
             pltpu.VMEM((rows, wide), bf16),
             pltpu.VMEM((rows, wide), bf16),
             pltpu.VMEM((2, rows, PTS), f32),
+            pltpu.VMEM((rows, w_hi.shape[0]), f32),
         ],
         compiler_params=pltpu.CompilerParams(vmem_limit_bytes=32 << 20),
         cost_estimate=pl.CostEstimate(flops=4_000_000_000, bytes_accessed=4_000_000, transcendentals=600_000),
@@ -669,15 +685,15 @@
 def shards(offsets, charges, counts, u_list, v_src, v_type, wanted, m2l, uc2e, dc2e):
     local_leaves = counts.shape[0]
     first = (lax.axis_index("cube") * local_leaves).astype(jnp.int32).reshape(1)
-    odd, pair, up, tile_hi, tile_lo = up_call(first, counts, offsets, charges, uc2e)
+    odd, pair, up = up_call(first, counts, offsets, charges, uc2e)
     count = lax.axis_size("cube")
     odd = lax.ppermute(odd, "cube", [(i, i + 1 if i % 2 else i - 1) for i in range(1, count - 1)])
     pieces = [from_partner(up, "cube", bit) for bit in range(count.bit_length() - 2, 0, -1)]
     pair = from_partner(pair, "cube", 0)
     pieces = [pair] + pieces[::-1] + [up]
     depth = wanted.shape[1] * wanted.shape[2] + counts.shape[0]
-    near, w_hi, w_lo, twice = near_call(first, counts, offsets, charges, pair, odd, u_list, m2l, v_src, v_type, depth)
-    return far_call(counts, wanted[0], (tile_hi, tile_lo), near, w_hi, w_lo, twice, dc2e, pieces)
+    near, w_hi, w_lo, twice, *tiles = near_call(first, counts, offsets, charges, pair, odd, u_list, m2l, v_src, v_type, depth)
+    return far_call(counts, wanted[0], tiles, near, w_hi, w_lo, twice, dc2e, pieces)
 
 
 def solution(mesh):

time: 38.7 us -> 37.9 us (0.979)
  waiting for transfers between devices: 2.96 us -> 0.02 us
  Pallas kernels: 24 us -> 25.2 us
  local copies, waits for them, and re-layouts: 0.05 us -> 1.01 us
    ppermute x5, waiting for transfers between devices: 2.96 us -> 0.01 us  [from_partner(): lax.ppermute(array, axis, [(i, i ^ 1 << bit) for i in range(lax.axis_size...]
    pallas_call x1, Pallas kernels: 11.3 us -> 13.4 us  [near_call(): pl.pallas_call(near_kernel, out_shape=(jax.ShapeDtypeStruct((probes, loca...]
    unnamed x25 -> x23, local copies, waits for them, and re-layouts: 0.05 us -> 1.01 us
    pallas_call x1, Pallas kernels: 4.83 us -> 4.15 us  [up_call(): pl.pallas_call(up_kernel, out_shape=(jax.ShapeDtypeStruct((ghost, PTS), f...]
  transfers between devices with their start and end apart: 6 -> 6, of which waited for: 2 -> 0; matrix products, arithmetic and copies ran while one was open for 0% -> 0% of each run, Pallas kernels for 29% -> 35%
where the time goes in v5:
time: 37.9 us; the launch traced here: 37.8 us
  Pallas kernels  25.2 us (66%)
  starting transfers between devices  11.4 us (30%)
  local copies, waits for them, and re-layouts  1.01 us (3%)
    pallas_call x1, Pallas kernels, near_call(): pl.pallas_call(near_kernel, out_shape=(jax.ShapeDtypeStruct((probes, loca...  13.4 us
    ppermute x5, starting transfers between devices, from_partner(): lax.ppermute(array, axis, [(i, i ^ 1 << bit) for i in range(lax.axis_size...  10.7 us
    pallas_call x1, Pallas kernels, far_call(): pl.pallas_call(far_kernel, out_shape=jax.ShapeDtypeStruct((probes, points...  7.63 us
    pallas_call x1, Pallas kernels, up_call(): pl.pallas_call(up_kernel, out_shape=(jax.ShapeDtypeStruct((ghost, PTS), f...  4.15 us
    unnamed x23, local copies, waits for them, and re-layouts  1.01 us
  transfers between devices with their start and end apart: 6, of which 0 were waited for; matrix products, arithmetic and copies ran while one was open for 0% of the time, Pallas kernels for 35%

profile of v5, /device:TPU:0, one launch (start us, length us, event | category | flops | bytes accessed | tf_op | source)
XLA Modules:
  0.0 37.8 jit_solution(3970571627291244154)
XLA Ops:
  0.0 0.0 copy-start.8
  0.0 0.0 copy-start.2
  0.0 0.0 copy-start.7
  0.0 0.0 copy-start.6
  0.0 0.0 copy-start.5
  0.0 4.2 %upward.1 = (f32[192,128]{1,0:T(8,128)}, f32[832,128]{1,0:T(8,128)}, f32[640,128]{1,0:T(8,128)}) custom-call(s32[1]{0:T(128)} %bitcast.first_ref, s32[32]{0:T(128)} %counts_ref.3, f32[3,4096]{1,0:T(4,128)} %offsets_ref.1, f32[16,4096]{1,0:T(8,128)} %charges_ref.1, f32[152,152]{1,0:T(8,128)} %uc2e_hbm.1, f32[160,8]{1,0:T(8,128)} %constant.10.clone.surface_hbm), custom_call_target="tpu_custom_call" | custom-call | flops 500000000 | bytes 1500000 | tf_op jit(solution)/shard_map/upward/pallas_call | solution.py:532
  4.2 0.5 %collective-permute-start = (f32[832,128]{1,0:T(8,128)}, f32[832,128]{1,0:T(8,128)S(1)}, u32[]{:S(2)}, u32[]{:S(2)}) collective-permute-start(f32[832,128]{1,0:T(8,128)} %get-tuple-element.14), channel_id=1, source_target_pairs={{0,1},{1,0},{2,3},{3,2},{4,5},{5,4},{6,7},{7,6},{8,9},{9,8},{10,11... | collective-permute-start | bytes 1277960 | tf_op jit(solution)/shard_map/ppermute | solution.py:25
  4.7 0.7 %collective-permute-start.1 = (f32[192,128]{1,0:T(8,128)}, f32[192,128]{1,0:T(8,128)S(1)}, u32[]{:S(2)}, u32[]{:S(2)}) collective-permute-start(f32[192,128]{1,0:T(8,128)} %get-tuple-element.15), channel_id=1, source_target_pairs={{1,2},{2,1},{3,4},{4,3},{5,6},{6,5},{7,8},{8,7},{9,10},{10,9},{11,... | collective-permute-start | bytes 294920 | tf_op jit(solution)/shard_map/ppermute | solution.py:690
  5.4 3.8 %collective-permute-start.5 = (f32[640,128]{1,0:T(8,128)}, f32[640,128]{1,0:T(8,128)S(1)}, u32[]{:S(2)}, u32[]{:S(2)}) collective-permute-start(f32[640,128]{1,0:T(8,128)} %get-tuple-element.22.refs_0_), channel_id=1, source_target_pairs={{0,2},{1,3},{2,0},{3,1},{4,6},{5,7},{6,4},{7,5},{8,10},{9,11},{10,... | collective-permute-start | bytes 983048 | tf_op jit(solution)/shard_map/ppermute | solution.py:25
  9.2 2.1 %collective-permute-start.4 = (f32[640,128]{1,0:T(8,128)}, f32[640,128]{1,0:T(8,128)S(1)}, u32[]{:S(2)}, u32[]{:S(2)}) collective-permute-start(f32[640,128]{1,0:T(8,128)} %get-tuple-element.22.refs_0_), channel_id=1, source_target_pairs={{0,4},{1,5},{2,6},{3,7},{4,0},{5,1},{6,2},{7,3},{8,12},{9,13},{10,... | collective-permute-start | bytes 983048 | tf_op jit(solution)/shard_map/ppermute | solution.py:25
  11.4 2.6 %collective-permute-start.3 = (f32[640,128]{1,0:T(8,128)}, f32[640,128]{1,0:T(8,128)S(1)}, u32[]{:S(2)}, u32[]{:S(2)}) collective-permute-start(f32[640,128]{1,0:T(8,128)} %get-tuple-element.22.refs_0_), channel_id=1, source_target_pairs={{0,16},{1,17},{2,18},{3,19},{4,20},{5,21},{6,22},{7,23},{8,24},{9,... | collective-permute-start | bytes 983048 | tf_op jit(solution)/shard_map/ppermute | solution.py:25
  14.0 0.0 copy-done.10
  14.0 0.0 collective-permute-done.1.odd_ref
  14.0 1.6 %collective-permute-start.2 = (f32[640,128]{1,0:T(8,128)}, f32[640,128]{1,0:T(8,128)S(1)}, u32[]{:S(2)}, u32[]{:S(2)}) collective-permute-start(f32[640,128]{1,0:T(8,128)} %get-tuple-element.22.refs_0_), channel_id=1, source_target_pairs={{0,8},{1,9},{2,10},{3,11},{4,12},{5,13},{6,14},{7,15},{8,0},{9,1},... | collective-permute-start | bytes 983048 | tf_op jit(solution)/shard_map/ppermute | solution.py:25
  15.6 0.0 collective-permute-done.pair_ref.refs_5_
  15.6 0.0 copy-done.8
  15.6 0.0 copy-done.2
  15.6 0.0 copy-done.4
  15.6 0.0 copy-done
  15.7 0.0 copy-done.7
  15.7 0.0 copy-done.6
  15.7 0.0 copy-done.5
  15.7 0.0 copy-start.9
  15.7 1.0 %copy-done.9 = f32[4,160,128]{2,1,0:T(8,128)S(1)} copy-done((f32[4,160,128]{2,1,0:T(8,128)S(1)}, f32[4,160,128]{2,1,0:T(8,128)}, u32[]{:S(2)}) %copy-start.9) | copy-done | bytes 327704
  16.7 13.4 %near.1 = (f32[16,4096]{1,0:T(8,128)S(1)}, bf16[160,2560]{1,0:T(8,128)(2,1)S(1)}, bf16[160,2560]{1,0:T(8,128)(2,1)S(1)}, bf16[512,224]{1,0:T(8,128)(2,1)S(1)}, b...) custom-call(s32[1]{0:T(128)} %bitcast.first_ref, s32[32]{0:T(128)S(1)} %copy-done.8, f32[3,4096]{1,0:T(4,128)S(1)} %copy-done.4, ...), custom_call_target="tpu_custom_call" | custom-call | flops 4000000000 | bytes 2000000 | tf_op jit(solution)/shard_map/near/pallas_call | solution.py:372
  30.1 0.0 collective-permute-done.5.refs_4_
  30.1 0.0 collective-permute-done.4.refs_3_
  30.1 0.0 collective-permute-done.3.refs_2_
  30.1 0.0 collective-permute-done.2.refs_1_
  30.1 0.0 copy-done.1
  30.1 0.0 copy-done.3
  30.1 7.6 %far.1 = f32[16,4096]{1,0:T(8,128)} custom-call(s32[32]{0:T(128)S(1)} %copy-done.8, s32[5,16]{1,0:T(8,128)S(1)} %bitcast.4, bf16[160,4096]{1,0:T(8,128)(2,1)S(1)} %get-tuple-element.16.tile_hi_ref, bf16[160,4096]{1,0:T(8,128)(2,1)S(1)} %get-tuple-element.17.tile_lo_ref, f32[16,4096]{1,0:T(8,128)S(1)} %get-tuple-element.18.near_ref, ...), custom_call_target="tpu_custom_call" | custom-call | flops 4000000000 | bytes 4000000 | tf_op jit(solution)/shard_map/far/pallas_call | solution.py:666
  (6 shorter events, 0.0 us)
Async XLA Ops:
  0.0 15.6 %copy-start.8 = (s32[32]{0:T(128)S(1)}, s32[32]{0:T(128)}, u32[]{:S(2)}) copy-start(s32[32]{0:T(128)} %counts_ref.3) | copy-start | bytes 388
  0.0 15.6 %copy-start.2 = (f32[16,4096]{1,0:T(8,128)S(1)}, f32[16,4096]{1,0:T(8,128)}, u32[]{:S(2)}) copy-start(f32[16,4096]{1,0:T(8,128)} %charges_ref.1) | copy-start | bytes 786436
  0.0 15.6 %copy-start.4 = (f32[3,4096]{1,0:T(4,128)S(1)}, f32[3,4096]{1,0:T(4,128)}, u32[]{:S(2)}) copy-start(f32[3,4096]{1,0:T(4,128)} %offsets_ref.1) | copy-start | bytes 147460
  0.0 14.0 %copy-start.10 = (s32[1,5,16]{2,0,1:T(1,128)S(1)}, s32[1,5,16]{2,0,1:T(1,128)}, u32[]{:S(2)}) copy-start(s32[1,5,16]{2,0,1:T(1,128)} %param.18) | copy-start | bytes 964
  0.0 15.6 %copy-start = (f32[152,2432]{1,0:T(8,128)S(1)}, f32[152,2432]{1,0:T(8,128)}, u32[]{:S(2)}) copy-start(f32[152,2432]{1,0:T(8,128)} %m2l_ref.1) | copy-start | bytes 4435972
  0.0 15.6 %copy-start.7 = (s32[32,32]{1,0:T(8,128)S(1)}, s32[32,32]{1,0:T(8,128)}, u32[]{:S(2)}) copy-start(s32[32,32]{1,0:T(8,128)} %vtype_ref.1) | copy-start | bytes 12292
  0.0 15.6 %copy-start.6 = (s32[32,32]{1,0:T(8,128)S(1)}, s32[32,32]{1,0:T(8,128)}, u32[]{:S(2)}) copy-start(s32[32,32]{1,0:T(8,128)} %vsrc_ref.1) | copy-start | bytes 12292
  0.0 15.6 %copy-start.5 = (s32[32,27]{1,0:T(8,128)S(1)}, s32[32,27]{1,0:T(8,128)}, u32[]{:S(2)}) copy-start(s32[32,27]{1,0:T(8,128)} %ulist_ref.1) | copy-start | bytes 10372
  4.2 11.4 %collective-permute-start = (f32[832,128]{1,0:T(8,128)}, f32[832,128]{1,0:T(8,128)S(1)}, u32[]{:S(2)}, u32[]{:S(2)}) collective-permute-start(f32[832,128]{1,0:T(8,128)} %get-tuple-element.14), channel_id=1, source_target_pairs={{0,1},{1,0},{2,3},{3,2},{4,5},{5,4},{6,7},{7,6},{8,9},{9,8},{10,11... | collective-permute-start | bytes 1277960 | tf_op jit(solution)/shard_map/ppermute | solution.py:25
  4.7 9.2 %collective-permute-start.1 = (f32[192,128]{1,0:T(8,128)}, f32[192,128]{1,0:T(8,128)S(1)}, u32[]{:S(2)}, u32[]{:S(2)}) collective-permute-start(f32[192,128]{1,0:T(8,128)} %get-tuple-element.15), channel_id=1, source_target_pairs={{1,2},{2,1},{3,4},{4,3},{5,6},{6,5},{7,8},{8,7},{9,10},{10,9},{11,... | collective-permute-start | bytes 294920 | tf_op jit(solution)/shard_map/ppermute | solution.py:690
  5.4 24.7 %collective-permute-start.5 = (f32[640,128]{1,0:T(8,128)}, f32[640,128]{1,0:T(8,128)S(1)}, u32[]{:S(2)}, u32[]{:S(2)}) collective-permute-start(f32[640,128]{1,0:T(8,128)} %get-tuple-element.22.refs_0_), channel_id=1, source_target_pairs={{0,2},{1,3},{2,0},{3,1},{4,6},{5,7},{6,4},{7,5},{8,10},{9,11},{10,... | collective-permute-start | bytes 983048 | tf_op jit(solution)/shard_map/ppermute | solution.py:25
  9.2 20.9 %collective-permute-start.4 = (f32[640,128]{1,0:T(8,128)}, f32[640,128]{1,0:T(8,128)S(1)}, u32[]{:S(2)}, u32[]{:S(2)}) collective-permute-start(f32[640,128]{1,0:T(8,128)} %get-tuple-element.22.refs_0_), channel_id=1, source_target_pairs={{0,4},{1,5},{2,6},{3,7},{4,0},{5,1},{6,2},{7,3},{8,12},{9,13},{10,... | collective-permute-start | bytes 983048 | tf_op jit(solution)/shard_map/ppermute | solution.py:25
  11.4 18.7 %collective-permute-start.3 = (f32[640,128]{1,0:T(8,128)}, f32[640,128]{1,0:T(8,128)S(1)}, u32[]{:S(2)}, u32[]{:S(2)}) collective-permute-start(f32[640,128]{1,0:T(8,128)} %get-tuple-element.22.refs_0_), channel_id=1, source_target_pairs={{0,16},{1,17},{2,18},{3,19},{4,20},{5,21},{6,22},{7,23},{8,24},{9,... | collective-permute-start | bytes 983048 | tf_op jit(solution)/shard_map/ppermute | solution.py:25
  14.0 16.2 %copy-start.1 = (f32[640,128]{1,0:T(8,128)S(1)}, f32[640,128]{1,0:T(8,128)}, u32[]{:S(2)}) copy-start(f32[640,128]{1,0:T(8,128)} %get-tuple-element.22.refs_0_) | copy-start | bytes 983044
  14.0 16.2 %copy-start.3 = (f32[152,152]{1,0:T(8,128)S(1)}, f32[152,152]{1,0:T(8,128)}, u32[]{:S(2)}) copy-start(f32[152,152]{1,0:T(8,128)} %dc2e_ref.1) | copy-start | bytes 277252
  14.0 16.1 %collective-permute-start.2 = (f32[640,128]{1,0:T(8,128)}, f32[640,128]{1,0:T(8,128)S(1)}, u32[]{:S(2)}, u32[]{:S(2)}) collective-permute-start(f32[640,128]{1,0:T(8,128)} %get-tuple-element.22.refs_0_), channel_id=1, source_target_pairs={{0,8},{1,9},{2,10},{3,11},{4,12},{5,13},{6,14},{7,15},{8,0},{9,1},... | collective-permute-start | bytes 983048 | tf_op jit(solution)/shard_map/ppermute | solution.py:25
  15.7 1.0 %copy-start.9 = (f32[4,160,128]{2,1,0:T(8,128)S(1)}, f32[4,160,128]{2,1,0:T(8,128)}, u32[]{:S(2)}) copy-start(f32[4,160,128]{2,1,0:T(8,128)} %constant.11.clone.surface_ref) | copy-start | bytes 983044

commit v6 on v5

--- a/solution.py
+++ b/solution.py
@@ -345,7 +345,7 @@
                 tile_hi_ref[rows, at], tile_lo_ref[rows, at] = split(lax.rsqrt(s))
         return 0
 
-    lax.fori_loop(0, local // 2, tile, 0, unroll=2)
+    lax.fori_loop(0, local // 2, tile, 0, unroll=True)
 
     for g in range(local):
         at = starts[g + GHOST] - base

time: 37.9 us -> 37.8 us (level)
  Pallas kernels: 25.2 us -> 22.7 us
  waiting for transfers between devices: 0.02 us -> 2.3 us
    pallas_call x1, Pallas kernels: 13.4 us -> 11 us  [near_call(): pl.pallas_call(near_kernel, out_shape=(jax.ShapeDtypeStruct((probes, loca...]
    ppermute x5, waiting for transfers between devices: 0.01 us -> 2.29 us  [from_partner(): lax.ppermute(array, axis, [(i, i ^ 1 << bit) for i in range(lax.axis_size...]
  transfers between devices with their start and end apart: 6 -> 6, of which waited for: 0 -> 2; matrix products, arithmetic and copies ran while one was open for 0% -> 0% of each run, Pallas kernels for 35% -> 29%
where the time goes in v6:
time: 37.8 us; the launch traced here: 37.6 us
  Pallas kernels  22.7 us (60%)
  starting transfers between devices  11.4 us (30%)
  waiting for transfers between devices  2.3 us (6%)
  local copies, waits for them, and re-layouts  1.01 us (3%)
    pallas_call x1, Pallas kernels, near_call(): pl.pallas_call(near_kernel, out_shape=(jax.ShapeDtypeStruct((probes, loca...  11 us
    ppermute x5, starting transfers between devices, from_partner(): lax.ppermute(array, axis, [(i, i ^ 1 << bit) for i in range(lax.axis_size...  10.7 us
    pallas_call x1, Pallas kernels, far_call(): pl.pallas_call(far_kernel, out_shape=jax.ShapeDtypeStruct((probes, points...  7.63 us
    pallas_call x1, Pallas kernels, up_call(): pl.pallas_call(up_kernel, out_shape=(jax.ShapeDtypeStruct((ghost, PTS), f...  4.15 us
    ppermute x5, waiting for transfers between devices, from_partner(): lax.ppermute(array, axis, [(i, i ^ 1 << bit) for i in range(lax.axis_size...  2.29 us
    unnamed x23, local copies, waits for them, and re-layouts  1.01 us
  transfers between devices with their start and end apart: 6, of which 2 were waited for; matrix products, arithmetic and copies ran while one was open for 0% of the time, Pallas kernels for 29%

profile of v6, /device:TPU:0, one launch (start us, length us, event | category | flops | bytes accessed | tf_op | source)
XLA Modules:
  0.0 37.6 jit_solution(12412941678432759988)
XLA Ops:
  0.0 0.0 copy-start.8
  0.0 0.0 copy-start.2
  0.0 0.0 copy-start.7
  0.0 0.0 copy-start.6
  0.0 0.0 copy-start.5
  0.0 4.2 %upward.1 = (f32[192,128]{1,0:T(8,128)}, f32[832,128]{1,0:T(8,128)}, f32[640,128]{1,0:T(8,128)}) custom-call(s32[1]{0:T(128)} %bitcast.first_ref, s32[32]{0:T(128)} %counts_ref.3, f32[3,4096]{1,0:T(4,128)} %offsets_ref.1, f32[16,4096]{1,0:T(8,128)} %charges_ref.1, f32[152,152]{1,0:T(8,128)} %uc2e_hbm.1, f32[160,8]{1,0:T(8,128)} %constant.10.clone.surface_hbm), custom_call_target="tpu_custom_call" | custom-call | flops 500000000 | bytes 1500000 | tf_op jit(solution)/shard_map/upward/pallas_call | solution.py:532
  4.2 0.5 %collective-permute-start = (f32[832,128]{1,0:T(8,128)}, f32[832,128]{1,0:T(8,128)S(1)}, u32[]{:S(2)}, u32[]{:S(2)}) collective-permute-start(f32[832,128]{1,0:T(8,128)} %get-tuple-element.14), channel_id=1, source_target_pairs={{0,1},{1,0},{2,3},{3,2},{4,5},{5,4},{6,7},{7,6},{8,9},{9,8},{10,11... | collective-permute-start | bytes 1277960 | tf_op jit(solution)/shard_map/ppermute | solution.py:25
  4.7 0.7 %collective-permute-start.1 = (f32[192,128]{1,0:T(8,128)}, f32[192,128]{1,0:T(8,128)S(1)}, u32[]{:S(2)}, u32[]{:S(2)}) collective-permute-start(f32[192,128]{1,0:T(8,128)} %get-tuple-element.15), channel_id=1, source_target_pairs={{1,2},{2,1},{3,4},{4,3},{5,6},{6,5},{7,8},{8,7},{9,10},{10,9},{11,... | collective-permute-start | bytes 294920 | tf_op jit(solution)/shard_map/ppermute | solution.py:690
  5.4 3.8 %collective-permute-start.5 = (f32[640,128]{1,0:T(8,128)}, f32[640,128]{1,0:T(8,128)S(1)}, u32[]{:S(2)}, u32[]{:S(2)}) collective-permute-start(f32[640,128]{1,0:T(8,128)} %get-tuple-element.22.refs_0_), channel_id=1, source_target_pairs={{0,2},{1,3},{2,0},{3,1},{4,6},{5,7},{6,4},{7,5},{8,10},{9,11},{10,... | collective-permute-start | bytes 983048 | tf_op jit(solution)/shard_map/ppermute | solution.py:25
  9.2 2.1 %collective-permute-start.4 = (f32[640,128]{1,0:T(8,128)}, f32[640,128]{1,0:T(8,128)S(1)}, u32[]{:S(2)}, u32[]{:S(2)}) collective-permute-start(f32[640,128]{1,0:T(8,128)} %get-tuple-element.22.refs_0_), channel_id=1, source_target_pairs={{0,4},{1,5},{2,6},{3,7},{4,0},{5,1},{6,2},{7,3},{8,12},{9,13},{10,... | collective-permute-start | bytes 983048 | tf_op jit(solution)/shard_map/ppermute | solution.py:25
  11.4 2.6 %collective-permute-start.3 = (f32[640,128]{1,0:T(8,128)}, f32[640,128]{1,0:T(8,128)S(1)}, u32[]{:S(2)}, u32[]{:S(2)}) collective-permute-start(f32[640,128]{1,0:T(8,128)} %get-tuple-element.22.refs_0_), channel_id=1, source_target_pairs={{0,16},{1,17},{2,18},{3,19},{4,20},{5,21},{6,22},{7,23},{8,24},{9,... | collective-permute-start | bytes 983048 | tf_op jit(solution)/shard_map/ppermute | solution.py:25
  14.0 0.0 copy-done.10
  14.0 0.0 collective-permute-done.1.odd_ref
  14.0 1.6 %collective-permute-start.2 = (f32[640,128]{1,0:T(8,128)}, f32[640,128]{1,0:T(8,128)S(1)}, u32[]{:S(2)}, u32[]{:S(2)}) collective-permute-start(f32[640,128]{1,0:T(8,128)} %get-tuple-element.22.refs_0_), channel_id=1, source_target_pairs={{0,8},{1,9},{2,10},{3,11},{4,12},{5,13},{6,14},{7,15},{8,0},{9,1},... | collective-permute-start | bytes 983048 | tf_op jit(solution)/shard_map/ppermute | solution.py:25
  15.6 0.0 collective-permute-done.pair_ref.refs_5_
  15.6 0.0 copy-done.8
  15.6 0.0 copy-done.2
  15.6 0.0 copy-done.4
  15.6 0.0 copy-done
  15.7 0.0 copy-done.7
  15.7 0.0 copy-done.6
  15.7 0.0 copy-done.5
  15.7 0.0 copy-start.9
  15.7 1.0 %copy-done.9 = f32[4,160,128]{2,1,0:T(8,128)S(1)} copy-done((f32[4,160,128]{2,1,0:T(8,128)S(1)}, f32[4,160,128]{2,1,0:T(8,128)}, u32[]{:S(2)}) %copy-start.9) | copy-done | bytes 327704
  16.7 11.0 %near.1 = (f32[16,4096]{1,0:T(8,128)S(1)}, bf16[160,2560]{1,0:T(8,128)(2,1)S(1)}, bf16[160,2560]{1,0:T(8,128)(2,1)S(1)}, bf16[512,224]{1,0:T(8,128)(2,1)S(1)}, b...) custom-call(s32[1]{0:T(128)} %bitcast.first_ref, s32[32]{0:T(128)S(1)} %copy-done.8, f32[3,4096]{1,0:T(4,128)S(1)} %copy-done.4, ...), custom_call_target="tpu_custom_call" | custom-call | flops 4000000000 | bytes 2000000 | tf_op jit(solution)/shard_map/near/pallas_call | solution.py:372
  27.6 0.0 collective-permute-done.5.refs_4_
  27.6 0.0 collective-permute-done.4.refs_3_
  27.6 2.0 %collective-permute-done.3.refs_2_ = f32[640,128]{1,0:T(8,128)S(1)} collective-permute-done((f32[640,128]{1,0:T(8,128)}, f32[640,128]{1,0:T(8,128)S(1)}, u32[]{:S(2)}, u32[]{:S(2)}) %collective-permute-start.3) | collective-permute-done | bytes 327712 | tf_op jit(solution)/shard_map/ppermute | solution.py:25
  29.7 0.3 collective-permute-done.2.refs_1_
  29.9 0.0 copy-done.1
  29.9 0.0 copy-done.3
  29.9 7.6 %far.1 = f32[16,4096]{1,0:T(8,128)} custom-call(s32[32]{0:T(128)S(1)} %copy-done.8, s32[5,16]{1,0:T(8,128)S(1)} %bitcast.4, bf16[160,4096]{1,0:T(8,128)(2,1)S(1)} %get-tuple-element.16.tile_hi_ref, bf16[160,4096]{1,0:T(8,128)(2,1)S(1)} %get-tuple-element.17.tile_lo_ref, f32[16,4096]{1,0:T(8,128)S(1)} %get-tuple-element.18.near_ref, ...), custom_call_target="tpu_custom_call" | custom-call | flops 4000000000 | bytes 4000000 | tf_op jit(solution)/shard_map/far/pallas_call | solution.py:666
  (6 shorter events, 0.0 us)
Async XLA Ops:
  0.0 15.6 %copy-start.8 = (s32[32]{0:T(128)S(1)}, s32[32]{0:T(128)}, u32[]{:S(2)}) copy-start(s32[32]{0:T(128)} %counts_ref.3) | copy-start | bytes 388
  0.0 15.6 %copy-start.2 = (f32[16,4096]{1,0:T(8,128)S(1)}, f32[16,4096]{1,0:T(8,128)}, u32[]{:S(2)}) copy-start(f32[16,4096]{1,0:T(8,128)} %charges_ref.1) | copy-start | bytes 786436
  0.0 15.6 %copy-start.4 = (f32[3,4096]{1,0:T(4,128)S(1)}, f32[3,4096]{1,0:T(4,128)}, u32[]{:S(2)}) copy-start(f32[3,4096]{1,0:T(4,128)} %offsets_ref.1) | copy-start | bytes 147460
  0.0 14.0 %copy-start.10 = (s32[1,5,16]{2,0,1:T(1,128)S(1)}, s32[1,5,16]{2,0,1:T(1,128)}, u32[]{:S(2)}) copy-start(s32[1,5,16]{2,0,1:T(1,128)} %param.18) | copy-start | bytes 964
  0.0 15.6 %copy-start = (f32[152,2432]{1,0:T(8,128)S(1)}, f32[152,2432]{1,0:T(8,128)}, u32[]{:S(2)}) copy-start(f32[152,2432]{1,0:T(8,128)} %m2l_ref.1) | copy-start | bytes 4435972
  0.0 15.6 %copy-start.7 = (s32[32,32]{1,0:T(8,128)S(1)}, s32[32,32]{1,0:T(8,128)}, u32[]{:S(2)}) copy-start(s32[32,32]{1,0:T(8,128)} %vtype_ref.1) | copy-start | bytes 12292
  0.0 15.6 %copy-start.6 = (s32[32,32]{1,0:T(8,128)S(1)}, s32[32,32]{1,0:T(8,128)}, u32[]{:S(2)}) copy-start(s32[32,32]{1,0:T(8,128)} %vsrc_ref.1) | copy-start | bytes 12292
  0.0 15.6 %copy-start.5 = (s32[32,27]{1,0:T(8,128)S(1)}, s32[32,27]{1,0:T(8,128)}, u32[]{:S(2)}) copy-start(s32[32,27]{1,0:T(8,128)} %ulist_ref.1) | copy-start | bytes 10372
  4.2 11.4 %collective-permute-start = (f32[832,128]{1,0:T(8,128)}, f32[832,128]{1,0:T(8,128)S(1)}, u32[]{:S(2)}, u32[]{:S(2)}) collective-permute-start(f32[832,128]{1,0:T(8,128)} %get-tuple-element.14), channel_id=1, source_target_pairs={{0,1},{1,0},{2,3},{3,2},{4,5},{5,4},{6,7},{7,6},{8,9},{9,8},{10,11... | collective-permute-start | bytes 1277960 | tf_op jit(solution)/shard_map/ppermute | solution.py:25
  4.7 9.2 %collective-permute-start.1 = (f32[192,128]{1,0:T(8,128)}, f32[192,128]{1,0:T(8,128)S(1)}, u32[]{:S(2)}, u32[]{:S(2)}) collective-permute-start(f32[192,128]{1,0:T(8,128)} %get-tuple-element.15), channel_id=1, source_target_pairs={{1,2},{2,1},{3,4},{4,3},{5,6},{6,5},{7,8},{8,7},{9,10},{10,9},{11,... | collective-permute-start | bytes 294920 | tf_op jit(solution)/shard_map/ppermute | solution.py:690
  5.4 22.2 %collective-permute-start.5 = (f32[640,128]{1,0:T(8,128)}, f32[640,128]{1,0:T(8,128)S(1)}, u32[]{:S(2)}, u32[]{:S(2)}) collective-permute-start(f32[640,128]{1,0:T(8,128)} %get-tuple-element.22.refs_0_), channel_id=1, source_target_pairs={{0,2},{1,3},{2,0},{3,1},{4,6},{5,7},{6,4},{7,5},{8,10},{9,11},{10,... | collective-permute-start | bytes 983048 | tf_op jit(solution)/shard_map/ppermute | solution.py:25
  9.2 18.4 %collective-permute-start.4 = (f32[640,128]{1,0:T(8,128)}, f32[640,128]{1,0:T(8,128)S(1)}, u32[]{:S(2)}, u32[]{:S(2)}) collective-permute-start(f32[640,128]{1,0:T(8,128)} %get-tuple-element.22.refs_0_), channel_id=1, source_target_pairs={{0,4},{1,5},{2,6},{3,7},{4,0},{5,1},{6,2},{7,3},{8,12},{9,13},{10,... | collective-permute-start | bytes 983048 | tf_op jit(solution)/shard_map/ppermute | solution.py:25
  11.4 18.3 %collective-permute-start.3 = (f32[640,128]{1,0:T(8,128)}, f32[640,128]{1,0:T(8,128)S(1)}, u32[]{:S(2)}, u32[]{:S(2)}) collective-permute-start(f32[640,128]{1,0:T(8,128)} %get-tuple-element.22.refs_0_), channel_id=1, source_target_pairs={{0,16},{1,17},{2,18},{3,19},{4,20},{5,21},{6,22},{7,23},{8,24},{9,... | collective-permute-start | bytes 983048 | tf_op jit(solution)/shard_map/ppermute | solution.py:25
  14.0 16.0 %copy-start.1 = (f32[640,128]{1,0:T(8,128)S(1)}, f32[640,128]{1,0:T(8,128)}, u32[]{:S(2)}) copy-start(f32[640,128]{1,0:T(8,128)} %get-tuple-element.22.refs_0_) | copy-start | bytes 983044
  14.0 16.0 %copy-start.3 = (f32[152,152]{1,0:T(8,128)S(1)}, f32[152,152]{1,0:T(8,128)}, u32[]{:S(2)}) copy-start(f32[152,152]{1,0:T(8,128)} %dc2e_ref.1) | copy-start | bytes 277252
  14.0 16.0 %collective-permute-start.2 = (f32[640,128]{1,0:T(8,128)}, f32[640,128]{1,0:T(8,128)S(1)}, u32[]{:S(2)}, u32[]{:S(2)}) collective-permute-start(f32[640,128]{1,0:T(8,128)} %get-tuple-element.22.refs_0_), channel_id=1, source_target_pairs={{0,8},{1,9},{2,10},{3,11},{4,12},{5,13},{6,14},{7,15},{8,0},{9,1},... | collective-permute-start | bytes 983048 | tf_op jit(solution)/shard_map/ppermute | solution.py:25
  15.7 1.0 %copy-start.9 = (f32[4,160,128]{2,1,0:T(8,128)S(1)}, f32[4,160,128]{2,1,0:T(8,128)}, u32[]{:S(2)}) copy-start(f32[4,160,128]{2,1,0:T(8,128)} %constant.11.clone.surface_ref) | copy-start | bytes 983044
